TPU v7x, 128 devices: a whole 4x4x4 slice. The times are simulated.
128 devices in a mesh: grp: 4 (over z), shard: 32 (over x, y, core).
Axes of the slice: x: 4, y: 4, z: 4, core: 2. Of those that a mesh axis runs over, the one named last changes fastest.
Arguments:
- latents: bfloat16 [16384, 1024], P(('grp', 'shard')), may hold values from -24 to 24
- head_weight: bfloat16 [1024, 1024], P('shard'), may hold values from -0.1875 to 0.1875
- norm_gain: float32 [1024], replicated, may hold values from 0.1 to 1.9
- color_head: bfloat16 [4, 256], replicated, may hold values from -1.5 to 1.5
- sample_points: float32 [8192, 192], P(('grp', 'shard')), may hold values from -1 to 1
- sample_spacing: float32 [8192, 64], P(('grp', 'shard')), may hold values from 0.002 to 0.02
- ray_targets: float32 [3, 8192], P(None, ('grp', 'shard')), may hold values from 0 to 1
- ray_scene: int32 [8192], P(('grp', 'shard')), may hold values from 0 to 127, as said below
Outputs:
- rendered_color: float32 [3, 8192], P(None, ('grp', 'shard'))
- loss: float32 [], replicated
- head_grad: float32 [1024, 1024], P('shard')
- norm_gain_grad: float32 [1024], replicated
- latent_grad: bfloat16 [16384, 1024], P(('grp', 'shard'))
Inputs may be any that keep to these rules, and one draw needn't show every extreme that they name: `ray_scene`: one scene, drawn from the seed, is named by exactly 2 rays of every device; no device names any scene more than 2 times; every scene is named by one ray or more, and the totals of the other scenes differ from one another by one at most.
All inputs are finite; a program needn't handle non-finite values.
Results may differ from a plain program's by a relative error of at most 0.017.
Values may be sent and summed in bfloat16 or wider, within the bound.
No kernel may reach another device: no remote copies, remote signals or barrier semaphores. Data moves between devices by JAX's collectives and lax.ppermute only.
A program may use at most 64 MiB of HBM per device.

v0:
```python
import math

import jax
import jax.numpy as jnp
from jax import lax
from jax.sharding import PartitionSpec as P

norm_eps = 1e-06


def encode(sample_rows, field_width):
    column = jnp.arange(field_width)
    component = column % 3
    octave = (column // 6 % 8).astype(jnp.float32)
    frequency = jnp.exp2(octave) * math.pi
    phase_shift = (column // 3 % 2).astype(jnp.float32) * (0.5 * math.pi)
    picked = jnp.zeros((sample_rows.shape[0], field_width), jnp.float32)
    for coord in range(3):
        chosen = (component == coord).astype(jnp.float32)
        picked = picked + sample_rows[:, coord : coord + 1] * chosen[None, :]
    return jnp.sin(picked * frequency + phase_shift)


def point_rows(points, ray_depth):
    ray_number = points.shape[0]
    return (
        points.reshape(ray_number, 3, ray_depth)
        .transpose(0, 2, 1)
        .reshape(ray_number * ray_depth, 3)
    )


def render_rays(points, spacing, target, live_rays, scene_factor, w_first, w_second, color_head):
    ray_number, ray_depth = spacing.shape
    field_width = w_first.shape[0]
    fan_scale = field_width ** (-0.5)
    sample_rows = point_rows(points, ray_depth)
    h_zero = encode(sample_rows, field_width).astype(jnp.bfloat16)
    h_one = jax.nn.relu(
        jnp.dot(h_zero, w_first, preferred_element_type=jnp.float32) * fan_scale
    ).astype(jnp.bfloat16)
    h_two = jax.nn.relu(
        jnp.dot(h_one, w_second, preferred_element_type=jnp.float32) * fan_scale
    ).astype(jnp.bfloat16)
    raw_out = lax.dot_general(
        color_head, h_two, (((1,), (1,)), ((), ())), preferred_element_type=jnp.float32
    )
    density = jax.nn.softplus(raw_out[0]).reshape(ray_number, ray_depth)
    albedo = jax.nn.sigmoid(raw_out[1:4]).reshape(3, ray_number, ray_depth)
    optical = density * spacing
    optical_before = jnp.cumsum(optical, axis=1) - optical
    transmit = jnp.exp(-optical_before)
    survive = jnp.exp(-optical)
    blend = transmit * (1.0 - survive)
    ray_color = jnp.sum(blend[None] * (albedo - 1.0), axis=2) + 1.0
    residual = ray_color - target.T
    loss_part = jnp.sum(
        jnp.where(live_rays, jnp.sum(residual * residual, axis=0) * scene_factor, 0.0)
    )
    grad_color = jnp.where(live_rays[None, :], 2.0 * residual * scene_factor, 0.0)
    d_albedo = grad_color[:, :, None] * blend[None]
    d_blend = jnp.sum(grad_color[:, :, None] * (albedo - 1.0), axis=0)
    weighted = d_blend * blend
    behind = jnp.sum(weighted, axis=1, keepdims=True) - jnp.cumsum(weighted, axis=1)
    d_optical = d_blend * transmit * survive - behind
    d_density = (
        d_optical * spacing * jax.nn.sigmoid(raw_out[0]).reshape(ray_number, ray_depth)
    ).reshape(1, ray_number * ray_depth)
    d_tint = (d_albedo * albedo * (1.0 - albedo)).reshape(3, ray_number * ray_depth)
    d_raw = jnp.concatenate([d_density, d_tint], axis=0).astype(jnp.bfloat16)
    d_htwo = lax.dot_general(
        d_raw, color_head, (((0,), (0,)), ((), ())), preferred_element_type=jnp.float32
    )
    d_atwo = (jnp.where(h_two > 0, d_htwo, 0.0) * fan_scale).astype(jnp.bfloat16)
    grad_second = lax.dot_general(
        h_one, d_atwo, (((0,), (0,)), ((), ())), preferred_element_type=jnp.float32
    )
    d_hone = lax.dot_general(
        d_atwo, w_second, (((1,), (1,)), ((), ())), preferred_element_type=jnp.float32
    )
    d_aone = (jnp.where(h_one > 0, d_hone, 0.0) * fan_scale).astype(jnp.bfloat16)
    grad_first = lax.dot_general(
        h_zero, d_aone, (((0,), (0,)), ((), ())), preferred_element_type=jnp.float32
    )
    return (ray_color, loss_part, grad_first, grad_second)


def body(
    latents,
    head_weight,
    norm_gain,
    color_head,
    sample_points,
    sample_spacing,
    ray_targets,
    ray_scene,
):
    devices = lax.axis_size(("grp", "shard"))
    ray_count, ray_depth = sample_spacing.shape
    tokens, model = latents.shape
    field_width = color_head.shape[1]
    per_layer = field_width * field_width // model
    per_device = 4 * ray_count // devices
    slot_total = per_device * devices
    latent_f32 = latents.astype(jnp.float32)
    inv_rms = lax.rsqrt(jnp.mean(latent_f32 * latent_f32, axis=1, keepdims=True) + norm_eps)
    x_hat = latent_f32 * inv_rms
    x_norm = (x_hat * norm_gain).astype(jnp.bfloat16)
    columns = x_norm
    field_sum = jnp.dot(
        columns,
        lax.all_gather(head_weight, "shard", axis=0, tiled=True),
        preferred_element_type=jnp.float32,
    )
    field_rows = field_sum.astype(jnp.bfloat16)
    w_first = field_rows[:per_layer].reshape(field_width, field_width)
    w_second = field_rows[per_layer:].reshape(field_width, field_width)
    ray_ids = jnp.arange(ray_count, dtype=jnp.int32)
    same_scene = ray_scene[:, None] == ray_scene[None, :]
    earlier = ray_ids[:, None] < ray_ids[None, :]
    ray_rank = jnp.sum(jnp.logical_and(same_scene, earlier).astype(jnp.int32), axis=0)
    slot_of_ray = ray_scene * per_device + ray_rank
    payload = jnp.concatenate([sample_points, sample_spacing], axis=1)
    send_payload = (
        jnp.zeros((slot_total, payload.shape[1]), jnp.float32).at[slot_of_ray].set(payload)
    )
    send_target = jnp.zeros((slot_total, 3), jnp.float32).at[slot_of_ray].set(ray_targets.T)
    send_live = jnp.zeros((slot_total,), jnp.float32).at[slot_of_ray].set(1.0)
    recv_payload, recv_target, recv_live = (
        lax.all_to_all(send_payload, ("grp", "shard"), split_axis=0, concat_axis=0, tiled=True),
        lax.all_to_all(send_target, ("grp", "shard"), split_axis=0, concat_axis=0, tiled=True),
        lax.all_to_all(send_live, ("grp", "shard"), split_axis=0, concat_axis=0, tiled=True),
    )
    block_rays = 1024 // ray_depth
    block_total = slot_total // block_rays
    scene_rays = jnp.sum(recv_live)
    scene_factor = 1.0 / (devices * scene_rays)

    def render_block(running, block_item):
        grad_first, grad_second, loss_sum = running
        block_payload, block_target, block_live = block_item
        ray_color, loss_part, more_first, more_second = render_rays(
            block_payload[:, : 3 * ray_depth],
            block_payload[:, 3 * ray_depth :],
            block_target,
            block_live > 0.5,
            scene_factor,
            w_first,
            w_second,
            color_head,
        )
        return (
            (grad_first + more_first, grad_second + more_second, loss_sum + loss_part),
            ray_color,
        )

    zero_grad = jnp.zeros((field_width, field_width), jnp.float32)
    block_items = (
        recv_payload.reshape(block_total, block_rays, payload.shape[1]),
        recv_target.reshape(block_total, block_rays, 3),
        recv_live.reshape(block_total, block_rays),
    )
    (grad_first, grad_second, loss_sum), block_colors = lax.scan(
        render_block, (zero_grad, zero_grad, jnp.zeros((), jnp.float32)), block_items
    )
    slot_colors = block_colors.transpose(1, 0, 2).reshape(3, slot_total)
    returned = lax.all_to_all(
        slot_colors, ("grp", "shard"), split_axis=1, concat_axis=1, tiled=True
    )
    rendered = returned[:, slot_of_ray]
    d_field = jnp.concatenate(
        [grad_first.reshape(per_layer, model), grad_second.reshape(per_layer, model)], axis=0
    ).astype(jnp.bfloat16)
    d_norm = lax.dot_general(
        d_field,
        lax.all_gather(head_weight, "shard", axis=0, tiled=True),
        (((1,), (1,)), ((), ())),
        preferred_element_type=jnp.float32,
    )
    columns = x_norm
    group_part = lax.psum_scatter(
        lax.dot_general(
            columns, d_field, (((0,), (0,)), ((), ())), preferred_element_type=jnp.float32
        ).astype(jnp.bfloat16),
        "shard",
        scatter_dimension=0,
        tiled=True,
    )
    head_grad = lax.psum(group_part, "grp").astype(jnp.float32)
    gain_part = jnp.sum(d_norm * x_hat, axis=0)
    norm_gain_grad, loss_total = lax.psum((gain_part, loss_sum), ("grp", "shard"))
    d_scaled = d_norm * norm_gain
    latent_grad = (
        inv_rms * (d_scaled - x_hat * jnp.mean(d_scaled * x_hat, axis=1, keepdims=True))
    ).astype(jnp.bfloat16)
    return (rendered, loss_total, head_grad, norm_gain_grad, latent_grad)


def solution(mesh):
    placed = (
        P(("grp", "shard"), None),
        P("shard", None),
        P(),
        P(),
        P(("grp", "shard"), None),
        P(("grp", "shard"), None),
        P(None, ("grp", "shard")),
        P(("grp", "shard")),
    )
    return jax.shard_map(
        body,
        mesh=mesh,
        in_specs=placed,
        out_specs=(
            P(None, ("grp", "shard")),
            P(),
            P("shard", None),
            P(),
            P(("grp", "shard"), None),
        ),
        check_vma=False,
    )
```

profile of v0, /device:TPU:0, one launch (start us, length us, event | category | flops | bytes accessed | tf_op | source)
XLA Modules:
  0.0 428.4 jit_solution(16951223381793124593)
XLA Ops:
  11.0 11.2 %all-to-all-start.1 = ((f32[128,2,1]{1,2,0:T(1,128)}), f32[128,2,1]{1,2,0:T(1,128)S(1)}, u32[]{:S(2)}, u32[]{:S(2)}) async-start(f32[128,2,1]{1,2,0:T(1,128)} %bitcast), calls=%async_computation.1 | async-start | bytes 131072 | tf_op jit(solution)/shard_map/all_to_all | solution.py:132
  24.2 7.1 %all-to-all-done.1 = f32[128,2,1]{1,2,0:T(1,128)S(1)} async-done(((f32[128,2,1]{1,2,0:T(1,128)}), f32[128,2,1]{1,2,0:T(1,128)S(1)}, u32[]{:S(2)}, u32[]{:S(2)}) %all-to-all-start.1) | async-done | bytes 1056 | tf_op jit(solution)/shard_map/all_to_all | solution.py:132
  31.4 4.7 %all-to-all-start.2 = ((f32[128,2,3]{2,1,0:T(2,128)}), f32[128,2,3]{2,1,0:T(2,128)S(1)}, u32[]{:S(2)}, u32[]{:S(2)}) async-start(f32[128,2,3]{2,1,0:T(2,128)} %bitcast.2), calls=%async_computation.2 | async-start | bytes 262144 | tf_op jit(solution)/shard_map/all_to_all | solution.py:131
  39.3 6.2 %all-to-all-done.2 = f32[128,2,3]{2,1,0:T(2,128)S(1)} async-done(((f32[128,2,3]{2,1,0:T(2,128)}), f32[128,2,3]{2,1,0:T(2,128)S(1)}, u32[]{:S(2)}, u32[]{:S(2)}) %all-to-all-start.2) | async-done | bytes 3104 | tf_op jit(solution)/shard_map/all_to_all | solution.py:131
  45.5 4.7 %all-to-all-start = ((f32[128,2,256]{2,1,0:T(2,128)}), f32[128,2,256]{2,1,0:T(2,128)S(1)}, u32[]{:S(2)}, u32[]{:S(2)}) async-start(f32[128,2,256]{2,1,0:T(2,128)} %all_to_all.26), calls=%async_computation | async-start | bytes 524288 | tf_op jit(solution)/shard_map/all_to_all | solution.py:130
  53.3 8.4 %all-to-all-done = f32[128,2,256]{2,1,0:T(2,128)S(1)} async-done(((f32[128,2,256]{2,1,0:T(2,128)}), f32[128,2,256]{2,1,0:T(2,128)S(1)}, u32[]{:S(2)}, u32[]{:S(2)}) %all-to-all-start) | async-done | bytes 262176 | tf_op jit(solution)/shard_map/all_to_all | solution.py:130
  64.3 210.9 %while.20 = (s32[]{:T(128)}, f32[256,256]{1,0:T(8,128)S(1)}, f32[256,256]{1,0:T(8,128)S(1)}, f32[]{:T(128)}, f32[16,3,16]{2,1,0:T(4,128)S(1)}, /*index=5*/f32[16...) while((s32[]{:T(128)}, f32[256,256]{1,0:T(8,128)S(1)}, ...), condition=%wide.region_14.15_spmd.clone, body=%wide.region_6.14_spmd.clone.sunk | while | flops 683649216 | bytes 7148404 | solution.py:163
  64.5 4.6 %fusion.108 = bf16[1024,256]{1,0:T(8,128)(2,1)S(1)} fusion(bf16[256,256]{1,0:T(8,128)(2,1)S(1)} %get-tuple-element.516, f32[256]{0:T(256)S(1)} %get-tuple-element.465, f32[256]{0:T(256)S(1)} %get-tuple-element.466, f32[256]{0:T(256)S(1)} %get-tuple-element.467, f32[1024]{0:T(1024)S(1)} %bitcast.93, f32[256]{0:T(256)S(1)} %get-tuple-element.469, ...), kind=kOutput, calls=%fused_computation.12.clone.1 | convolution fusion | flops 137101312 | bytes 672768 | tf_op jit(solution)/shard_map/while/body/eval_jaxpr/dot_general | solution.py:40
  77.7 4.6 %fusion.108 = bf16[1024,256]{1,0:T(8,128)(2,1)S(1)} fusion(bf16[256,256]{1,0:T(8,128)(2,1)S(1)} %get-tuple-element.516, f32[256]{0:T(256)S(1)} %get-tuple-element.465, f32[256]{0:T(256)S(1)} %get-tuple-element.466, f32[256]{0:T(256)S(1)} %get-tuple-element.467, f32[1024]{0:T(1024)S(1)} %bitcast.93, f32[256]{0:T(256)S(1)} %get-tuple-element.469, ...), kind=kOutput, calls=%fused_computation.12.clone.1 | convolution fusion | flops 137101312 | bytes 672768 | tf_op jit(solution)/shard_map/while/body/eval_jaxpr/dot_general | solution.py:40
  90.9 4.6 %fusion.108 = bf16[1024,256]{1,0:T(8,128)(2,1)S(1)} fusion(bf16[256,256]{1,0:T(8,128)(2,1)S(1)} %get-tuple-element.516, f32[256]{0:T(256)S(1)} %get-tuple-element.465, f32[256]{0:T(256)S(1)} %get-tuple-element.466, f32[256]{0:T(256)S(1)} %get-tuple-element.467, f32[1024]{0:T(1024)S(1)} %bitcast.93, f32[256]{0:T(256)S(1)} %get-tuple-element.469, ...), kind=kOutput, calls=%fused_computation.12.clone.1 | convolution fusion | flops 137101312 | bytes 672768 | tf_op jit(solution)/shard_map/while/body/eval_jaxpr/dot_general | solution.py:40
  104.1 4.6 %fusion.108 = bf16[1024,256]{1,0:T(8,128)(2,1)S(1)} fusion(bf16[256,256]{1,0:T(8,128)(2,1)S(1)} %get-tuple-element.516, f32[256]{0:T(256)S(1)} %get-tuple-element.465, f32[256]{0:T(256)S(1)} %get-tuple-element.466, f32[256]{0:T(256)S(1)} %get-tuple-element.467, f32[1024]{0:T(1024)S(1)} %bitcast.93, f32[256]{0:T(256)S(1)} %get-tuple-element.469, ...), kind=kOutput, calls=%fused_computation.12.clone.1 | convolution fusion | flops 137101312 | bytes 672768 | tf_op jit(solution)/shard_map/while/body/eval_jaxpr/dot_general | solution.py:40
  117.3 4.6 %fusion.108 = bf16[1024,256]{1,0:T(8,128)(2,1)S(1)} fusion(bf16[256,256]{1,0:T(8,128)(2,1)S(1)} %get-tuple-element.516, f32[256]{0:T(256)S(1)} %get-tuple-element.465, f32[256]{0:T(256)S(1)} %get-tuple-element.466, f32[256]{0:T(256)S(1)} %get-tuple-element.467, f32[1024]{0:T(1024)S(1)} %bitcast.93, f32[256]{0:T(256)S(1)} %get-tuple-element.469, ...), kind=kOutput, calls=%fused_computation.12.clone.1 | convolution fusion | flops 137101312 | bytes 672768 | tf_op jit(solution)/shard_map/while/body/eval_jaxpr/dot_general | solution.py:40
  130.4 4.6 %fusion.108 = bf16[1024,256]{1,0:T(8,128)(2,1)S(1)} fusion(bf16[256,256]{1,0:T(8,128)(2,1)S(1)} %get-tuple-element.516, f32[256]{0:T(256)S(1)} %get-tuple-element.465, f32[256]{0:T(256)S(1)} %get-tuple-element.466, f32[256]{0:T(256)S(1)} %get-tuple-element.467, f32[1024]{0:T(1024)S(1)} %bitcast.93, f32[256]{0:T(256)S(1)} %get-tuple-element.469, ...), kind=kOutput, calls=%fused_computation.12.clone.1 | convolution fusion | flops 137101312 | bytes 672768 | tf_op jit(solution)/shard_map/while/body/eval_jaxpr/dot_general | solution.py:40
  156.8 4.6 %fusion.108 = bf16[1024,256]{1,0:T(8,128)(2,1)S(1)} fusion(bf16[256,256]{1,0:T(8,128)(2,1)S(1)} %get-tuple-element.516, f32[256]{0:T(256)S(1)} %get-tuple-element.465, f32[256]{0:T(256)S(1)} %get-tuple-element.466, f32[256]{0:T(256)S(1)} %get-tuple-element.467, f32[1024]{0:T(1024)S(1)} %bitcast.93, f32[256]{0:T(256)S(1)} %get-tuple-element.469, ...), kind=kOutput, calls=%fused_computation.12.clone.1 | convolution fusion | flops 137101312 | bytes 672768 | tf_op jit(solution)/shard_map/while/body/eval_jaxpr/dot_general | solution.py:40
  170.0 4.6 %fusion.108 = bf16[1024,256]{1,0:T(8,128)(2,1)S(1)} fusion(bf16[256,256]{1,0:T(8,128)(2,1)S(1)} %get-tuple-element.516, f32[256]{0:T(256)S(1)} %get-tuple-element.465, f32[256]{0:T(256)S(1)} %get-tuple-element.466, f32[256]{0:T(256)S(1)} %get-tuple-element.467, f32[1024]{0:T(1024)S(1)} %bitcast.93, f32[256]{0:T(256)S(1)} %get-tuple-element.469, ...), kind=kOutput, calls=%fused_computation.12.clone.1 | convolution fusion | flops 137101312 | bytes 672768 | tf_op jit(solution)/shard_map/while/body/eval_jaxpr/dot_general | solution.py:40
  196.3 4.6 %fusion.108 = bf16[1024,256]{1,0:T(8,128)(2,1)S(1)} fusion(bf16[256,256]{1,0:T(8,128)(2,1)S(1)} %get-tuple-element.516, f32[256]{0:T(256)S(1)} %get-tuple-element.465, f32[256]{0:T(256)S(1)} %get-tuple-element.466, f32[256]{0:T(256)S(1)} %get-tuple-element.467, f32[1024]{0:T(1024)S(1)} %bitcast.93, f32[256]{0:T(256)S(1)} %get-tuple-element.469, ...), kind=kOutput, calls=%fused_computation.12.clone.1 | convolution fusion | flops 137101312 | bytes 672768 | tf_op jit(solution)/shard_map/while/body/eval_jaxpr/dot_general | solution.py:40
  209.5 4.6 %fusion.108 = bf16[1024,256]{1,0:T(8,128)(2,1)S(1)} fusion(bf16[256,256]{1,0:T(8,128)(2,1)S(1)} %get-tuple-element.516, f32[256]{0:T(256)S(1)} %get-tuple-element.465, f32[256]{0:T(256)S(1)} %get-tuple-element.466, f32[256]{0:T(256)S(1)} %get-tuple-element.467, f32[1024]{0:T(1024)S(1)} %bitcast.93, f32[256]{0:T(256)S(1)} %get-tuple-element.469, ...), kind=kOutput, calls=%fused_computation.12.clone.1 | convolution fusion | flops 137101312 | bytes 672768 | tf_op jit(solution)/shard_map/while/body/eval_jaxpr/dot_general | solution.py:40
  222.7 4.6 %fusion.108 = bf16[1024,256]{1,0:T(8,128)(2,1)S(1)} fusion(bf16[256,256]{1,0:T(8,128)(2,1)S(1)} %get-tuple-element.516, f32[256]{0:T(256)S(1)} %get-tuple-element.465, f32[256]{0:T(256)S(1)} %get-tuple-element.466, f32[256]{0:T(256)S(1)} %get-tuple-element.467, f32[1024]{0:T(1024)S(1)} %bitcast.93, f32[256]{0:T(256)S(1)} %get-tuple-element.469, ...), kind=kOutput, calls=%fused_computation.12.clone.1 | convolution fusion | flops 137101312 | bytes 672768 | tf_op jit(solution)/shard_map/while/body/eval_jaxpr/dot_general | solution.py:40
  235.9 4.6 %fusion.108 = bf16[1024,256]{1,0:T(8,128)(2,1)S(1)} fusion(bf16[256,256]{1,0:T(8,128)(2,1)S(1)} %get-tuple-element.516, f32[256]{0:T(256)S(1)} %get-tuple-element.465, f32[256]{0:T(256)S(1)} %get-tuple-element.466, f32[256]{0:T(256)S(1)} %get-tuple-element.467, f32[1024]{0:T(1024)S(1)} %bitcast.93, f32[256]{0:T(256)S(1)} %get-tuple-element.469, ...), kind=kOutput, calls=%fused_computation.12.clone.1 | convolution fusion | flops 137101312 | bytes 672768 | tf_op jit(solution)/shard_map/while/body/eval_jaxpr/dot_general | solution.py:40
  249.1 4.6 %fusion.108 = bf16[1024,256]{1,0:T(8,128)(2,1)S(1)} fusion(bf16[256,256]{1,0:T(8,128)(2,1)S(1)} %get-tuple-element.516, f32[256]{0:T(256)S(1)} %get-tuple-element.465, f32[256]{0:T(256)S(1)} %get-tuple-element.466, f32[256]{0:T(256)S(1)} %get-tuple-element.467, f32[1024]{0:T(1024)S(1)} %bitcast.93, f32[256]{0:T(256)S(1)} %get-tuple-element.469, ...), kind=kOutput, calls=%fused_computation.12.clone.1 | convolution fusion | flops 137101312 | bytes 672768 | tf_op jit(solution)/shard_map/while/body/eval_jaxpr/dot_general | solution.py:40
  262.2 4.6 %fusion.108 = bf16[1024,256]{1,0:T(8,128)(2,1)S(1)} fusion(bf16[256,256]{1,0:T(8,128)(2,1)S(1)} %get-tuple-element.516, f32[256]{0:T(256)S(1)} %get-tuple-element.465, f32[256]{0:T(256)S(1)} %get-tuple-element.466, f32[256]{0:T(256)S(1)} %get-tuple-element.467, f32[1024]{0:T(1024)S(1)} %bitcast.93, f32[256]{0:T(256)S(1)} %get-tuple-element.469, ...), kind=kOutput, calls=%fused_computation.12.clone.1 | convolution fusion | flops 137101312 | bytes 672768 | tf_op jit(solution)/shard_map/while/body/eval_jaxpr/dot_general | solution.py:40
  278.4 4.7 %all-to-all-start.3 = ((f32[3,128,2]{0,2,1:T(2,128)}), f32[3,128,2]{0,2,1:T(2,128)S(1)}, u32[]{:S(2)}, u32[]{:S(2)}) async-start(f32[3,128,2]{0,2,1:T(2,128)} %bitcast.5), calls=%async_computation.3 | async-start | bytes 262144 | tf_op jit(solution)/shard_map/all_to_all | solution.py:167
  284.1 68.3 %reduce-scatter.2.cloned.1.call-done = bf16[32,1024]{1,0:T(8,128)(2,1)} async-done(((bf16[1024,1024]{1,0:T(8,128)(2,1)}), bf16[32,1024]{1,0:T(8,128)(2,1)}) %reduce-scatter.2.cloned.1.call-update) | async-done | bytes 65552 | tf_op jit(solution)/shard_map/reduce_scatter | solution.py:181
  353.3 65.7 %all-reduce = (f32[]{:T(128)}, f32[1024]{0:T(1024)}) all-reduce(f32[]{:T(128)} %get-tuple-element.221, f32[1024]{0:T(1024)S(1)} %get-tuple-element.326), channel_id=1, replica_groups=mesh['grp'=4,'shard'=32] {'grp','shard'}, use_global_device_ids=true, to_apply=%region_15.16 | all-reduce | flops 1025 | bytes 8200 | tf_op jit(solution)/shard_map/psum | solution.py:191
  (601 shorter events, 156.5 us)
Async XLA Ops:
  7.2 54.8 %copy-start.1 = (bf16[128,1024]{1,0:T(8,128)(2,1)S(1)}, bf16[128,1024]{1,0:T(8,128)(2,1)}, u32[]{:S(2)}) copy-start(bf16[128,1024]{1,0:T(8,128)(2,1)} %param.10) | copy-start | bytes 786436
  7.2 54.8 %copy-start.2 = (f32[1024]{0:T(1024)S(1)}, f32[1024]{0:T(1024)}, u32[]{:S(2)}) copy-start(f32[1024]{0:T(1024)} %param.12) | copy-start | bytes 12292
  7.2 54.7 %all-gather.2.cloned.1.call-start = ((), (), s32[]{:S(2)}) async-start(), calls=%async_computation.5 | async-start | bytes 2162688 | tf_op jit(solution)/shard_map/all_gather | solution.py:112
  11.0 20.4 %all-to-all-start.1 = ((f32[128,2,1]{1,2,0:T(1,128)}), f32[128,2,1]{1,2,0:T(1,128)S(1)}, u32[]{:S(2)}, u32[]{:S(2)}) async-start(f32[128,2,1]{1,2,0:T(1,128)} %bitcast), calls=%async_computation.1 | async-start | bytes 131072 | tf_op jit(solution)/shard_map/all_to_all | solution.py:132
  31.4 14.1 %all-to-all-start.2 = ((f32[128,2,3]{2,1,0:T(2,128)}), f32[128,2,3]{2,1,0:T(2,128)S(1)}, u32[]{:S(2)}, u32[]{:S(2)}) async-start(f32[128,2,3]{2,1,0:T(2,128)} %bitcast.2), calls=%async_computation.2 | async-start | bytes 262144 | tf_op jit(solution)/shard_map/all_to_all | solution.py:131
  45.5 16.2 %all-to-all-start = ((f32[128,2,256]{2,1,0:T(2,128)}), f32[128,2,256]{2,1,0:T(2,128)S(1)}, u32[]{:S(2)}, u32[]{:S(2)}) async-start(f32[128,2,256]{2,1,0:T(2,128)} %all_to_all.26), calls=%async_computation | async-start | bytes 524288 | tf_op jit(solution)/shard_map/all_to_all | solution.py:130
  50.2 302.2 %reduce-scatter.2.cloned.1.call-start = ((), (), s32[]{:S(2)}) async-start(), calls=%async_computation.6 | async-start | bytes 2162688 | tf_op jit(solution)/shard_map/reduce_scatter | solution.py:181
  53.3 10.9 %copy-start.3 = (bf16[4,256]{1,0:T(4,128)(2,1)S(1)}, bf16[4,256]{1,0:T(4,128)(2,1)}, u32[]{:S(2)}) copy-start(bf16[4,256]{1,0:T(4,128)(2,1)} %param.13) | copy-start | bytes 6148
  275.4 7.7 %copy-start = (bf16[1024,1024]{1,0:T(8,128)(2,1)S(1)}, bf16[1024,1024]{1,0:T(8,128)(2,1)}, u32[]{:S(2)}) copy-start(bf16[1024,1024]{1,0:T(8,128)(2,1)} %all-gather.2.cloned.1.call-done) | copy-start | bytes 6291460
  278.4 140.7 %all-to-all-start.3 = ((f32[3,128,2]{0,2,1:T(2,128)}), f32[3,128,2]{0,2,1:T(2,128)S(1)}, u32[]{:S(2)}, u32[]{:S(2)}) async-start(f32[3,128,2]{0,2,1:T(2,128)} %bitcast.5), calls=%async_computation.3 | async-start | bytes 262144 | tf_op jit(solution)/shard_map/all_to_all | solution.py:167
  283.1 137.3 %all-reduce.3.cloned.1.call-start = ((), (), s32[]{:S(2)}) async-start(), calls=%async_computation.7 | async-start | bytes 131072 | tf_op jit(solution)/shard_map/psum | solution.py:189
Sparse Core Ops, SparseCore 0:
  10.3 47.5 all-gather.1
  277.7 74.6 reduce-scatter.1
  354.7 40.4 all-reduce.2
where the time goes:
time: 429 us; the launch traced here: 428 us
  matrix products  167 us (39%)
  waiting for transfers between devices  90.7 us (21%)
  blocking collectives  65.7 us (15%)
  other arithmetic  32.8 us (8%)
  starting transfers between devices  25.5 us (6%)
  local copies, waits for them, and re-layouts  20.1 us (5%)
  between operations  14.7 us (3%)
  loops' own time  12.2 us (3%)
    dot_general x16, matrix products, render_rays(): jnp.dot(h_zero, w_first, preferred_element_type=jnp.float32) * fan_scale  73.2 us
    reduce_scatter x1, waiting for transfers between devices, body(): lax.psum_scatter(lax.dot_general(columns, d_field, (((0,), (0,)), ((), ()...  68.3 us
    dot_general x16, matrix products, render_rays(): lax.dot_general(h_zero, d_aone, (((0,), (0,)), ((), ())), preferred_eleme...  67.3 us
    psum x1, blocking collectives, body(): lax.psum((gain_part, loss_sum), ('grp', 'shard'))  65.7 us
    another operation x1, loops' own time, body(): lax.scan(render_block, (zero_grad, zero_grad, jnp.zeros((), jnp.float32))...  12.2 us
    all_to_all x1, starting transfers between devices, body(): lax.all_to_all(send_live, ('grp', 'shard'), split_axis=0, concat_axis=0,...  11.2 us
    reduce_sum x16, other arithmetic, render_rays(): jnp.sum(jnp.where(live_rays, jnp.sum(residual * residual, axis=0) * scene...  9.79 us
  transfers between devices with their start and end apart: 7, of which 4 were waited for; matrix products, arithmetic and copies ran while one was open for 3% of the time, Pallas kernels for 0%

commit v1 on v0

v1 whole, which is shorter than its diff:
```python
import jax
import jax.numpy as jnp
import numpy as np
from jax import lax
from jax.experimental import pallas as pl
from jax.experimental.pallas import tpu as pltpu
from jax.sharding import PartitionSpec as P

norm_eps = 1e-06
f32, bf16 = jnp.float32, jnp.bfloat16
both = ("grp", "shard")

sin_coef = (3.141590256747904, -5.167405766362, 2.544000216186916, -0.5594350008327638)
cos_coef = (0.999999953027512, -4.934792802489427, 4.058410790762133, -1.3318729727851486, 0.21968242357146)

step_block = 8
features = 48


def fold_matrix():
    fold = np.zeros((features, 256), np.float32)
    for j in range(256):
        jm = j % features
        m = (jm % 3) * 16 + (jm // 3 % 2) * 8 + jm // 6
        fold[m, (j % 4) * 64 + j // 4] = 1.0
    return fold


def dot(a, b, dims=(((1,), (0,)), ((), ())), precision=None):
    return lax.dot_general(a, b, dims, preferred_element_type=f32, precision=precision)


def pack_kernel(scene_ref, points_ref, spacing_ref, target_ref, out_ref, slot_ref, count_ref, pay_ref, tint_ref):
    rays = points_ref.shape[0]
    for d in range(count_ref.shape[0]):
        count_ref[d] = 0
    out_ref[...] = jnp.zeros_like(out_ref)
    pay_ref[:, 0:192] = points_ref[...]
    pay_ref[:, 192:256] = spacing_ref[...]
    target = jnp.concatenate([target_ref[...], jnp.zeros((5, rays), f32)], axis=0).T
    lane = lax.broadcasted_iota(jnp.int32, (rays, 128), 1)
    for k in range(2):
        placed = jnp.zeros((rays, 128), f32)
        for c in range(3):
            placed = jnp.where(lane == 3 * k + c, target[:, c : c + 1], placed)
        tint_ref[k] = placed

    for r in range(rays):
        scene = scene_ref[r]
        rank = count_ref[scene]
        count_ref[scene] = rank + 1
        slot_ref[r] = scene * 2 + rank
        out_ref[scene, :, pl.ds(pl.multiple_of(rank * 256, 256), 256)] = pay_ref[r : r + 1, :]
        out_ref[scene, :, 512:640] += tint_ref[rank, r : r + 1, :]


def pack(ray_scene, points, spacing, targets, slots):
    rays = points.shape[0]
    return pl.pallas_call(
        pack_kernel,
        out_shape=(
            jax.ShapeDtypeStruct((slots, 1, 640), f32),
            jax.ShapeDtypeStruct((rays,), jnp.int32),
        ),
        in_specs=[pl.BlockSpec(memory_space=pltpu.SMEM)] + [pl.BlockSpec(memory_space=pltpu.VMEM)] * 3,
        out_specs=(pl.BlockSpec(memory_space=pltpu.VMEM), pl.BlockSpec(memory_space=pltpu.SMEM)),
        scratch_shapes=[
            pltpu.SMEM((slots,), jnp.int32),
            pltpu.VMEM((rays, 256), f32),
            pltpu.VMEM((2, rays, 128), f32),
        ],
        cost_estimate=pl.CostEstimate(flops=200000, bytes_accessed=1000000, transcendentals=0),
        name="pack",
    )(ray_scene, points, spacing, targets)


def horner(u, coef):
    value = coef[-1] * u + coef[-2]
    for c in coef[-3::-1]:
        value = value * u + c
    return value


def render_kernel(
    core_ref,
    latent_ref,
    weight_ref,
    gain_ref,
    head_ref,
    recv_ref,
    fold_ref,
    unfold_ref,
    color_ref,
    dfield_ref,
    keep_ref,
    send_ref,
    rays_ref,
    h0_ref,
    h1_ref,
    h2_ref,
    raw_ref,
    draw_ref,
    g0_ref,
    g1_ref,
    rows_ref,
    xnt_ref,
):
    scale = 1.0 / 16.0
    slots = recv_ref.shape[0]
    rays = 2 * slots
    wide = step_block * rays
    blocks = 64 // step_block

    for k in range(2):
        rays_ref[0:256, k * slots : (k + 1) * slots] = recv_ref[:, k * 256 : (k + 1) * 256].T
    tint = recv_ref[:, 512:640].T

    latent = latent_ref[...].astype(f32)
    inv_rms = lax.rsqrt(jnp.mean(latent * latent, axis=1, keepdims=True) + norm_eps)
    normed = latent * inv_rms * gain_ref[...]
    xnt_ref[...] = normed.T.astype(bf16)
    field = dot(normed.astype(bf16), weight_ref[...]).astype(bf16)
    stacked = jnp.concatenate([field[0:64, q * 256 : (q + 1) * 256] for q in range(4)], axis=0)
    folded = dot(fold_ref[...], stacked) * scale
    high = folded.astype(bf16).astype(f32)
    split = jnp.concatenate([high, folded - high, jnp.zeros((32, 256), f32)], axis=0)
    w0t = split.T.astype(bf16)[:, 0:96]
    field1 = field[64:128, :].astype(f32) * scale
    for q in range(4):
        for n in range(2):
            rows_ref[n, pl.ds(q, 64, stride=4), :] = field1[:, q * 256 + n * 128 : q * 256 + (n + 1) * 128]
    w1f = jnp.concatenate([rows_ref[0], rows_ref[1]], axis=1)
    w1 = w1f.astype(bf16)
    w1t = w1f.T.astype(bf16)
    head_f = jnp.concatenate([head_ref[...].astype(f32), jnp.zeros((4, 256), f32)], axis=0)
    head = head_f.astype(bf16)
    head_t = (head_f * scale).T.astype(bf16)

    octave = jnp.left_shift(1, lax.broadcasted_iota(jnp.int32, (8, rays), 0)).astype(f32)

    def forward(b, carry):
        parts = [[] for _ in range(6)]
        for c in range(3):
            group = rays_ref[pl.ds(pl.multiple_of(c * 64 + b * step_block, 8), step_block), :]
            for s in range(step_block):
                y = group[s : s + 1, :] * octave
                whole = jnp.floor(y + 0.5)
                r = y - whole
                half = whole * 0.5
                sign = 1.0 - 4.0 * (half - jnp.floor(half))
                u = r * r
                parts[2 * c].append(r * sign * horner(u, sin_coef))
                parts[2 * c + 1].append(sign * horner(u, cos_coef))
        h0 = jnp.concatenate([jnp.concatenate(p, axis=1) for p in parts], axis=0).astype(bf16)
        h0_ref[b] = h0
        h1 = jnp.maximum(dot(w0t, jnp.concatenate([h0, h0], axis=0)), 0.0).astype(bf16)
        h1_ref[b] = h1
        h2 = jnp.maximum(dot(w1t, h1), 0.0).astype(bf16)
        h2_ref[b] = h2
        raw = dot(head, h2)
        for s in range(step_block):
            at = pl.ds(pl.multiple_of((b * step_block + s) * 8, 8), 8)
            for k in range(2):
                raw_ref[k, at, :] = raw[:, (2 * s + k) * slots : (2 * s + k + 1) * slots]
        return carry

    lax.fori_loop(0, blocks, forward, 0)

    def spread(c):
        return jnp.concatenate([raw_ref[k, pl.ds(c, 64, stride=8), :] for k in range(2)], axis=1)

    def store_gradient(c, value):
        for k in range(2):
            draw_ref[k, pl.ds(c, 64, stride=8), :] = value[:, k * slots : (k + 1) * slots]

    spacing = rays_ref[192:256, :]
    row = lax.broadcasted_iota(jnp.int32, (64, 64), 0)
    column = lax.broadcasted_iota(jnp.int32, (64, 64), 1)
    raw0 = spread(0)
    density = jnp.maximum(raw0, 0.0) + jnp.log1p(jnp.exp(-jnp.abs(raw0)))
    optical = density * spacing
    before = dot((column < row).astype(f32), optical, precision=lax.Precision.HIGHEST)
    transmit = jnp.exp(-before)
    survive = jnp.exp(-optical)
    blend = transmit * (1.0 - survive)
    live = (spacing[0:1, :] > 0.0).astype(f32)
    factor = 1.0 / (float(slots) * jnp.sum(live, axis=1, keepdims=True))
    albedo = [jax.nn.sigmoid(spread(1 + c)) for c in range(3)]
    d_blend = jnp.zeros_like(blend)
    square = jnp.zeros_like(live)
    colors, grads = [], []
    for c in range(3):
        color = jnp.sum(blend * (albedo[c] - 1.0), axis=0, keepdims=True) + 1.0
        target = jnp.concatenate([tint[c : c + 1, :], tint[3 + c : 4 + c, :]], axis=1)
        residual = (color - target) * live
        square = square + residual * residual
        grad = 2.0 * residual * factor
        d_blend = d_blend + grad * (albedo[c] - 1.0)
        colors.append(color)
        grads.append(grad)
    loss = jnp.sum(square, axis=1, keepdims=True) * factor
    rows = [colors[c][:, k * slots : (k + 1) * slots] for k in range(2) for c in range(3)]
    rows += [jnp.broadcast_to(loss, (1, slots)), jnp.zeros((slots - 7, slots), f32)]
    color_ref[...] = jnp.concatenate(rows, axis=0).T
    weighted = d_blend * blend
    behind = dot((column > row).astype(f32), weighted, precision=lax.Precision.HIGHEST)
    d_optical = d_blend * transmit * survive - behind
    draw_ref[...] = jnp.zeros_like(draw_ref)
    store_gradient(0, d_optical * spacing * jax.nn.sigmoid(raw0))
    for c in range(3):
        store_gradient(1 + c, grads[c] * blend * albedo[c] * (1.0 - albedo[c]))

    g0_ref[...] = jnp.zeros_like(g0_ref)
    g1_ref[...] = jnp.zeros_like(g1_ref)
    on_lanes = (((1,), (1,)), ((), ()))

    def backward(b, carry):
        d_raw = jnp.concatenate(
            [
                draw_ref[k, pl.ds(pl.multiple_of((b * step_block + s) * 8, 8), 8), :]
                for s in range(step_block)
                for k in range(2)
            ],
            axis=1,
        ).astype(bf16)
        h1 = h1_ref[b]
        d_a2 = jnp.where(h2_ref[b] > 0, dot(head_t, d_raw).astype(bf16), jnp.zeros((), bf16))
        d_a1 = jnp.where(h1 > 0, dot(w1, d_a2).astype(bf16), jnp.zeros((), bf16))
        g1_ref[...] += dot(h1, d_a2, on_lanes)
        g0_ref[...] += dot(h0_ref[b], d_a1, on_lanes)
        return carry

    lax.fori_loop(0, blocks, backward, 0)

    g0 = dot(unfold_ref[...], g0_ref[...].astype(bf16)).astype(bf16)
    for n in range(2):
        rows_ref[n] = g1_ref[:, n * 128 : (n + 1) * 128]
    for q in range(4):
        dfield_ref[0:64, q * 256 : (q + 1) * 256] = g0[q * 64 : (q + 1) * 64, :]
        for n in range(2):
            at = slice(q * 256 + n * 128, q * 256 + (n + 1) * 128)
            dfield_ref[64:128, at] = rows_ref[n, pl.ds(q, 64, stride=4), :].astype(bf16)
    d_field = dfield_ref[...]
    own = core_ref[0]
    for out, part in ((keep_ref, own), (send_ref, 1 - own)):
        lhs = jnp.concatenate(
            [xnt_ref[pl.ds(pl.multiple_of(i * 64 + part * 32, 32), 32), :] for i in range(16)], axis=0
        )
        out[...] = dot(lhs, d_field).astype(bf16)


def render(core, latents, weight, gain, head, recv):
    slots = recv.shape[0]
    rays = 2 * slots
    blocks, wide = 64 // step_block, step_block * rays
    fold = fold_matrix()
    vmem = pl.BlockSpec(memory_space=pltpu.VMEM)
    return pl.pallas_call(
        render_kernel,
        out_shape=(
            jax.ShapeDtypeStruct((slots, 128), f32),
            jax.ShapeDtypeStruct(latents.shape, bf16),
            jax.ShapeDtypeStruct((512, 1024), bf16),
            jax.ShapeDtypeStruct((512, 1024), bf16),
        ),
        in_specs=[pl.BlockSpec(memory_space=pltpu.SMEM)] + [vmem] * 7,
        out_specs=(vmem,) * 4,
        scratch_shapes=[
            pltpu.VMEM((256, rays), f32),
            pltpu.VMEM((blocks, features, wide), bf16),
            pltpu.VMEM((blocks, 256, wide), bf16),
            pltpu.VMEM((blocks, 256, wide), bf16),
            pltpu.VMEM((2, 512, slots), f32),
            pltpu.VMEM((2, 512, slots), f32),
            pltpu.VMEM((features, 256), f32),
            pltpu.VMEM((256, 256), f32),
            pltpu.VMEM((2, 256, 128), f32),
            pltpu.VMEM((1024, 128), bf16),
        ],
        compiler_params=pltpu.CompilerParams(vmem_limit_bytes=48 * 1024 * 1024),
        cost_estimate=pl.CostEstimate(flops=12_000_000_000, bytes_accessed=8_000_000, transcendentals=1_000_000),
        name="render",
    )(core, latents, weight, gain, head, recv, jnp.asarray(fold, bf16), jnp.asarray(fold.T, bf16))


def latent_kernel(latent_ref, weight_ref, gain_ref, dfield_ref, out_ref):
    latent = latent_ref[...].astype(f32)
    inv_rms = lax.rsqrt(jnp.mean(latent * latent, axis=1, keepdims=True) + norm_eps)
    x_hat = latent * inv_rms
    d_scaled = dot(dfield_ref[...], weight_ref[...], (((1,), (1,)), ((), ()))) * gain_ref[...]
    mean = jnp.mean(d_scaled * x_hat, axis=1, keepdims=True)
    out_ref[...] = (inv_rms * (d_scaled - x_hat * mean)).astype(bf16)


def latent_gradient(latents, weight, gain, d_field):
    vmem = pl.BlockSpec(memory_space=pltpu.VMEM)
    return pl.pallas_call(
        latent_kernel,
        out_shape=jax.ShapeDtypeStruct(latents.shape, bf16),
        in_specs=[vmem] * 4,
        out_specs=vmem,
        compiler_params=pltpu.CompilerParams(vmem_limit_bytes=24 * 1024 * 1024),
        cost_estimate=pl.CostEstimate(flops=300_000_000, bytes_accessed=3_000_000, transcendentals=0),
        name="latent_gradient",
    )(latents, weight, gain, d_field)


def plane_kernel(terms_ref, weight_ref, gain_ref, sum_ref, gain_out_ref):
    total = terms_ref[0].astype(f32)
    for i in range(1, terms_ref.shape[0]):
        total = total + terms_ref[i].astype(f32)
    sum_ref[...] = total.astype(bf16)
    gain_part = jnp.sum(total * weight_ref[...].astype(f32), axis=1, keepdims=True) / gain_ref[...]
    line = jnp.concatenate([jnp.broadcast_to(gain_part, (32, 128)), jnp.zeros((96, 128), f32)], axis=0).T
    gain_out_ref[...] = line


def plane_sum(terms, weight_rows, gain_rows, slots):
    vmem = pl.BlockSpec(memory_space=pltpu.VMEM)
    return pl.pallas_call(
        plane_kernel,
        out_shape=(
            jax.ShapeDtypeStruct(weight_rows.shape, bf16),
            jax.ShapeDtypeStruct((slots, 128), f32),
        ),
        in_specs=[vmem] * 3,
        out_specs=(vmem,) * 2,
        cost_estimate=pl.CostEstimate(flops=1_000_000, bytes_accessed=1_300_000, transcendentals=0),
        name="plane_sum",
    )(terms, weight_rows, gain_rows)


def unpack_kernel(slot_ref, ret_ref, color_ref, loss_ref, rows_ref):
    rays = color_ref.shape[1]
    lane = lax.broadcasted_iota(jnp.int32, (1, 128), 1)
    for r in range(rays):
        slot = slot_ref[r]
        first = 3 * jnp.bitwise_and(slot, 1)
        kept = jnp.logical_and(lane >= first, lane < first + 3)
        rows_ref[r : r + 1, :] = jnp.where(kept, ret_ref[lax.shift_right_logical(slot, 1)], 0.0)
    turned = rows_ref[...].T
    color_ref[...] = turned[0:3, :] + turned[3:6, :]
    losses = jnp.where(lane == 6, jnp.sum(ret_ref[...], axis=0), 0.0)
    loss_ref[...] = jnp.sum(losses, axis=1, keepdims=True)


def unpack(slot, returned):
    vmem = pl.BlockSpec(memory_space=pltpu.VMEM)
    return pl.pallas_call(
        unpack_kernel,
        out_shape=(
            jax.ShapeDtypeStruct((3, slot.shape[0]), f32),
            jax.ShapeDtypeStruct((1, 1), f32),
        ),
        in_specs=[pl.BlockSpec(memory_space=pltpu.SMEM), vmem],
        out_specs=(vmem,) * 2,
        scratch_shapes=[pltpu.VMEM((slot.shape[0], 128), f32)],
        cost_estimate=pl.CostEstimate(flops=100_000, bytes_accessed=100_000, transcendentals=0),
        name="unpack",
    )(slot, returned)


def body(
    latents,
    head_weight,
    norm_gain,
    color_head,
    sample_points,
    sample_spacing,
    ray_targets,
    ray_scene,
):
    slots = lax.axis_size(both)
    shards = lax.axis_size("shard")
    groups = lax.axis_size("grp")
    shard = lax.axis_index("shard")
    gain_line = norm_gain[None, :]
    weight = lax.all_gather(head_weight, "shard", axis=0, tiled=True)
    sent, slot = pack(ray_scene, sample_points, sample_spacing, ray_targets, slots)
    recv = lax.all_to_all(sent, both, split_axis=0, concat_axis=0, tiled=True).reshape(slots, 640)
    core = (shard % 2).reshape(1).astype(jnp.int32)
    slot_colors, d_field, keep, send = render(core, latents, weight, gain_line, color_head, recv)

    other = lax.ppermute(send, "shard", [(i, i ^ 1) for i in range(shards)])
    paired = (keep.astype(f32) + other.astype(f32)).astype(bf16).reshape(shards // 2, shards, 1024)
    returned = lax.all_to_all(slot_colors.reshape(slots, 1, 128), both, split_axis=0, concat_axis=0, tiled=True)
    same_core = [[i for i in range(shards) if i % 2 == c] for c in range(2)]
    terms = lax.all_to_all(
        paired, "shard", split_axis=0, concat_axis=0, tiled=True, axis_index_groups=same_core
    )
    rendered, loss = unpack(slot, returned)
    latent_grad = latent_gradient(latents, weight, gain_line, d_field)
    gain_rows = lax.dynamic_slice(norm_gain, (shard * shards,), (shards,))[:, None]
    plane, gain_lines = plane_sum(terms, head_weight, gain_rows, slots)
    turns = [
        lax.ppermute(plane, "grp", [(i, (i + k) % groups) for i in range(groups)]).astype(f32)
        for k in range(1, groups)
    ]
    head_grad = (plane.astype(f32) + turns[1]) + (turns[0] + turns[2])
    gains = lax.all_to_all(gain_lines, both, split_axis=0, concat_axis=0, tiled=True)
    norm_gain_grad = jnp.sum(gains[:, :shards].reshape(groups, shards, shards), axis=0).reshape(-1)
    return (rendered, loss.reshape(()), head_grad, norm_gain_grad, latent_grad)


def solution(mesh):
    placed = (
        P(both, None),
        P("shard", None),
        P(),
        P(),
        P(both, None),
        P(both, None),
        P(None, both),
        P(both),
    )
    return jax.shard_map(
        body,
        mesh=mesh,
        in_specs=placed,
        out_specs=(
            P(None, both),
            P(),
            P("shard", None),
            P(),
            P(both, None),
        ),
        check_vma=False,
    )
```

time: 429 us -> 152 us (0.35)
  matrix products: 167 us -> 0 us
  blocking collectives: 65.7 us -> 0 us
  other arithmetic: 32.8 us -> 2.06 us
  Pallas kernels: 0 us -> 27 us
  waiting for transfers between devices: 90.7 us -> 64.5 us
  local copies, waits for them, and re-layouts: 20.1 us -> 6.96 us
  loops' own time: 12.2 us -> 0 us
  starting transfers between devices: 25.5 us -> 35.7 us
    dot_general x99 -> x0, matrix products: 167 us -> none  [the longest x16 73.2 us: render_rays(): jnp.dot(h_zero, w_first, preferred_element_type=jnp.float32) * fan_scale]
    reduce_scatter x1 -> x0, waiting for transfers between devices: 68.3 us -> none  [body(): lax.psum_scatter(lax.dot_general(columns, d_field, (((0,), (0,)), ((), ()...]
    psum x1 -> x0, blocking collectives: 65.7 us -> none  [body(): lax.psum((gain_part, loss_sum), ('grp', 'shard'))]
    pallas_call x0 -> x5, Pallas kernels: none -> 27 us  [the longest x1 19.2 us: render(): pl.pallas_call(render_kernel, out_shape=(jax.ShapeDtypeStruct((slots, 128...]
    all_gather x1, waiting for transfers between devices: 0.02 us -> 24.1 us  [body(): weight = lax.all_gather(head_weight, 'shard', axis=0, tiled=True)]
    reduce_sum x83 -> x1, other arithmetic: 17.5 us -> 0.01 us  [body(): jnp.sum(gains[:, :shards].reshape(groups, shards, shards), axis=0)]
    all_to_all x4, waiting for transfers between devices: 21.7 us -> 37.3 us  [the longest x1 18.3 us: body(): lax.all_to_all(paired, 'shard', split_axis=0, concat_axis=0, tiled=True,...]
    another operation x1 -> x0, loops' own time: 12.2 us -> none  [body(): lax.scan(render_block, (zero_grad, zero_grad, jnp.zeros((), jnp.float32))...]
  transfers between devices with their start and end apart: 7 -> 9, of which waited for: 4 -> 6; matrix products, arithmetic and copies ran while one was open for 3% -> 1% of each run, Pallas kernels for 0% -> 5%
where the time goes in v1:
time: 152 us; the launch traced here: 150 us
  waiting for transfers between devices  64.5 us (42%)
  starting transfers between devices  35.7 us (23%)
  Pallas kernels  27 us (18%)
  between operations  14.1 us (9%)
  local copies, waits for them, and re-layouts  6.96 us (5%)
  other arithmetic  2.06 us (1%)
    all_gather x1, waiting for transfers between devices, body(): weight = lax.all_gather(head_weight, 'shard', axis=0, tiled=True)  24.1 us
    pallas_call x1, Pallas kernels, render(): pl.pallas_call(render_kernel, out_shape=(jax.ShapeDtypeStruct((slots, 128...  19.2 us
    all_to_all x1, waiting for transfers between devices, body(): lax.all_to_all(paired, 'shard', split_axis=0, concat_axis=0, tiled=True,...  18.3 us
    all_to_all x1, waiting for transfers between devices, body(): lax.all_to_all(sent, both, split_axis=0, concat_axis=0, tiled=True)  11.8 us
    all_to_all x1, starting transfers between devices, body(): lax.all_to_all(sent, both, split_axis=0, concat_axis=0, tiled=True)  11.1 us
    all_to_all x1, starting transfers between devices, body(): lax.all_to_all(gain_lines, both, split_axis=0, concat_axis=0, tiled=True)  7.67 us
    all_to_all x1, starting transfers between devices, body(): lax.all_to_all(slot_colors.reshape(slots, 1, 128), both, split_axis=0, co...  6.71 us
    all_to_all x1, waiting for transfers between devices, body(): lax.all_to_all(gain_lines, both, split_axis=0, concat_axis=0, tiled=True)  5.99 us
  transfers between devices with their start and end apart: 9, of which 6 were waited for; matrix products, arithmetic and copies ran while one was open for 1% of the time, Pallas kernels for 5%

profile of v1, /device:TPU:0, one launch (start us, length us, event | category | flops | bytes accessed | tf_op | source)
XLA Modules:
  0.0 150.4 jit_solution(10205715983371695072)
XLA Ops:
  7.9 2.2 %pack.1 = (f32[128,1,640]{2,1,0:T(1,128)}, s32[64]{0:T(128)}) custom-call(s32[64]{0:T(128)} %scene_ref.1, f32[64,192]{1,0:T(8,128)} %points_ref.1, f32[64,64]{1,0:T(8,128)} %spacing_ref.1, f32[3,64]{1,0:T(4,128)} %target_ref.1), custom_call_target="tpu_custom_call" | custom-call | flops 200000 | bytes 1000000 | tf_op jit(solution)/shard_map/pack/pallas_call | solution.py:59
  10.1 11.1 %all-to-all-start = ((f32[128,1,640]{2,1,0:T(1,128)}), f32[128,1,640]{2,1,0:T(1,128)S(1)}, u32[]{:S(2)}, u32[]{:S(2)}) async-start(f32[128,1,640]{2,1,0:T(1,128)} %get-tuple-element.16), calls=%async_computation | async-start | bytes 655360 | tf_op jit(solution)/shard_map/all_to_all | solution.py:380
  21.3 11.8 %all-to-all-done = f32[128,1,640]{2,1,0:T(1,128)S(1)} async-done(((f32[128,1,640]{2,1,0:T(1,128)}), f32[128,1,640]{2,1,0:T(1,128)S(1)}, u32[]{:S(2)}, u32[]{:S(2)}) %all-to-all-start) | async-done | bytes 327712 | tf_op jit(solution)/shard_map/all_to_all | solution.py:380
  33.1 24.1 %all-gather.2.cloned.1.call-done.weight_ref = bf16[1024,1024]{1,0:T(8,128)(2,1)} async-done(((bf16[32,1024]{1,0:T(8,128)(2,1)}), bf16[1024,1024]{1,0:T(8,128)(2,1)}) %all-gather.2.cloned.1.call-update) | async-done | bytes 2097168 | tf_op jit(solution)/shard_map/all_gather | solution.py:378
  57.2 1.6 %copy-done = bf16[1024,1024]{1,0:T(8,128)(2,1)S(1)} copy-done((bf16[1024,1024]{1,0:T(8,128)(2,1)S(1)}, bf16[1024,1024]{1,0:T(8,128)(2,1)}, u32[]{:S(2)}) %copy-start) | copy-done | bytes 2097176
  58.8 0.9 copy-done.2
  61.1 0.8 copy-done.7
  61.9 0.7 copy-done.8
  62.7 19.2 %render.1 = (f32[128,128]{1,0:T(8,128)}, bf16[128,1024]{1,0:T(8,128)(2,1)S(1)}, bf16[512,1024]{1,0:T(8,128)(2,1)S(1)}, bf16[512,1024]{1,0:T(8,128)(2,1)S(1)}) custom-call(s32[1]{0:T(128)} %bitcast.core_ref, bf16[128,1024]{1,0:T(8,128)(2,1)S(1)} %copy-done.2, bf16[1024,1024]{1,0:T(8,128)(2,1)S(1)} %copy-done, f32[1,1024]{1,0:T(1,128)S(1)} %bitcast.17, ...), custom_call_target="tpu_custom_call" | custom-call | flops 12000000000 | bytes 8000000 | tf_op jit(solution)/shard_map/render/pallas_call | solution.py:258
  82.1 2.4 %collective-permute-done = bf16[512,1024]{1,0:T(8,128)(2,1)S(1)} collective-permute-done((bf16[512,1024]{1,0:T(8,128)(2,1)S(1)}, bf16[512,1024]{1,0:T(8,128)(2,1)S(1)}, u32[]{:S(2)}, u32[]{:S(2)}) %collective-permute-start) | collective-permute-done | bytes 1048608 | tf_op jit(solution)/shard_map/ppermute | solution.py:384
  84.5 1.4 add_convert_fusion
  85.9 5.0 %all-to-all-start.2 = ((bf16[16,32,1024]{2,1,0:T(8,128)(2,1)}), bf16[16,32,1024]{2,1,0:T(8,128)(2,1)}, u32[]{:S(2)}, u32[]{:S(2)}) async-start(bf16[16,32,1024]{2,1,0:T(8,128)(2,1)} %bitcast.19), calls=%async_computation.2 | async-start | bytes 2097152 | tf_op jit(solution)/shard_map/all_to_all | solution.py:388
  90.9 18.3 %all-to-all-done.2.terms_ref = bf16[16,32,1024]{2,1,0:T(8,128)(2,1)} async-done(((bf16[16,32,1024]{2,1,0:T(8,128)(2,1)}), bf16[16,32,1024]{2,1,0:T(8,128)(2,1)}, u32[]{:S(2)}, u32[]{:S(2)}) %all-to-all-start.2) | async-done | bytes 1048608 | tf_op jit(solution)/shard_map/all_to_all | solution.py:388
  109.2 6.7 %all-to-all-start.1 = ((f32[128,1,128]{2,1,0:T(1,128)}), f32[128,1,128]{2,1,0:T(1,128)S(1)}, u32[]{:S(2)}, u32[]{:S(2)}) async-start(f32[128,1,128]{2,1,0:T(1,128)} %bitcast.2), calls=%async_computation.1 | async-start | bytes 131072 | tf_op jit(solution)/shard_map/all_to_all | solution.py:386
  116.0 0.7 copy.17.gain_ref
  116.7 2.3 %plane_sum.1 = (bf16[32,1024]{1,0:T(8,128)(2,1)}, f32[128,128]{1,0:T(8,128)}) custom-call(bf16[16,32,1024]{2,1,0:T(8,128)(2,1)} %all-to-all-done.2.terms_ref, bf16[32,1024]{1,0:T(8,128)(2,1)} %weight_ref.1, f32[32,1]{1,0:T(8,128)} %copy.17.gain_ref), custom_call_target="tpu_custom_call" | custom-call | flops 1000000 | bytes 1300000 | tf_op jit(solution)/shard_map/plane_sum/pallas_call | solution.py:320
  119.0 2.8 %collective-permute-start.3 = (bf16[32,1024]{1,0:T(8,128)(2,1)}, bf16[32,1024]{1,0:T(8,128)(2,1)S(1)}, u32[]{:S(2)}, u32[]{:S(2)}) collective-permute-start(bf16[32,1024]{1,0:T(8,128)(2,1)} %get-tuple-element.22), channel_id=1, source_target_pairs={{0,96},{32,0},{64,32},{96,64},{1,97},{33,1},{65,33},{97,65},{2,98}... | collective-permute-start | bytes 196616 | tf_op jit(solution)/shard_map/ppermute | solution.py:396
  121.8 2.0 %collective-permute-start.1 = (bf16[32,1024]{1,0:T(8,128)(2,1)}, bf16[32,1024]{1,0:T(8,128)(2,1)S(1)}, u32[]{:S(2)}, u32[]{:S(2)}) collective-permute-start(bf16[32,1024]{1,0:T(8,128)(2,1)} %get-tuple-element.22), channel_id=1, source_target_pairs={{0,64},{32,96},{64,0},{96,32},{1,65},{33,97},{65,1},{97,33},{2,66}... | collective-permute-start | bytes 196616 | tf_op jit(solution)/shard_map/ppermute | solution.py:396
  123.8 1.3 all-to-all-done.1.ret_ref
  125.1 7.7 %all-to-all-start.3 = ((f32[128,1,128]{2,1,0:T(1,128)}), f32[128,1,128]{2,1,0:T(1,128)S(1)}, u32[]{:S(2)}, u32[]{:S(2)}) async-start(f32[128,1,128]{2,1,0:T(1,128)} %bitcast.21), calls=%async_computation.3 | async-start | bytes 131072 | tf_op jit(solution)/shard_map/all_to_all | solution.py:400
  132.8 1.6 %latent_gradient.1 = bf16[128,1024]{1,0:T(8,128)(2,1)} custom-call(bf16[128,1024]{1,0:T(8,128)(2,1)S(1)} %copy-done.3, bf16[1024,1024]{1,0:T(8,128)(2,1)S(1)} %copy-done.1, f32[1,1024]{1,0:T(1,128)S(1)} %bitcast.18, bf16[128,1024]{1,0:T(8,128)(2,1)S(1)} %get-tuple-element.24.dfield_ref), custom_call_target="tpu_custom_call" | custom-call | flops 300000000 | bytes 3000000 | tf_op jit(solution)/shard_map/latent_gradient/pallas_call | solution.py:297
  134.5 1.7 %unpack.1 = (f32[3,64]{1,0:T(4,128)}, f32[1,1]{1,0:T(1,128)}) custom-call(s32[64]{0:T(128)} %get-tuple-element.15.slot_ref, f32[128,1,128]{2,1,0:T(1,128)} %copy-done.9), custom_call_target="tpu_custom_call" | custom-call | flops 100000 | bytes 100000 | tf_op jit(solution)/shard_map/unpack/pallas_call | solution.py:349
  136.1 6.0 %all-to-all-done.3 = f32[128,1,128]{2,1,0:T(1,128)S(1)} async-done(((f32[128,1,128]{2,1,0:T(1,128)}), f32[128,1,128]{2,1,0:T(1,128)S(1)}, u32[]{:S(2)}, u32[]{:S(2)}) %all-to-all-start.3) | async-done | bytes 65568 | tf_op jit(solution)/shard_map/all_to_all | solution.py:400
  142.8 0.7 add_add_fusion
  (29 shorter events, 3.2 us)
Async XLA Ops:
  7.2 50.0 %all-gather.2.cloned.1.call-start = ((), (), s32[]{:S(2)}) async-start(), calls=%async_computation.4 | async-start | bytes 2162688 | tf_op jit(solution)/shard_map/all_gather | solution.py:378
  10.1 22.9 %all-to-all-start = ((f32[128,1,640]{2,1,0:T(1,128)}), f32[128,1,640]{2,1,0:T(1,128)S(1)}, u32[]{:S(2)}, u32[]{:S(2)}) async-start(f32[128,1,640]{2,1,0:T(1,128)} %get-tuple-element.16), calls=%async_computation | async-start | bytes 655360 | tf_op jit(solution)/shard_map/all_to_all | solution.py:380
  57.2 1.6 %copy-start = (bf16[1024,1024]{1,0:T(8,128)(2,1)S(1)}, bf16[1024,1024]{1,0:T(8,128)(2,1)}, u32[]{:S(2)}) copy-start(bf16[1024,1024]{1,0:T(8,128)(2,1)} %all-gather.2.cloned.1.call-done.weight_ref) | copy-start | bytes 6291460
  58.8 0.9 copy-start.2
  59.7 0.7 copy-start.4
  60.4 0.7 copy-start.6
  61.1 0.8 copy-start.7
  61.9 0.7 copy-start.8
  81.9 2.7 %collective-permute-start = (bf16[512,1024]{1,0:T(8,128)(2,1)S(1)}, bf16[512,1024]{1,0:T(8,128)(2,1)S(1)}, u32[]{:S(2)}, u32[]{:S(2)}) collective-permute-start(bf16[512,1024]{1,0:T(8,128)(2,1)S(1)} %get-tuple-element.21), channel_id=1, source_target_pairs={{0,1},{1,0},{2,3},{3,2},{4,5},{5,4},{6,7},{7,6},{8,9},{9,8},{10,11... | collective-permute-start | bytes 3145736 | tf_op jit(solution)/shard_map/ppermute | solution.py:384
  84.5 31.4 %copy-start.5 = (f32[1024]{0:T(1024)S(1)}, f32[1024]{0:T(1024)}, u32[]{:S(2)}) copy-start(f32[1024]{0:T(1024)} %param.12) | copy-start | bytes 12292
  85.9 46.9 %copy-start.1 = (bf16[1024,1024]{1,0:T(8,128)(2,1)S(1)}, bf16[1024,1024]{1,0:T(8,128)(2,1)}, u32[]{:S(2)}) copy-start(bf16[1024,1024]{1,0:T(8,128)(2,1)} %all-gather.2.cloned.1.call-done.weight_ref) | copy-start | bytes 6291460
  85.9 46.9 %copy-start.3 = (bf16[128,1024]{1,0:T(8,128)(2,1)S(1)}, bf16[128,1024]{1,0:T(8,128)(2,1)}, u32[]{:S(2)}) copy-start(bf16[128,1024]{1,0:T(8,128)(2,1)} %latent_ref.3) | copy-start | bytes 786436
  85.9 23.3 %all-to-all-start.2 = ((bf16[16,32,1024]{2,1,0:T(8,128)(2,1)}), bf16[16,32,1024]{2,1,0:T(8,128)(2,1)}, u32[]{:S(2)}, u32[]{:S(2)}) async-start(bf16[16,32,1024]{2,1,0:T(8,128)(2,1)} %bitcast.19), calls=%async_computation.2 | async-start | bytes 2097152 | tf_op jit(solution)/shard_map/all_to_all | solution.py:388
  109.2 16.0 %all-to-all-start.1 = ((f32[128,1,128]{2,1,0:T(1,128)}), f32[128,1,128]{2,1,0:T(1,128)S(1)}, u32[]{:S(2)}, u32[]{:S(2)}) async-start(f32[128,1,128]{2,1,0:T(1,128)} %bitcast.2), calls=%async_computation.1 | async-start | bytes 131072 | tf_op jit(solution)/shard_map/all_to_all | solution.py:386
  119.0 23.9 %copy-start.10 = (bf16[32,1024]{1,0:T(8,128)(2,1)S(1)}, bf16[32,1024]{1,0:T(8,128)(2,1)}, u32[]{:S(2)}) copy-start(bf16[32,1024]{1,0:T(8,128)(2,1)} %get-tuple-element.22) | copy-start | bytes 196612
  119.0 23.8 %collective-permute-start.3 = (bf16[32,1024]{1,0:T(8,128)(2,1)}, bf16[32,1024]{1,0:T(8,128)(2,1)S(1)}, u32[]{:S(2)}, u32[]{:S(2)}) collective-permute-start(bf16[32,1024]{1,0:T(8,128)(2,1)} %get-tuple-element.22), channel_id=1, source_target_pairs={{0,96},{32,0},{64,32},{96,64},{1,97},{33,1},{65,33},{97,65},{2,98}... | collective-permute-start | bytes 196616 | tf_op jit(solution)/shard_map/ppermute | solution.py:396
  121.8 21.0 %collective-permute-start.2 = (bf16[32,1024]{1,0:T(8,128)(2,1)}, bf16[32,1024]{1,0:T(8,128)(2,1)S(1)}, u32[]{:S(2)}, u32[]{:S(2)}) collective-permute-start(bf16[32,1024]{1,0:T(8,128)(2,1)} %get-tuple-element.22), channel_id=1, source_target_pairs={{0,32},{32,64},{64,96},{96,0},{1,33},{33,65},{65,97},{97,1},{2,34}... | collective-permute-start | bytes 196616 | tf_op jit(solution)/shard_map/ppermute | solution.py:396
  121.8 21.0 %collective-permute-start.1 = (bf16[32,1024]{1,0:T(8,128)(2,1)}, bf16[32,1024]{1,0:T(8,128)(2,1)S(1)}, u32[]{:S(2)}, u32[]{:S(2)}) collective-permute-start(bf16[32,1024]{1,0:T(8,128)(2,1)} %get-tuple-element.22), channel_id=1, source_target_pairs={{0,64},{32,96},{64,0},{96,32},{1,65},{33,97},{65,1},{97,33},{2,66}... | collective-permute-start | bytes 196616 | tf_op jit(solution)/shard_map/ppermute | solution.py:396
  125.1 9.3 %copy-start.9 = (f32[128,1,128]{2,1,0:T(1,128)}, f32[128,1,128]{2,1,0:T(1,128)S(1)}, u32[]{:S(2)}) copy-start(f32[128,1,128]{2,1,0:T(1,128)S(1)} %all-to-all-done.1.ret_ref) | copy-start | bytes 196612
  125.1 17.0 %all-to-all-start.3 = ((f32[128,1,128]{2,1,0:T(1,128)}), f32[128,1,128]{2,1,0:T(1,128)S(1)}, u32[]{:S(2)}, u32[]{:S(2)}) async-start(f32[128,1,128]{2,1,0:T(1,128)} %bitcast.21), calls=%async_computation.3 | async-start | bytes 131072 | tf_op jit(solution)/shard_map/all_to_all | solution.py:400
Sparse Core Ops, SparseCore 0:
  10.3 46.8 all-gather.1

commit v2 on v1

--- a/solution.py
+++ b/solution.py
@@ -1,6 +1,5 @@
 import jax
 import jax.numpy as jnp
-import numpy as np
 from jax import lax
 from jax.experimental import pallas as pl
 from jax.experimental.pallas import tpu as pltpu
@@ -18,12 +17,15 @@
 
 
 def fold_matrix():
-    fold = np.zeros((features, 256), np.float32)
-    for j in range(256):
-        jm = j % features
-        m = (jm % 3) * 16 + (jm // 3 % 2) * 8 + jm // 6
-        fold[m, (j % 4) * 64 + j // 4] = 1.0
-    return fold
+    m = lax.broadcasted_iota(jnp.int32, (features, 256), 0).astype(f32)
+    i = lax.broadcasted_iota(jnp.int32, (features, 256), 1).astype(f32)
+    q = jnp.floor(i * (1 / 64) + 1 / 128)
+    j = 4.0 * (i - 64.0 * q) + q
+    jm = j - features * jnp.floor((j + 0.5) * (1 / features))
+    coordinate = jnp.floor((m + 0.5) * (1 / 16))
+    phase = jnp.floor((m - 16.0 * coordinate + 0.5) * (1 / 8))
+    octave = m - 16.0 * coordinate - 8.0 * phase
+    return (jm == coordinate + 3.0 * phase + 6.0 * octave).astype(f32)
 
 
 def dot(a, b, dims=(((1,), (0,)), ((), ())), precision=None):
@@ -74,6 +76,63 @@
     )(ray_scene, points, spacing, targets)
 
 
+def field_kernel(
+    core_ref,
+    latent_ref,
+    own_ref,
+    other_ref,
+    gain_ref,
+    weight_ref,
+    w0t_ref,
+    w1_ref,
+    w1t_ref,
+    keep_ref,
+    send_ref,
+    rows_ref,
+    turned_ref,
+):
+    scale = 1.0 / 16.0
+    own = core_ref[0]
+    for i in range(16):
+        for part, ref in ((own, own_ref), (1 - own, other_ref)):
+            weight_ref[pl.ds(pl.multiple_of(i * 64 + part * 32, 32), 32), :] = ref[i * 32 : (i + 1) * 32, :]
+    latent = latent_ref[...].astype(f32)
+    inv_rms = lax.rsqrt(jnp.mean(latent * latent, axis=1, keepdims=True) + norm_eps)
+    normed = latent * inv_rms * gain_ref[...]
+    field = dot(normed.astype(bf16), weight_ref[...]).astype(bf16)
+    stacked = jnp.concatenate([field[0:64, q * 256 : (q + 1) * 256] for q in range(4)], axis=0)
+    folded = dot(fold_matrix().astype(bf16), stacked) * scale
+    high = folded.astype(bf16).astype(f32)
+    split = jnp.concatenate([high, folded - high, jnp.zeros((32, 256), f32)], axis=0)
+    w0t_ref[...] = split.T.astype(bf16)
+    field1 = field[64:128, :].astype(f32) * scale
+    for q in range(4):
+        for n in range(2):
+            rows_ref[n, pl.ds(q, 64, stride=4), :] = field1[:, q * 256 + n * 128 : q * 256 + (n + 1) * 128]
+    w1f = jnp.concatenate([rows_ref[0], rows_ref[1]], axis=1)
+    w1_ref[...] = w1f.astype(bf16)
+    w1t_ref[...] = w1f.T.astype(bf16)
+    turned_ref[...] = normed.T.astype(bf16)
+    for out, part in ((keep_ref, own), (send_ref, 1 - own)):
+        for i in range(16):
+            out[i * 32 : (i + 1) * 32, :] = turned_ref[pl.ds(pl.multiple_of(i * 64 + part * 32, 32), 32), :]
+
+
+def make_field(core, latents, own_rows, other_rows, gain):
+    vmem = pl.BlockSpec(memory_space=pltpu.VMEM)
+    shapes = ((1024, 1024), (256, 128), (256, 256), (256, 256), (512, 128), (512, 128))
+    return pl.pallas_call(
+        field_kernel,
+        out_shape=tuple(jax.ShapeDtypeStruct(shape, bf16) for shape in shapes),
+        in_specs=[pl.BlockSpec(memory_space=pltpu.SMEM)] + [vmem] * 4,
+        out_specs=(vmem,) * 6,
+        scratch_shapes=[pltpu.VMEM((2, 256, 128), f32), pltpu.VMEM((1024, 128), bf16)],
+        compiler_params=pltpu.CompilerParams(vmem_limit_bytes=24 * 1024 * 1024),
+        cost_estimate=pl.CostEstimate(flops=400_000_000, bytes_accessed=5_000_000, transcendentals=0),
+        name="field",
+    )(core, latents, own_rows, other_rows, gain)
+
+
 def horner(u, coef):
     value = coef[-1] * u + coef[-2]
     for c in coef[-3::-1]:
@@ -82,18 +141,13 @@
 
 
 def render_kernel(
-    core_ref,
-    latent_ref,
-    weight_ref,
-    gain_ref,
+    recv_ref,
+    w0t_ref,
+    w1_ref,
+    w1t_ref,
     head_ref,
-    recv_ref,
-    fold_ref,
-    unfold_ref,
     color_ref,
     dfield_ref,
-    keep_ref,
-    send_ref,
     rays_ref,
     h0_ref,
     h1_ref,
@@ -103,35 +157,18 @@
     g0_ref,
     g1_ref,
     rows_ref,
-    xnt_ref,
 ):
     scale = 1.0 / 16.0
     slots = recv_ref.shape[0]
     rays = 2 * slots
-    wide = step_block * rays
     blocks = 64 // step_block
 
     for k in range(2):
         rays_ref[0:256, k * slots : (k + 1) * slots] = recv_ref[:, k * 256 : (k + 1) * 256].T
     tint = recv_ref[:, 512:640].T
-
-    latent = latent_ref[...].astype(f32)
-    inv_rms = lax.rsqrt(jnp.mean(latent * latent, axis=1, keepdims=True) + norm_eps)
-    normed = latent * inv_rms * gain_ref[...]
-    xnt_ref[...] = normed.T.astype(bf16)
-    field = dot(normed.astype(bf16), weight_ref[...]).astype(bf16)
-    stacked = jnp.concatenate([field[0:64, q * 256 : (q + 1) * 256] for q in range(4)], axis=0)
-    folded = dot(fold_ref[...], stacked) * scale
-    high = folded.astype(bf16).astype(f32)
-    split = jnp.concatenate([high, folded - high, jnp.zeros((32, 256), f32)], axis=0)
-    w0t = split.T.astype(bf16)[:, 0:96]
-    field1 = field[64:128, :].astype(f32) * scale
-    for q in range(4):
-        for n in range(2):
-            rows_ref[n, pl.ds(q, 64, stride=4), :] = field1[:, q * 256 + n * 128 : q * 256 + (n + 1) * 128]
-    w1f = jnp.concatenate([rows_ref[0], rows_ref[1]], axis=1)
-    w1 = w1f.astype(bf16)
-    w1t = w1f.T.astype(bf16)
+    w0t = w0t_ref[:, 0:96]
+    w1 = w1_ref[...]
+    w1t = w1t_ref[...]
     head_f = jnp.concatenate([head_ref[...].astype(f32), jnp.zeros((4, 256), f32)], axis=0)
     head = head_f.astype(bf16)
     head_t = (head_f * scale).T.astype(bf16)
@@ -200,8 +237,8 @@
         grads.append(grad)
     loss = jnp.sum(square, axis=1, keepdims=True) * factor
     rows = [colors[c][:, k * slots : (k + 1) * slots] for k in range(2) for c in range(3)]
-    rows += [jnp.broadcast_to(loss, (1, slots)), jnp.zeros((slots - 7, slots), f32)]
-    color_ref[...] = jnp.concatenate(rows, axis=0).T
+    rows = [jnp.zeros((40, slots), f32), *rows, jnp.broadcast_to(loss, (1, slots))]
+    color_ref[...] = jnp.concatenate([*rows, jnp.zeros((slots - 47, slots), f32)], axis=0).T
     weighted = d_blend * blend
     behind = dot((column > row).astype(f32), weighted, precision=lax.Precision.HIGHEST)
     d_optical = d_blend * transmit * survive - behind
@@ -232,7 +269,8 @@
 
     lax.fori_loop(0, blocks, backward, 0)
 
-    g0 = dot(unfold_ref[...], g0_ref[...].astype(bf16)).astype(bf16)
+    unfold = jnp.concatenate([fold_matrix(), jnp.zeros((80, 256), f32)], axis=0).T[:, 0:features].astype(bf16)
+    g0 = dot(unfold, g0_ref[...].astype(bf16)).astype(bf16)
     for n in range(2):
         rows_ref[n] = g1_ref[:, n * 128 : (n + 1) * 128]
     for q in range(4):
@@ -240,31 +278,21 @@
         for n in range(2):
             at = slice(q * 256 + n * 128, q * 256 + (n + 1) * 128)
             dfield_ref[64:128, at] = rows_ref[n, pl.ds(q, 64, stride=4), :].astype(bf16)
-    d_field = dfield_ref[...]
-    own = core_ref[0]
-    for out, part in ((keep_ref, own), (send_ref, 1 - own)):
-        lhs = jnp.concatenate(
-            [xnt_ref[pl.ds(pl.multiple_of(i * 64 + part * 32, 32), 32), :] for i in range(16)], axis=0
-        )
-        out[...] = dot(lhs, d_field).astype(bf16)
-
-
-def render(core, latents, weight, gain, head, recv):
+
+
+def render(recv, w0t, w1, w1t, head):
     slots = recv.shape[0]
     rays = 2 * slots
     blocks, wide = 64 // step_block, step_block * rays
-    fold = fold_matrix()
     vmem = pl.BlockSpec(memory_space=pltpu.VMEM)
     return pl.pallas_call(
         render_kernel,
         out_shape=(
             jax.ShapeDtypeStruct((slots, 128), f32),
-            jax.ShapeDtypeStruct(latents.shape, bf16),
-            jax.ShapeDtypeStruct((512, 1024), bf16),
-            jax.ShapeDtypeStruct((512, 1024), bf16),
+            jax.ShapeDtypeStruct((128, 1024), bf16),
         ),
-        in_specs=[pl.BlockSpec(memory_space=pltpu.SMEM)] + [vmem] * 7,
-        out_specs=(vmem,) * 4,
+        in_specs=[vmem] * 5,
+        out_specs=(vmem,) * 2,
         scratch_shapes=[
             pltpu.VMEM((256, rays), f32),
             pltpu.VMEM((blocks, features, wide), bf16),
@@ -275,12 +303,28 @@
             pltpu.VMEM((features, 256), f32),
             pltpu.VMEM((256, 256), f32),
             pltpu.VMEM((2, 256, 128), f32),
-            pltpu.VMEM((1024, 128), bf16),
         ],
-        compiler_params=pltpu.CompilerParams(vmem_limit_bytes=48 * 1024 * 1024),
-        cost_estimate=pl.CostEstimate(flops=12_000_000_000, bytes_accessed=8_000_000, transcendentals=1_000_000),
+        compiler_params=pltpu.CompilerParams(vmem_limit_bytes=44 * 1024 * 1024),
+        cost_estimate=pl.CostEstimate(flops=12_000_000_000, bytes_accessed=2_000_000, transcendentals=1_000_000),
         name="render",
-    )(core, latents, weight, gain, head, recv, jnp.asarray(fold, bf16), jnp.asarray(fold.T, bf16))
+    )(recv, w0t, w1, w1t, head)
+
+
+def pair_kernel(keep_ref, other_ref, dfield_ref, dother_ref, out_ref):
+    out_ref[...] = (dot(keep_ref[...], dfield_ref[...]) + dot(other_ref[...], dother_ref[...])).astype(bf16)
+
+
+def pair_terms(keep, other, d_field, d_other):
+    vmem = pl.BlockSpec(memory_space=pltpu.VMEM)
+    return pl.pallas_call(
+        pair_kernel,
+        out_shape=jax.ShapeDtypeStruct((512, 1024), bf16),
+        in_specs=[vmem] * 4,
+        out_specs=vmem,
+        compiler_params=pltpu.CompilerParams(vmem_limit_bytes=16 * 1024 * 1024),
+        cost_estimate=pl.CostEstimate(flops=270_000_000, bytes_accessed=2_000_000, transcendentals=0),
+        name="pair_terms",
+    )(keep, other, d_field, d_other)
 
 
 def latent_kernel(latent_ref, weight_ref, gain_ref, dfield_ref, out_ref):
@@ -305,59 +349,66 @@
     )(latents, weight, gain, d_field)
 
 
-def plane_kernel(terms_ref, weight_ref, gain_ref, sum_ref, gain_out_ref):
+def plane_kernel(terms_ref, weight_ref, color_ref, sum_ref, line_ref):
     total = terms_ref[0].astype(f32)
     for i in range(1, terms_ref.shape[0]):
         total = total + terms_ref[i].astype(f32)
     sum_ref[...] = total.astype(bf16)
-    gain_part = jnp.sum(total * weight_ref[...].astype(f32), axis=1, keepdims=True) / gain_ref[...]
-    line = jnp.concatenate([jnp.broadcast_to(gain_part, (32, 128)), jnp.zeros((96, 128), f32)], axis=0).T
-    gain_out_ref[...] = line
-
-
-def plane_sum(terms, weight_rows, gain_rows, slots):
+    part = jnp.sum(total * weight_ref[...].astype(f32), axis=1, keepdims=True)
+    line = jnp.concatenate([jnp.broadcast_to(part, (32, 128)), jnp.zeros((96, 128), f32)], axis=0).T
+    line_ref[...] = line + color_ref[...]
+
+
+def plane_sum(terms, weight_rows, colors):
     vmem = pl.BlockSpec(memory_space=pltpu.VMEM)
     return pl.pallas_call(
         plane_kernel,
         out_shape=(
             jax.ShapeDtypeStruct(weight_rows.shape, bf16),
-            jax.ShapeDtypeStruct((slots, 128), f32),
+            jax.ShapeDtypeStruct(colors.shape, f32),
         ),
         in_specs=[vmem] * 3,
         out_specs=(vmem,) * 2,
         cost_estimate=pl.CostEstimate(flops=1_000_000, bytes_accessed=1_300_000, transcendentals=0),
         name="plane_sum",
-    )(terms, weight_rows, gain_rows)
-
-
-def unpack_kernel(slot_ref, ret_ref, color_ref, loss_ref, rows_ref):
+    )(terms, weight_rows, colors)
+
+
+def unpack_kernel(slot_ref, ret_ref, gain_ref, color_ref, loss_ref, gain_out_ref, rows_ref):
     rays = color_ref.shape[1]
     lane = lax.broadcasted_iota(jnp.int32, (1, 128), 1)
+    total = ret_ref[0:32, 0, :]
+    for z in range(1, 4):
+        total = total + ret_ref[z * 32 : (z + 1) * 32, 0, :]
+    rows_ref[0:32, :] = total
+    gains = [rows_ref[pl.ds(i, 8, stride=4), :][:, 0:32] for i in range(4)]
+    gain_out_ref[...] = jnp.concatenate(gains, axis=1) / gain_ref[...]
     for r in range(rays):
         slot = slot_ref[r]
-        first = 3 * jnp.bitwise_and(slot, 1)
+        first = 40 + 3 * jnp.bitwise_and(slot, 1)
         kept = jnp.logical_and(lane >= first, lane < first + 3)
         rows_ref[r : r + 1, :] = jnp.where(kept, ret_ref[lax.shift_right_logical(slot, 1)], 0.0)
     turned = rows_ref[...].T
-    color_ref[...] = turned[0:3, :] + turned[3:6, :]
-    losses = jnp.where(lane == 6, jnp.sum(ret_ref[...], axis=0), 0.0)
+    color_ref[...] = turned[40:43, :] + turned[43:46, :]
+    losses = jnp.where(lane == 46, jnp.sum(ret_ref[...], axis=0), 0.0)
     loss_ref[...] = jnp.sum(losses, axis=1, keepdims=True)
 
 
-def unpack(slot, returned):
+def unpack(slot, returned, gain):
     vmem = pl.BlockSpec(memory_space=pltpu.VMEM)
     return pl.pallas_call(
         unpack_kernel,
         out_shape=(
             jax.ShapeDtypeStruct((3, slot.shape[0]), f32),
             jax.ShapeDtypeStruct((1, 1), f32),
+            jax.ShapeDtypeStruct(gain.shape, f32),
         ),
-        in_specs=[pl.BlockSpec(memory_space=pltpu.SMEM), vmem],
-        out_specs=(vmem,) * 2,
+        in_specs=[pl.BlockSpec(memory_space=pltpu.SMEM), vmem, vmem],
+        out_specs=(vmem,) * 3,
         scratch_shapes=[pltpu.VMEM((slot.shape[0], 128), f32)],
         cost_estimate=pl.CostEstimate(flops=100_000, bytes_accessed=100_000, transcendentals=0),
         name="unpack",
-    )(slot, returned)
+    )(slot, returned, gain)
 
 
 def body(
@@ -373,33 +424,39 @@
     slots = lax.axis_size(both)
     shards = lax.axis_size("shard")
     groups = lax.axis_size("grp")
-    shard = lax.axis_index("shard")
+    core = (lax.axis_index("shard") % 2).reshape(1).astype(jnp.int32)
     gain_line = norm_gain[None, :]
-    weight = lax.all_gather(head_weight, "shard", axis=0, tiled=True)
+    same_core = [[i for i in range(shards) if i % 2 == c] for c in range(2)]
+    across = [(i, i ^ 1) for i in range(shards)]
+
+    def among_same_core(x):
+        return lax.all_to_all(x, "shard", split_axis=0, concat_axis=0, tiled=True, axis_index_groups=same_core)
+
+    def among_all(x):
+        return lax.all_to_all(x, both, split_axis=0, concat_axis=0, tiled=True)
+
+    own_rows = among_same_core(jnp.broadcast_to(head_weight[None], (shards // 2, *head_weight.shape)))
+    own_rows = own_rows.reshape(512, 1024)
     sent, slot = pack(ray_scene, sample_points, sample_spacing, ray_targets, slots)
-    recv = lax.all_to_all(sent, both, split_axis=0, concat_axis=0, tiled=True).reshape(slots, 640)
-    core = (shard % 2).reshape(1).astype(jnp.int32)
-    slot_colors, d_field, keep, send = render(core, latents, weight, gain_line, color_head, recv)
-
-    other = lax.ppermute(send, "shard", [(i, i ^ 1) for i in range(shards)])
-    paired = (keep.astype(f32) + other.astype(f32)).astype(bf16).reshape(shards // 2, shards, 1024)
-    returned = lax.all_to_all(slot_colors.reshape(slots, 1, 128), both, split_axis=0, concat_axis=0, tiled=True)
-    same_core = [[i for i in range(shards) if i % 2 == c] for c in range(2)]
-    terms = lax.all_to_all(
-        paired, "shard", split_axis=0, concat_axis=0, tiled=True, axis_index_groups=same_core
-    )
-    rendered, loss = unpack(slot, returned)
+    sent, own_rows = lax.optimization_barrier((sent, own_rows))
+    other_rows = lax.ppermute(own_rows, "shard", across)
+    recv = among_all(sent).reshape(slots, 640)
+    weight, w0t, w1, w1t, keep, send = make_field(core, latents, own_rows, other_rows, gain_line)
+    x_other = lax.ppermute(send, "shard", across)
+    colors, d_field = render(recv, w0t, w1, w1t, color_head)
+    d_other = lax.ppermute(d_field, "shard", across)
+    paired = pair_terms(keep, x_other, d_field, d_other)
+    terms = among_same_core(paired.reshape(shards // 2, shards, 1024))
     latent_grad = latent_gradient(latents, weight, gain_line, d_field)
-    gain_rows = lax.dynamic_slice(norm_gain, (shard * shards,), (shards,))[:, None]
-    plane, gain_lines = plane_sum(terms, head_weight, gain_rows, slots)
+    plane, lines = plane_sum(terms, head_weight, colors)
     turns = [
         lax.ppermute(plane, "grp", [(i, (i + k) % groups) for i in range(groups)]).astype(f32)
         for k in range(1, groups)
     ]
     head_grad = (plane.astype(f32) + turns[1]) + (turns[0] + turns[2])
-    gains = lax.all_to_all(gain_lines, both, split_axis=0, concat_axis=0, tiled=True)
-    norm_gain_grad = jnp.sum(gains[:, :shards].reshape(groups, shards, shards), axis=0).reshape(-1)
-    return (rendered, loss.reshape(()), head_grad, norm_gain_grad, latent_grad)
+    returned = among_all(lines.reshape(slots, 1, 128))
+    rendered, loss, gain_grad = unpack(slot, returned, norm_gain.reshape(8, 128))
+    return (rendered, loss.reshape(()), head_grad, gain_grad.reshape(-1), latent_grad)
 
 
 def solution(mesh):

time: 152 us -> 115 us (0.76)
  waiting for transfers between devices: 64.5 us -> 35.8 us
  blocking collectives: 0 us -> 21 us
  between operations: 14.1 us -> 0.79 us
  starting transfers between devices: 35.7 us -> 24.1 us
  local copies, waits for them, and re-layouts: 6.96 us -> 4.89 us
    all_gather x1 -> x0, waiting for transfers between devices: 24.1 us -> none  [body(): weight = lax.all_gather(head_weight, 'shard', axis=0, tiled=True)]
    all_to_all x0 -> x1, blocking collectives: none -> 21 us  [among_same_core(): lax.all_to_all(x, 'shard', split_axis=0, concat_axis=0, tiled=True, axis_...]
    all_to_all x4 -> x3, starting transfers between devices: 30.5 us -> 20.4 us  [the longest x2 13.3 us: among_all(): return lax.all_to_all(x, both, split_axis=0, concat_axis=0, tiled=True)]
    all_to_all x4 -> x3, waiting for transfers between devices: 37.3 us -> 34.5 us  [the longest x2 19.1 us: among_all(): return lax.all_to_all(x, both, split_axis=0, concat_axis=0, tiled=True)]
    unnamed x23 -> x17, local copies, waits for them, and re-layouts: 5.52 us -> 2.89 us
    ppermute x3, starting transfers between devices: 4.88 us -> 3.07 us  [body(): lax.ppermute(plane, 'grp', [(i, (i + k) % groups) for i in range(groups)])]
    pallas_call x0 -> x2, Pallas kernels: none -> 1.59 us  [the longest x1 0.91 us: make_field(): pl.pallas_call(field_kernel, out_shape=tuple((jax.ShapeDtypeStruct(shape,...]
  transfers between devices with their start and end apart: 9 -> 9, of which waited for: 6 -> 4; matrix products, arithmetic and copies ran while one was open for 1% -> 0% of each run, Pallas kernels for 5% -> 5%
where the time goes in v2:
time: 115 us; the launch traced here: 114 us
  waiting for transfers between devices  35.8 us (31%)
  Pallas kernels  27.1 us (24%)
  starting transfers between devices  24.1 us (21%)
  blocking collectives  21 us (18%)
  local copies, waits for them, and re-layouts  4.89 us (4%)
    all_to_all x1, blocking collectives, among_same_core(): lax.all_to_all(x, 'shard', split_axis=0, concat_axis=0, tiled=True, axis_...  21 us
    all_to_all x2, waiting for transfers between devices, among_all(): return lax.all_to_all(x, both, split_axis=0, concat_axis=0, tiled=True)  19.1 us
    pallas_call x1, Pallas kernels, render(): pl.pallas_call(render_kernel, out_shape=(jax.ShapeDtypeStruct((slots, 128...  17.8 us
    all_to_all x1, waiting for transfers between devices, among_same_core(): lax.all_to_all(x, 'shard', split_axis=0, concat_axis=0, tiled=True, axis_...  15.5 us
    all_to_all x2, starting transfers between devices, among_all(): return lax.all_to_all(x, both, split_axis=0, concat_axis=0, tiled=True)  13.3 us
    all_to_all x1, starting transfers between devices, among_same_core(): lax.all_to_all(x, 'shard', split_axis=0, concat_axis=0, tiled=True, axis_...  7.12 us
    ppermute x3, starting transfers between devices, body(): lax.ppermute(plane, 'grp', [(i, (i + k) % groups) for i in range(groups)])  3.07 us
    unnamed x17, local copies, waits for them, and re-layouts  2.89 us
  transfers between devices with their start and end apart: 9, of which 4 were waited for; matrix products, arithmetic and copies ran while one was open for 0% of the time, Pallas kernels for 5%

profile of v2, /device:TPU:0, one launch (start us, length us, event | category | flops | bytes accessed | tf_op | source)
XLA Modules:
  0.0 114.4 jit_solution(4767142365764315367)
XLA Ops:
  0.7 2.0 %broadcast_in_dim.4 = bf16[16,32,1024]{2,1,0:T(8,128)(2,1)} broadcast(bf16[32,1024]{1,0:T(8,128)(2,1)} %weight_ref.1), dimensions={1,2} | broadcast | bytes 1114112 | tf_op jit(solution)/shard_map/broadcast_in_dim | solution.py:438
  2.7 7.1 %all-to-all-start = ((bf16[16,32,1024]{2,1,0:T(8,128)(2,1)}), bf16[16,32,1024]{2,1,0:T(8,128)(2,1)S(1)}, u32[]{:S(2)}, u32[]{:S(2)}) async-start(bf16[16,32,1024]{2,1,0:T(8,128)(2,1)} %broadcast_in_dim.4), calls=%async_computation | async-start | bytes 2097152 | tf_op jit(solution)/shard_map/all_to_all | solution.py:433
  9.8 2.2 %pack.1 = (f32[128,1,640]{2,1,0:T(1,128)}, s32[64]{0:T(128)}) custom-call(s32[64]{0:T(128)} %scene_ref.1, f32[64,192]{1,0:T(8,128)} %points_ref.1, f32[64,64]{1,0:T(8,128)} %spacing_ref.1, f32[3,64]{1,0:T(4,128)} %target_ref.1), custom_call_target="tpu_custom_call" | custom-call | flops 200000 | bytes 1000000 | tf_op jit(solution)/shard_map/pack/pallas_call | solution.py:61
  12.0 15.5 %all-to-all-done = bf16[16,32,1024]{2,1,0:T(8,128)(2,1)S(1)} async-done(((bf16[16,32,1024]{2,1,0:T(8,128)(2,1)}), bf16[16,32,1024]{2,1,0:T(8,128)(2,1)S(1)}, u32[]{:S(2)}, u32[]{:S(2)}) %all-to-all-start) | async-done | bytes 1048608 | tf_op jit(solution)/shard_map/all_to_all | solution.py:433
  27.5 7.4 %all-to-all-start.1 = ((f32[128,1,640]{2,1,0:T(1,128)}), f32[128,1,640]{2,1,0:T(1,128)S(1)}, u32[]{:S(2)}, u32[]{:S(2)}) async-start(f32[128,1,640]{2,1,0:T(1,128)} %get-tuple-element.27), calls=%async_computation.1 | async-start | bytes 655360 | tf_op jit(solution)/shard_map/all_to_all | solution.py:436
  34.9 11.4 %all-to-all-done.1 = f32[128,1,640]{2,1,0:T(1,128)S(1)} async-done(((f32[128,1,640]{2,1,0:T(1,128)}), f32[128,1,640]{2,1,0:T(1,128)S(1)}, u32[]{:S(2)}, u32[]{:S(2)}) %all-to-all-start.1) | async-done | bytes 327712 | tf_op jit(solution)/shard_map/all_to_all | solution.py:436
  46.4 1.0 copy-done
  47.4 1.2 %copy-done.1 = bf16[512,1024]{1,0:T(8,128)(2,1)S(1)} copy-done((bf16[512,1024]{1,0:T(8,128)(2,1)S(1)}, bf16[512,1024]{1,0:T(8,128)(2,1)}, u32[]{:S(2)}) %copy-start.1) | copy-done | bytes 1048600
  48.6 0.9 field.1
  49.5 17.8 %render.1 = (f32[128,128]{1,0:T(8,128)S(1)}, bf16[128,1024]{1,0:T(8,128)(2,1)S(1)}) custom-call(f32[128,640]{1,0:T(8,128)S(1)} %bitcast.14, bf16[256,128]{1,0:T(8,128)(2,1)S(1)} %get-tuple-element.28.w0t_ref, bf16[256,256]{1,0:T(8,128)(2,1)S(1)} %get-tuple-element.29.w1_ref, bf16[256,256]{1,0:T(8,128)(2,1)S(1)} %get-tuple-element.30.w1t_ref, ...), custom_call_target="tpu_custom_call" | custom-call | flops 12000000000 | bytes 2000000 | tf_op jit(solution)/shard_map/render/pallas_call | solution.py:288
  67.4 0.5 collective-permute-start.1
  67.9 1.2 %collective-permute-done.1.other_ref = bf16[512,128]{1,0:T(8,128)(2,1)S(1)} collective-permute-done((bf16[512,128]{1,0:T(8,128)(2,1)S(1)}, bf16[512,128]{1,0:T(8,128)(2,1)S(1)}, u32[]{:S(2)}, u32[]{:S(2)}) %collective-permute-start.1) | collective-permute-done | bytes 131104 | tf_op jit(solution)/shard_map/ppermute | solution.py:445
  69.1 0.7 pair_terms.1
  69.8 21.0 %all_to_all.20.terms_ref = bf16[16,32,1024]{2,1,0:T(8,128)(2,1)} all-to-all(bf16[16,32,1024]{2,1,0:T(8,128)(2,1)S(1)} %bitcast.11), channel_id=1, replica_groups={{0,2,4,6,8,10,12,14,16,18,20,22,24,26,28,30},{1,3,5,7,9,11,13,15,17,19,..., dimensions={0} | all-to-all | bytes 2097152 | tf_op jit(solution)/shard_map/all_to_all | solution.py:433
  90.8 2.2 %plane_sum.1 = (bf16[32,1024]{1,0:T(8,128)(2,1)}, f32[128,128]{1,0:T(8,128)}) custom-call(bf16[16,32,1024]{2,1,0:T(8,128)(2,1)} %all_to_all.20.terms_ref, bf16[32,1024]{1,0:T(8,128)(2,1)} %weight_ref.1, f32[128,128]{1,0:T(8,128)} %copy-done.3), custom_call_target="tpu_custom_call" | custom-call | flops 1000000 | bytes 1300000 | tf_op jit(solution)/shard_map/plane_sum/pallas_call | solution.py:364
  93.0 0.9 collective-permute-start.5
  93.9 1.1 collective-permute-start.4
  95.0 1.0 collective-permute-start.3
  96.1 5.9 %all-to-all-start.3 = ((f32[128,1,128]{2,1,0:T(1,128)}), f32[128,1,128]{2,1,0:T(1,128)S(1)}, u32[]{:S(2)}, u32[]{:S(2)}) async-start(f32[128,1,128]{2,1,0:T(1,128)} %bitcast.18), calls=%async_computation.3 | async-start | bytes 131072 | tf_op jit(solution)/shard_map/all_to_all | solution.py:436
  102.0 1.6 %latent_gradient.1 = bf16[128,1024]{1,0:T(8,128)(2,1)} custom-call(bf16[128,1024]{1,0:T(8,128)(2,1)S(1)} %copy-done.2, bf16[1024,1024]{1,0:T(8,128)(2,1)S(1)} %get-tuple-element.38.weight_ref, f32[1,1024]{1,0:T(1,128)S(1)} %bitcast.17, bf16[128,1024]{1,0:T(8,128)(2,1)S(1)} %get-tuple-element.31.dfield_ref), custom_call_target="tpu_custom_call" | custom-call | flops 300000000 | bytes 3000000 | tf_op jit(solution)/shard_map/latent_gradient/pallas_call | solution.py:341
  103.6 7.7 %all-to-all-done.3.ret_ref = f32[128,1,128]{2,1,0:T(1,128)S(1)} async-done(((f32[128,1,128]{2,1,0:T(1,128)}), f32[128,1,128]{2,1,0:T(1,128)S(1)}, u32[]{:S(2)}, u32[]{:S(2)}) %all-to-all-start.3) | async-done | bytes 65568 | tf_op jit(solution)/shard_map/all_to_all | solution.py:436
  111.3 0.6 copy-done.6
  111.9 1.7 %unpack.1 = (f32[3,64]{1,0:T(4,128)}, f32[1,1]{1,0:T(1,128)}, f32[8,128]{1,0:T(8,128)}) custom-call(s32[64]{0:T(128)} %get-tuple-element.22.slot_ref, f32[128,1,128]{2,1,0:T(1,128)} %copy-done.6, f32[8,128]{1,0:T(8,128)} %bitcast.15), custom_call_target="tpu_custom_call" | custom-call | flops 100000 | bytes 100000 | tf_op jit(solution)/shard_map/unpack/pallas_call | solution.py:399
  113.7 0.7 add_add_fusion
  (21 shorter events, 0.2 us)
Async XLA Ops:
  0.6 46.7 %copy-start.4 = (f32[1024]{0:T(1024)S(1)}, f32[1024]{0:T(1024)}, u32[]{:S(2)}) copy-start(f32[1024]{0:T(1024)} %param.10) | copy-start | bytes 12292
  0.6 46.7 %copy-start.2 = (bf16[128,1024]{1,0:T(8,128)(2,1)S(1)}, bf16[128,1024]{1,0:T(8,128)(2,1)}, u32[]{:S(2)}) copy-start(bf16[128,1024]{1,0:T(8,128)(2,1)} %latent_ref.3) | copy-start | bytes 786436
  2.7 24.8 %all-to-all-start = ((bf16[16,32,1024]{2,1,0:T(8,128)(2,1)}), bf16[16,32,1024]{2,1,0:T(8,128)(2,1)S(1)}, u32[]{:S(2)}, u32[]{:S(2)}) async-start(bf16[16,32,1024]{2,1,0:T(8,128)(2,1)} %broadcast_in_dim.4), calls=%async_computation | async-start | bytes 2097152 | tf_op jit(solution)/shard_map/all_to_all | solution.py:433
  9.8 39.7 %copy-start.5 = (bf16[4,256]{1,0:T(4,128)(2,1)S(1)}, bf16[4,256]{1,0:T(4,128)(2,1)}, u32[]{:S(2)}) copy-start(bf16[4,256]{1,0:T(4,128)(2,1)} %head_ref.1) | copy-start | bytes 6148
  27.5 18.9 %collective-permute-start = (bf16[512,1024]{1,0:T(8,128)(2,1)S(1)}, bf16[512,1024]{1,0:T(8,128)(2,1)S(1)}, u32[]{:S(2)}, u32[]{:S(2)}) collective-permute-start(bf16[512,1024]{1,0:T(8,128)(2,1)S(1)} %bitcast.12), channel_id=1, source_target_pairs={{0,1},{1,0},{2,3},{3,2},{4,5},{5,4},{6,7},{7,6},{8,9},{9,8},{10,11... | collective-permute-start | bytes 3145736 | tf_op jit(solution)/shard_map/ppermute | solution.py:442
  27.5 18.8 %all-to-all-start.1 = ((f32[128,1,640]{2,1,0:T(1,128)}), f32[128,1,640]{2,1,0:T(1,128)S(1)}, u32[]{:S(2)}, u32[]{:S(2)}) async-start(f32[128,1,640]{2,1,0:T(1,128)} %get-tuple-element.27), calls=%async_computation.1 | async-start | bytes 655360 | tf_op jit(solution)/shard_map/all_to_all | solution.py:436
  46.4 1.0 copy-start
  47.3 1.2 %copy-start.1 = (bf16[512,1024]{1,0:T(8,128)(2,1)S(1)}, bf16[512,1024]{1,0:T(8,128)(2,1)}, u32[]{:S(2)}) copy-start(bf16[512,1024]{1,0:T(8,128)(2,1)} %copy-done) | copy-start | bytes 3145732
  67.3 23.5 %copy-start.3 = (f32[128,128]{1,0:T(8,128)}, f32[128,128]{1,0:T(8,128)S(1)}, u32[]{:S(2)}) copy-start(f32[128,128]{1,0:T(8,128)S(1)} %get-tuple-element.32.color_ref) | copy-start | bytes 196612
  67.3 1.8 %collective-permute-start.2 = (bf16[128,1024]{1,0:T(8,128)(2,1)S(1)}, bf16[128,1024]{1,0:T(8,128)(2,1)S(1)}, u32[]{:S(2)}, u32[]{:S(2)}) collective-permute-start(bf16[128,1024]{1,0:T(8,128)(2,1)S(1)} %get-tuple-element.31.dfield_ref), channel_id=1, source_target_pairs={{0,1},{1,0},{2,3},{3,2},{4,5},{5,4},{6,7},{7,6},{8,9},{9,8},{10,11... | collective-permute-start | bytes 786440 | tf_op jit(solution)/shard_map/ppermute | solution.py:447
  67.4 1.7 %collective-permute-start.1 = (bf16[512,128]{1,0:T(8,128)(2,1)S(1)}, bf16[512,128]{1,0:T(8,128)(2,1)S(1)}, u32[]{:S(2)}, u32[]{:S(2)}) collective-permute-start(bf16[512,128]{1,0:T(8,128)(2,1)S(1)} %get-tuple-element.26), channel_id=1, source_target_pairs={{0,1},{1,0},{2,3},{3,2},{4,5},{5,4},{6,7},{7,6},{8,9},{9,8},{10,11... | collective-permute-start | bytes 393224 | tf_op jit(solution)/shard_map/ppermute | solution.py:445
  93.0 20.7 %copy-start.7 = (bf16[32,1024]{1,0:T(8,128)(2,1)S(1)}, bf16[32,1024]{1,0:T(8,128)(2,1)}, u32[]{:S(2)}) copy-start(bf16[32,1024]{1,0:T(8,128)(2,1)} %get-tuple-element.36) | copy-start | bytes 196612
  93.0 20.7 %collective-permute-start.5 = (bf16[32,1024]{1,0:T(8,128)(2,1)}, bf16[32,1024]{1,0:T(8,128)(2,1)S(1)}, u32[]{:S(2)}, u32[]{:S(2)}) collective-permute-start(bf16[32,1024]{1,0:T(8,128)(2,1)} %get-tuple-element.36), channel_id=1, source_target_pairs={{0,96},{32,0},{64,32},{96,64},{1,97},{33,1},{65,33},{97,65},{2,98}... | collective-permute-start | bytes 196616 | tf_op jit(solution)/shard_map/ppermute | solution.py:453
  93.9 19.8 %collective-permute-start.4 = (bf16[32,1024]{1,0:T(8,128)(2,1)}, bf16[32,1024]{1,0:T(8,128)(2,1)S(1)}, u32[]{:S(2)}, u32[]{:S(2)}) collective-permute-start(bf16[32,1024]{1,0:T(8,128)(2,1)} %get-tuple-element.36), channel_id=1, source_target_pairs={{0,32},{32,64},{64,96},{96,0},{1,33},{33,65},{65,97},{97,1},{2,34}... | collective-permute-start | bytes 196616 | tf_op jit(solution)/shard_map/ppermute | solution.py:453
  95.0 18.6 %collective-permute-start.3 = (bf16[32,1024]{1,0:T(8,128)(2,1)}, bf16[32,1024]{1,0:T(8,128)(2,1)S(1)}, u32[]{:S(2)}, u32[]{:S(2)}) collective-permute-start(bf16[32,1024]{1,0:T(8,128)(2,1)} %get-tuple-element.36), channel_id=1, source_target_pairs={{0,64},{32,96},{64,0},{96,32},{1,65},{33,97},{65,1},{97,33},{2,66}... | collective-permute-start | bytes 196616 | tf_op jit(solution)/shard_map/ppermute | solution.py:453
  96.1 15.2 %all-to-all-start.3 = ((f32[128,1,128]{2,1,0:T(1,128)}), f32[128,1,128]{2,1,0:T(1,128)S(1)}, u32[]{:S(2)}, u32[]{:S(2)}) async-start(f32[128,1,128]{2,1,0:T(1,128)} %bitcast.18), calls=%async_computation.3 | async-start | bytes 131072 | tf_op jit(solution)/shard_map/all_to_all | solution.py:436
  111.3 0.6 copy-start.6

commit v3 on v2

--- a/solution.py
+++ b/solution.py
@@ -201,7 +201,7 @@
                 raw_ref[k, at, :] = raw[:, (2 * s + k) * slots : (2 * s + k + 1) * slots]
         return carry
 
-    lax.fori_loop(0, blocks, forward, 0)
+    lax.fori_loop(0, blocks, forward, 0, unroll=True)
 
     def spread(c):
         return jnp.concatenate([raw_ref[k, pl.ds(c, 64, stride=8), :] for k in range(2)], axis=1)
@@ -237,8 +237,7 @@
         grads.append(grad)
     loss = jnp.sum(square, axis=1, keepdims=True) * factor
     rows = [colors[c][:, k * slots : (k + 1) * slots] for k in range(2) for c in range(3)]
-    rows = [jnp.zeros((40, slots), f32), *rows, jnp.broadcast_to(loss, (1, slots))]
-    color_ref[...] = jnp.concatenate([*rows, jnp.zeros((slots - 47, slots), f32)], axis=0).T
+    color_ref[...] = jnp.concatenate([*rows, jnp.broadcast_to(loss, (2, slots))], axis=0)
     weighted = d_blend * blend
     behind = dot((column > row).astype(f32), weighted, precision=lax.Precision.HIGHEST)
     d_optical = d_blend * transmit * survive - behind
@@ -267,7 +266,7 @@
         g0_ref[...] += dot(h0_ref[b], d_a1, on_lanes)
         return carry
 
-    lax.fori_loop(0, blocks, backward, 0)
+    lax.fori_loop(0, blocks, backward, 0, unroll=True)
 
     unfold = jnp.concatenate([fold_matrix(), jnp.zeros((80, 256), f32)], axis=0).T[:, 0:features].astype(bf16)
     g0 = dot(unfold, g0_ref[...].astype(bf16)).astype(bf16)
@@ -288,7 +287,7 @@
     return pl.pallas_call(
         render_kernel,
         out_shape=(
-            jax.ShapeDtypeStruct((slots, 128), f32),
+            jax.ShapeDtypeStruct((8, slots), f32),
             jax.ShapeDtypeStruct((128, 1024), bf16),
         ),
         in_specs=[vmem] * 5,
@@ -310,105 +309,160 @@
     )(recv, w0t, w1, w1t, head)
 
 
-def pair_kernel(keep_ref, other_ref, dfield_ref, dother_ref, out_ref):
-    out_ref[...] = (dot(keep_ref[...], dfield_ref[...]) + dot(other_ref[...], dother_ref[...])).astype(bf16)
-
-
-def pair_terms(keep, other, d_field, d_other):
+def latent_kernel(latent_ref, weight_ref, gain_ref, dfield_ref, color_ref, out_ref, note_ref):
+    latent = latent_ref[...].astype(f32)
+    inv_rms = lax.rsqrt(jnp.mean(latent * latent, axis=1, keepdims=True) + norm_eps)
+    x_hat = latent * inv_rms
+    d_norm = dot(dfield_ref[...], weight_ref[...], (((1,), (1,)), ((), ())))
+    term = d_norm * x_hat
+    gain = jnp.sum(term, axis=0, keepdims=True)
+    mean = jnp.mean(term * gain_ref[...], axis=1, keepdims=True)
+    out_ref[...] = (inv_rms * (d_norm * gain_ref[...] - x_hat * mean)).astype(bf16)
+    note_ref[0:8, :] = color_ref[...]
+    for i in range(8):
+        note_ref[8 + i : 9 + i, :] = gain[:, i * 128 : (i + 1) * 128]
+
+
+def latent_gradient(latents, weight, gain, d_field, colors):
     vmem = pl.BlockSpec(memory_space=pltpu.VMEM)
     return pl.pallas_call(
+        latent_kernel,
+        out_shape=(
+            jax.ShapeDtypeStruct(latents.shape, bf16),
+            jax.ShapeDtypeStruct((16, 128), f32),
+        ),
+        in_specs=[vmem] * 5,
+        out_specs=(vmem,) * 2,
+        compiler_params=pltpu.CompilerParams(vmem_limit_bytes=24 * 1024 * 1024),
+        cost_estimate=pl.CostEstimate(flops=300_000_000, bytes_accessed=3_000_000, transcendentals=0),
+        name="latent_gradient",
+    )(latents, weight, gain, d_field, colors)
+
+
+def two_terms(value):
+    high = value.astype(bf16).astype(f32)
+    return high, value - high
+
+
+def pair_kernel(
+    core_ref, keep_ref, other_ref, dfield_ref, dother_ref, note_ref, nother_ref, out_ref, turned_ref
+):
+    first = core_ref[0] == 0
+    mine, mate = note_ref[...], nother_ref[...]
+    colors = jnp.concatenate(
+        [jnp.where(first, mine, mate)[0:8, :], jnp.where(first, mate, mine)[0:8, :], jnp.zeros((112, 128), f32)],
+        axis=0,
+    )
+    turned_ref[...] = colors.T
+    gain = two_terms(mine[8:16, :] + mate[8:16, :])
+    terms = (dot(keep_ref[...], dfield_ref[...]) + dot(other_ref[...], dother_ref[...])).astype(bf16)
+    for i in range(16):
+        out_ref[i, :, 0:1024] = terms[i * 32 : (i + 1) * 32, :]
+        rows = [turned_ref[pl.ds(2 * i + c, 4, stride=32), :] for c in range(2)]
+        tint = two_terms(jnp.where(first, *rows))
+        out_ref[i, :, 1024:1152] = jnp.concatenate(
+            [*tint, *gain, jnp.zeros((8, 128), f32)], axis=0
+        ).astype(bf16)
+
+
+def pair_terms(core, keep, other, d_field, d_other, note, note_other):
+    vmem = pl.BlockSpec(memory_space=pltpu.VMEM)
+    return pl.pallas_call(
         pair_kernel,
-        out_shape=jax.ShapeDtypeStruct((512, 1024), bf16),
-        in_specs=[vmem] * 4,
+        out_shape=jax.ShapeDtypeStruct((16, 32, 1152), bf16),
+        in_specs=[pl.BlockSpec(memory_space=pltpu.SMEM)] + [vmem] * 6,
         out_specs=vmem,
+        scratch_shapes=[pltpu.VMEM((128, 128), f32)],
         compiler_params=pltpu.CompilerParams(vmem_limit_bytes=16 * 1024 * 1024),
         cost_estimate=pl.CostEstimate(flops=270_000_000, bytes_accessed=2_000_000, transcendentals=0),
         name="pair_terms",
-    )(keep, other, d_field, d_other)
-
-
-def latent_kernel(latent_ref, weight_ref, gain_ref, dfield_ref, out_ref):
-    latent = latent_ref[...].astype(f32)
-    inv_rms = lax.rsqrt(jnp.mean(latent * latent, axis=1, keepdims=True) + norm_eps)
-    x_hat = latent * inv_rms
-    d_scaled = dot(dfield_ref[...], weight_ref[...], (((1,), (1,)), ((), ()))) * gain_ref[...]
-    mean = jnp.mean(d_scaled * x_hat, axis=1, keepdims=True)
-    out_ref[...] = (inv_rms * (d_scaled - x_hat * mean)).astype(bf16)
-
-
-def latent_gradient(latents, weight, gain, d_field):
+    )(core, keep, other, d_field, d_other, note, note_other)
+
+
+def plane_kernel(group_ref, terms_ref, *rest):
+    outs, tint_ref = rest[:4], rest[4]
+    total = terms_ref[0, :, 0:1024].astype(f32)
+    gain = jnp.zeros((8, 128), f32)
+    for i in range(terms_ref.shape[0]):
+        if i:
+            total = total + terms_ref[i, :, 0:1024].astype(f32)
+        extra = terms_ref[i, :, 1024:1152].astype(f32)
+        gain = gain + (extra[8:16, :] + extra[16:24, :])
+        tint = extra[0:4, :] + extra[4:8, :]
+        for z in range(4):
+            tint_ref[z, i : i + 1, :] = tint[z : z + 1, :]
+    total = total.astype(bf16)
+    gain_rows = jnp.concatenate([*two_terms(gain), jnp.zeros((16, 128), f32)], axis=0).astype(bf16)
+    for k, out in enumerate(outs):
+        out[:, 0:1024] = total
+        tint = tint_ref[jnp.bitwise_and(group_ref[0] + k, 3)]
+        out[:, 1024:1152] = jnp.concatenate(two_terms(tint), axis=0).astype(bf16)
+        out[:, 1152:1280] = gain_rows
+
+
+def plane_sum(group, terms):
     vmem = pl.BlockSpec(memory_space=pltpu.VMEM)
     return pl.pallas_call(
-        latent_kernel,
-        out_shape=jax.ShapeDtypeStruct(latents.shape, bf16),
-        in_specs=[vmem] * 4,
-        out_specs=vmem,
-        compiler_params=pltpu.CompilerParams(vmem_limit_bytes=24 * 1024 * 1024),
-        cost_estimate=pl.CostEstimate(flops=300_000_000, bytes_accessed=3_000_000, transcendentals=0),
-        name="latent_gradient",
-    )(latents, weight, gain, d_field)
-
-
-def plane_kernel(terms_ref, weight_ref, color_ref, sum_ref, line_ref):
-    total = terms_ref[0].astype(f32)
-    for i in range(1, terms_ref.shape[0]):
-        total = total + terms_ref[i].astype(f32)
-    sum_ref[...] = total.astype(bf16)
-    part = jnp.sum(total * weight_ref[...].astype(f32), axis=1, keepdims=True)
-    line = jnp.concatenate([jnp.broadcast_to(part, (32, 128)), jnp.zeros((96, 128), f32)], axis=0).T
-    line_ref[...] = line + color_ref[...]
-
-
-def plane_sum(terms, weight_rows, colors):
-    vmem = pl.BlockSpec(memory_space=pltpu.VMEM)
-    return pl.pallas_call(
         plane_kernel,
-        out_shape=(
-            jax.ShapeDtypeStruct(weight_rows.shape, bf16),
-            jax.ShapeDtypeStruct(colors.shape, f32),
-        ),
-        in_specs=[vmem] * 3,
-        out_specs=(vmem,) * 2,
-        cost_estimate=pl.CostEstimate(flops=1_000_000, bytes_accessed=1_300_000, transcendentals=0),
+        out_shape=(jax.ShapeDtypeStruct((32, 1280), bf16),) * 4,
+        in_specs=[pl.BlockSpec(memory_space=pltpu.SMEM), vmem],
+        out_specs=(vmem,) * 4,
+        scratch_shapes=[pltpu.VMEM((4, 16, 128), f32)],
+        cost_estimate=pl.CostEstimate(flops=1_000_000, bytes_accessed=1_500_000, transcendentals=0),
         name="plane_sum",
-    )(terms, weight_rows, colors)
-
-
-def unpack_kernel(slot_ref, ret_ref, gain_ref, color_ref, loss_ref, gain_out_ref, rows_ref):
+    )(group, terms)
+
+
+def finish_kernel(group_ref, slot_ref, m0, m1, m2, m3, color_ref, loss_ref, head_ref, gain_out_ref, tint_ref, rows_ref):
     rays = color_ref.shape[1]
+    planes = (m0, m1, m2, m3)
+
+    def summed(parts):
+        return (parts[0] + parts[2]) + (parts[1] + parts[3])
+
+    head_ref[...] = summed([m[:, 0:1024].astype(f32) for m in planes])
+    gains = [m[:, 1152:1280].astype(f32) for m in planes]
+    gain_out_ref[...] = summed([g[0:8, :] + g[8:16, :] for g in gains])
+    losses = []
+    for k, m in enumerate(planes):
+        tint = m[:, 1024:1152].astype(f32)
+        tint = tint[0:16, :] + tint[16:32, :]
+        losses.append(jnp.sum(tint, axis=0, keepdims=True))
+        for i in range(16):
+            tint_ref[k * 16 + i] = tint[i : i + 1, :]
     lane = lax.broadcasted_iota(jnp.int32, (1, 128), 1)
-    total = ret_ref[0:32, 0, :]
-    for z in range(1, 4):
-        total = total + ret_ref[z * 32 : (z + 1) * 32, 0, :]
-    rows_ref[0:32, :] = total
-    gains = [rows_ref[pl.ds(i, 8, stride=4), :][:, 0:32] for i in range(4)]
-    gain_out_ref[...] = jnp.concatenate(gains, axis=1) / gain_ref[...]
+    loss = jnp.where(jnp.logical_or(lane == 6, lane == 14), summed(losses), 0.0)
+    loss_ref[...] = jnp.sum(loss, axis=1, keepdims=True)
     for r in range(rays):
         slot = slot_ref[r]
-        first = 40 + 3 * jnp.bitwise_and(slot, 1)
+        scene = lax.shift_right_logical(slot, 1)
+        turn = jnp.bitwise_and(group_ref[0] - lax.shift_right_logical(scene, 5), 3)
+        row = turn * 16 + jnp.bitwise_and(lax.shift_right_logical(scene, 1), 15)
+        first = 8 * jnp.bitwise_and(scene, 1) + 3 * jnp.bitwise_and(slot, 1)
         kept = jnp.logical_and(lane >= first, lane < first + 3)
-        rows_ref[r : r + 1, :] = jnp.where(kept, ret_ref[lax.shift_right_logical(slot, 1)], 0.0)
+        rows_ref[r : r + 1, :] = jnp.where(kept, tint_ref[row], 0.0)
     turned = rows_ref[...].T
-    color_ref[...] = turned[40:43, :] + turned[43:46, :]
-    losses = jnp.where(lane == 46, jnp.sum(ret_ref[...], axis=0), 0.0)
-    loss_ref[...] = jnp.sum(losses, axis=1, keepdims=True)
-
-
-def unpack(slot, returned, gain):
+    color_ref[...] = (turned[0:3, :] + turned[3:6, :]) + (turned[8:11, :] + turned[11:14, :])
+
+
+def finish(group, slot, planes):
     vmem = pl.BlockSpec(memory_space=pltpu.VMEM)
-    return pl.pallas_call(
-        unpack_kernel,
+    smem = pl.BlockSpec(memory_space=pltpu.SMEM)
+    rays = slot.shape[0]
+    return pl.pallas_call(
+        finish_kernel,
         out_shape=(
-            jax.ShapeDtypeStruct((3, slot.shape[0]), f32),
+            jax.ShapeDtypeStruct((3, rays), f32),
             jax.ShapeDtypeStruct((1, 1), f32),
-            jax.ShapeDtypeStruct(gain.shape, f32),
+            jax.ShapeDtypeStruct((32, 1024), f32),
+            jax.ShapeDtypeStruct((8, 128), f32),
         ),
-        in_specs=[pl.BlockSpec(memory_space=pltpu.SMEM), vmem, vmem],
-        out_specs=(vmem,) * 3,
-        scratch_shapes=[pltpu.VMEM((slot.shape[0], 128), f32)],
-        cost_estimate=pl.CostEstimate(flops=100_000, bytes_accessed=100_000, transcendentals=0),
-        name="unpack",
-    )(slot, returned, gain)
+        in_specs=[smem, smem] + [vmem] * 4,
+        out_specs=(vmem,) * 4,
+        scratch_shapes=[pltpu.VMEM((64, 1, 128), f32), pltpu.VMEM((rays, 128), f32)],
+        cost_estimate=pl.CostEstimate(flops=300_000, bytes_accessed=500_000, transcendentals=0),
+        name="finish",
+    )(group, slot, *planes)
 
 
 def body(
@@ -424,38 +478,33 @@
     slots = lax.axis_size(both)
     shards = lax.axis_size("shard")
     groups = lax.axis_size("grp")
-    core = (lax.axis_index("shard") % 2).reshape(1).astype(jnp.int32)
+    core = jnp.bitwise_and(lax.axis_index("shard"), 1).reshape(1).astype(jnp.int32)
+    group = lax.axis_index("grp").reshape(1).astype(jnp.int32)
     gain_line = norm_gain[None, :]
     same_core = [[i for i in range(shards) if i % 2 == c] for c in range(2)]
     across = [(i, i ^ 1) for i in range(shards)]
 
     def among_same_core(x):
         return lax.all_to_all(x, "shard", split_axis=0, concat_axis=0, tiled=True, axis_index_groups=same_core)
-
-    def among_all(x):
-        return lax.all_to_all(x, both, split_axis=0, concat_axis=0, tiled=True)
 
     own_rows = among_same_core(jnp.broadcast_to(head_weight[None], (shards // 2, *head_weight.shape)))
     own_rows = own_rows.reshape(512, 1024)
     sent, slot = pack(ray_scene, sample_points, sample_spacing, ray_targets, slots)
     sent, own_rows = lax.optimization_barrier((sent, own_rows))
     other_rows = lax.ppermute(own_rows, "shard", across)
-    recv = among_all(sent).reshape(slots, 640)
+    recv = lax.all_to_all(sent, both, split_axis=0, concat_axis=0, tiled=True).reshape(slots, 640)
     weight, w0t, w1, w1t, keep, send = make_field(core, latents, own_rows, other_rows, gain_line)
     x_other = lax.ppermute(send, "shard", across)
     colors, d_field = render(recv, w0t, w1, w1t, color_head)
     d_other = lax.ppermute(d_field, "shard", across)
-    paired = pair_terms(keep, x_other, d_field, d_other)
-    terms = among_same_core(paired.reshape(shards // 2, shards, 1024))
-    latent_grad = latent_gradient(latents, weight, gain_line, d_field)
-    plane, lines = plane_sum(terms, head_weight, colors)
-    turns = [
-        lax.ppermute(plane, "grp", [(i, (i + k) % groups) for i in range(groups)]).astype(f32)
-        for k in range(1, groups)
+    latent_grad, note = latent_gradient(latents, weight, gain_line, d_field, colors)
+    note_other = lax.ppermute(note, "shard", across)
+    paired = pair_terms(core, keep, x_other, d_field, d_other, note, note_other)
+    planes = plane_sum(group, among_same_core(paired))
+    planes = [planes[0]] + [
+        lax.ppermute(planes[k], "grp", [(i, (i + k) % groups) for i in range(groups)]) for k in range(1, groups)
     ]
-    head_grad = (plane.astype(f32) + turns[1]) + (turns[0] + turns[2])
-    returned = among_all(lines.reshape(slots, 1, 128))
-    rendered, loss, gain_grad = unpack(slot, returned, norm_gain.reshape(8, 128))
+    rendered, loss, head_grad, gain_grad = finish(group, slot, planes)
     return (rendered, loss.reshape(()), head_grad, gain_grad.reshape(-1), latent_grad)
 
 

time: 115 us -> 105 us (0.913)
  blocking collectives: 21 us -> 0 us
  waiting for transfers between devices: 35.8 us -> 51.7 us
  starting transfers between devices: 24.1 us -> 22.6 us
  local copies, waits for them, and re-layouts: 4.89 us -> 3.69 us
    all_to_all x1 -> x0, blocking collectives: 21 us -> none  [among_same_core(): lax.all_to_all(x, 'shard', split_axis=0, concat_axis=0, tiled=True, axis_...]
    all_to_all x1 -> x2, waiting for transfers between devices: 15.5 us -> 35.3 us  [among_same_core(): lax.all_to_all(x, 'shard', split_axis=0, concat_axis=0, tiled=True, axis_...]
    all_to_all x2 -> x1, waiting for transfers between devices: 19.1 us -> 11.4 us  [body(): lax.all_to_all(sent, both, split_axis=0, concat_axis=0, tiled=True)]
    all_to_all x2 -> x1, starting transfers between devices: 13.3 us -> 7.41 us  [body(): lax.all_to_all(sent, both, split_axis=0, concat_axis=0, tiled=True)]
    ppermute x3 -> x4, waiting for transfers between devices: 0.01 us -> 4.94 us  [the longest x3 3.86 us: body(): lax.ppermute(planes[k], 'grp', [(i, (i + k) % groups) for i in range(grou...]
    all_to_all x1 -> x2, starting transfers between devices: 7.12 us -> 10.8 us  [among_same_core(): lax.all_to_all(x, 'shard', split_axis=0, concat_axis=0, tiled=True, axis_...]
    ppermute x1, waiting for transfers between devices: 1.21 us -> 0.01 us  [body(): x_other = lax.ppermute(send, 'shard', across)]
    pallas_call x5, Pallas kernels: 24 us -> 22.8 us  [the longest x1 15.3 us: render(): pl.pallas_call(render_kernel, out_shape=(jax.ShapeDtypeStruct((8, slots),...]
  transfers between devices with their start and end apart: 9 -> 10, of which waited for: 4 -> 7; matrix products, arithmetic and copies ran while one was open for 0% -> 0% of each run, Pallas kernels for 5% -> 4%
where the time goes in v3:
time: 105 us
  waiting for transfers between devices  51.7 us (49%)
  Pallas kernels  26 us (25%)
  starting transfers between devices  22.6 us (22%)
  local copies, waits for them, and re-layouts  3.69 us (4%)
    all_to_all x2, waiting for transfers between devices, among_same_core(): lax.all_to_all(x, 'shard', split_axis=0, concat_axis=0, tiled=True, axis_...  35.3 us
    pallas_call x1, Pallas kernels, render(): pl.pallas_call(render_kernel, out_shape=(jax.ShapeDtypeStruct((8, slots),...  15.3 us
    all_to_all x1, waiting for transfers between devices, body(): lax.all_to_all(sent, both, split_axis=0, concat_axis=0, tiled=True)  11.4 us
    all_to_all x2, starting transfers between devices, among_same_core(): lax.all_to_all(x, 'shard', split_axis=0, concat_axis=0, tiled=True, axis_...  10.8 us
    all_to_all x1, starting transfers between devices, body(): lax.all_to_all(sent, both, split_axis=0, concat_axis=0, tiled=True)  7.41 us
    ppermute x3, waiting for transfers between devices, body(): lax.ppermute(planes[k], 'grp', [(i, (i + k) % groups) for i in range(grou...  3.86 us
    ppermute x3, starting transfers between devices, body(): lax.ppermute(planes[k], 'grp', [(i, (i + k) % groups) for i in range(grou...  3.73 us
    pallas_call x1, Pallas kernels, pack(): pl.pallas_call(pack_kernel, out_shape=(jax.ShapeDtypeStruct((slots, 1, 64...  2.25 us
  transfers between devices with their start and end apart: 10, of which 7 were waited for; matrix products, arithmetic and copies ran while one was open for 0% of the time, Pallas kernels for 4%

profile of v3, /device:TPU:0, one launch (start us, length us, event | category | flops | bytes accessed | tf_op | source)
XLA Modules:
  0.0 104.7 jit_solution(12801997308143913768)
XLA Ops:
  0.6 2.0 %broadcast_in_dim.4 = bf16[16,32,1024]{2,1,0:T(8,128)(2,1)} broadcast(bf16[32,1024]{1,0:T(8,128)(2,1)} %param.9), dimensions={1,2} | broadcast | bytes 1114112 | tf_op jit(solution)/shard_map/broadcast_in_dim | solution.py:490
  2.6 7.1 %all-to-all-start = ((bf16[16,32,1024]{2,1,0:T(8,128)(2,1)}), bf16[16,32,1024]{2,1,0:T(8,128)(2,1)S(1)}, u32[]{:S(2)}, u32[]{:S(2)}) async-start(bf16[16,32,1024]{2,1,0:T(8,128)(2,1)} %broadcast_in_dim.4), calls=%async_computation | async-start | bytes 2097152 | tf_op jit(solution)/shard_map/all_to_all | solution.py:488
  9.8 2.3 %pack.1 = (f32[128,1,640]{2,1,0:T(1,128)}, s32[64]{0:T(128)}) custom-call(s32[64]{0:T(128)} %scene_ref.1, f32[64,192]{1,0:T(8,128)} %points_ref.1, f32[64,64]{1,0:T(8,128)} %spacing_ref.1, f32[3,64]{1,0:T(4,128)} %target_ref.1), custom_call_target="tpu_custom_call" | custom-call | flops 200000 | bytes 1000000 | tf_op jit(solution)/shard_map/pack/pallas_call | solution.py:61
  12.0 15.4 %all-to-all-done = bf16[16,32,1024]{2,1,0:T(8,128)(2,1)S(1)} async-done(((bf16[16,32,1024]{2,1,0:T(8,128)(2,1)}), bf16[16,32,1024]{2,1,0:T(8,128)(2,1)S(1)}, u32[]{:S(2)}, u32[]{:S(2)}) %all-to-all-start) | async-done | bytes 1048608 | tf_op jit(solution)/shard_map/all_to_all | solution.py:488
  27.4 7.4 %all-to-all-start.1 = ((f32[128,1,640]{2,1,0:T(1,128)}), f32[128,1,640]{2,1,0:T(1,128)S(1)}, u32[]{:S(2)}, u32[]{:S(2)}) async-start(f32[128,1,640]{2,1,0:T(1,128)} %get-tuple-element.32), calls=%async_computation.1 | async-start | bytes 655360 | tf_op jit(solution)/shard_map/all_to_all | solution.py:495
  34.8 11.4 %all-to-all-done.1 = f32[128,1,640]{2,1,0:T(1,128)S(1)} async-done(((f32[128,1,640]{2,1,0:T(1,128)}), f32[128,1,640]{2,1,0:T(1,128)S(1)}, u32[]{:S(2)}, u32[]{:S(2)}) %all-to-all-start.1) | async-done | bytes 327712 | tf_op jit(solution)/shard_map/all_to_all | solution.py:495
  46.3 0.9 field.1
  47.3 15.3 %render.1 = (f32[8,128]{1,0:T(8,128)S(1)}, bf16[128,1024]{1,0:T(8,128)(2,1)S(1)}) custom-call(f32[128,640]{1,0:T(8,128)S(1)} %bitcast.11, bf16[256,128]{1,0:T(8,128)(2,1)S(1)} %get-tuple-element.33.w0t_ref, bf16[256,256]{1,0:T(8,128)(2,1)S(1)} %get-tuple-element.34.w1_ref, bf16[256,256]{1,0:T(8,128)(2,1)S(1)} %get-tuple-element.35.w1t_ref, ...), custom_call_target="tpu_custom_call" | custom-call | flops 12000000000 | bytes 2000000 | tf_op jit(solution)/shard_map/render/pallas_call | solution.py:287
  62.6 0.5 collective-permute-start.1
  63.1 1.7 %latent_gradient.1 = (bf16[128,1024]{1,0:T(8,128)(2,1)}, f32[16,128]{1,0:T(8,128)S(1)}) custom-call(bf16[128,1024]{1,0:T(8,128)(2,1)S(1)} %copy-done, bf16[1024,1024]{1,0:T(8,128)(2,1)S(1)} %get-tuple-element.37.weight_ref, f32[1,1024]{1,0:T(1,128)S(1)} %bitcast.13, bf16[128,1024]{1,0:T(8,128)(2,1)S(1)} %get-tuple-element.36.dfield_ref, ...), custom_call_target="tpu_custom_call" | custom-call | flops 300000000 | bytes 3000000 | tf_op jit(solution)/shard_map/latent_gradient/pallas_call | solution.py:328
  64.9 1.1 %collective-permute-done.3.nother_ref = f32[16,128]{1,0:T(8,128)S(1)} collective-permute-done((f32[16,128]{1,0:T(8,128)S(1)}, f32[16,128]{1,0:T(8,128)S(1)}, u32[]{:S(2)}, u32[]{:S(2)}) %collective-permute-start.3) | collective-permute-done | bytes 8224 | tf_op jit(solution)/shard_map/ppermute | solution.py:501
  66.0 1.7 %pair_terms.1 = bf16[16,32,1152]{2,1,0:T(8,128)(2,1)} custom-call(s32[1]{0:T(128)} %bitcast.1.core_ref, bf16[512,128]{1,0:T(8,128)(2,1)S(1)} %get-tuple-element.30.keep_ref, bf16[512,128]{1,0:T(8,128)(2,1)S(1)} %collective-permute-done.1.other_ref, bf16[128,1024]{1,0:T(8,128)(2,1)S(1)} %get-tuple-element.36.dfield_ref, ...), custom_call_target="tpu_custom_call" | custom-call | flops 270000000 | bytes 2000000 | tf_op jit(solution)/shard_map/pair_terms/pallas_call | solution.py:370
  67.7 3.7 %all-to-all-start.2 = ((bf16[16,32,1152]{2,1,0:T(8,128)(2,1)}), bf16[16,32,1152]{2,1,0:T(8,128)(2,1)S(1)}, u32[]{:S(2)}, u32[]{:S(2)}) async-start(bf16[16,32,1152]{2,1,0:T(8,128)(2,1)} %pair_terms.1), calls=%async_computation.2 | async-start | bytes 2359296 | tf_op jit(solution)/shard_map/all_to_all | solution.py:488
  71.4 19.9 %all-to-all-done.2.terms_ref = bf16[16,32,1152]{2,1,0:T(8,128)(2,1)S(1)} async-done(((bf16[16,32,1152]{2,1,0:T(8,128)(2,1)}), bf16[16,32,1152]{2,1,0:T(8,128)(2,1)S(1)}, u32[]{:S(2)}, u32[]{:S(2)}) %all-to-all-start.2) | async-done | bytes 1179680 | tf_op jit(solution)/shard_map/all_to_all | solution.py:488
  91.3 1.0 copy-done.3
  92.4 2.2 %plane_sum.1 = (bf16[32,1280]{1,0:T(8,128)(2,1)}, bf16[32,1280]{1,0:T(8,128)(2,1)}, bf16[32,1280]{1,0:T(8,128)(2,1)}, bf16[32,1280]{1,0:T(8,128)(2,1)}) custom-call(s32[1]{0:T(128)} %bitcast.group_ref, bf16[16,32,1152]{2,1,0:T(8,128)(2,1)} %copy-done.3), custom_call_target="tpu_custom_call" | custom-call | flops 1000000 | bytes 1500000 | tf_op jit(solution)/shard_map/plane_sum/pallas_call | solution.py:405
  94.5 0.9 collective-permute-start.4
  95.4 1.5 %collective-permute-start.5 = (bf16[32,1280]{1,0:T(8,128)(2,1)}, bf16[32,1280]{1,0:T(8,128)(2,1)S(1)}, u32[]{:S(2)}, u32[]{:S(2)}) collective-permute-start(bf16[32,1280]{1,0:T(8,128)(2,1)} %get-tuple-element.42), channel_id=1, source_target_pairs={{0,64},{32,96},{64,0},{96,32},{1,65},{33,97},{65,1},{97,33},{2,66}... | collective-permute-start | bytes 245768 | tf_op jit(solution)/shard_map/ppermute | solution.py:505
  96.9 1.3 %collective-permute-start.6 = (bf16[32,1280]{1,0:T(8,128)(2,1)}, bf16[32,1280]{1,0:T(8,128)(2,1)S(1)}, u32[]{:S(2)}, u32[]{:S(2)}) collective-permute-start(bf16[32,1280]{1,0:T(8,128)(2,1)} %get-tuple-element.43), channel_id=1, source_target_pairs={{0,96},{32,0},{64,32},{96,64},{1,97},{33,1},{65,33},{97,65},{2,98}... | collective-permute-start | bytes 245768 | tf_op jit(solution)/shard_map/ppermute | solution.py:505
  98.3 2.2 %collective-permute-done.4.m1 = bf16[32,1280]{1,0:T(8,128)(2,1)S(1)} collective-permute-done((bf16[32,1280]{1,0:T(8,128)(2,1)}, bf16[32,1280]{1,0:T(8,128)(2,1)S(1)}, u32[]{:S(2)}, u32[]{:S(2)}) %collective-permute-start.4) | collective-permute-done | bytes 81952 | tf_op jit(solution)/shard_map/ppermute | solution.py:505
  100.4 1.1 %collective-permute-done.5.m2 = bf16[32,1280]{1,0:T(8,128)(2,1)S(1)} collective-permute-done((bf16[32,1280]{1,0:T(8,128)(2,1)}, bf16[32,1280]{1,0:T(8,128)(2,1)S(1)}, u32[]{:S(2)}, u32[]{:S(2)}) %collective-permute-start.5) | collective-permute-done | bytes 81952 | tf_op jit(solution)/shard_map/ppermute | solution.py:505
  101.6 0.6 collective-permute-done.6.m3
  102.2 0.6 copy-done.6
  102.8 2.0 %finish.1 = (f32[3,64]{1,0:T(4,128)}, f32[1,1]{1,0:T(1,128)}, f32[32,1024]{1,0:T(8,128)}, f32[8,128]{1,0:T(8,128)}) custom-call(s32[1]{0:T(128)} %bitcast.group_ref, s32[64]{0:T(128)} %get-tuple-element.27.slot_ref, bf16[32,1280]{1,0:T(8,128)(2,1)} %get-tuple-element.40.m0, bf16[32,1280]{1,0:T(8,128)(2,1)} %copy-done.4, bf16[32,1280]{1,0:T(8,128)(2,1)} %copy-done.5, ...), custom_call_target="tpu_custom_call" | custom-call | flops 300000 | bytes 500000 | tf_op jit(solution)/shard_map/finish/pallas_call | solution.py:452
  (19 shorter events, 0.3 us)
Async XLA Ops:
  2.6 24.8 %all-to-all-start = ((bf16[16,32,1024]{2,1,0:T(8,128)(2,1)}), bf16[16,32,1024]{2,1,0:T(8,128)(2,1)S(1)}, u32[]{:S(2)}, u32[]{:S(2)}) async-start(bf16[16,32,1024]{2,1,0:T(8,128)(2,1)} %broadcast_in_dim.4), calls=%async_computation | async-start | bytes 2097152 | tf_op jit(solution)/shard_map/all_to_all | solution.py:488
  9.7 36.6 %copy-start = (bf16[128,1024]{1,0:T(8,128)(2,1)S(1)}, bf16[128,1024]{1,0:T(8,128)(2,1)}, u32[]{:S(2)}) copy-start(bf16[128,1024]{1,0:T(8,128)(2,1)} %latent_ref.3) | copy-start | bytes 786436
  9.7 36.6 %copy-start.1 = (f32[1024]{0:T(1024)S(1)}, f32[1024]{0:T(1024)}, u32[]{:S(2)}) copy-start(f32[1024]{0:T(1024)} %param.10) | copy-start | bytes 12292
  27.4 18.9 %collective-permute-start = (bf16[512,1024]{1,0:T(8,128)(2,1)S(1)}, bf16[512,1024]{1,0:T(8,128)(2,1)S(1)}, u32[]{:S(2)}, u32[]{:S(2)}) collective-permute-start(bf16[512,1024]{1,0:T(8,128)(2,1)S(1)} %bitcast.9), channel_id=1, source_target_pairs={{0,1},{1,0},{2,3},{3,2},{4,5},{5,4},{6,7},{7,6},{8,9},{9,8},{10,11... | collective-permute-start | bytes 3145736 | tf_op jit(solution)/shard_map/ppermute | solution.py:494
  27.4 18.8 %all-to-all-start.1 = ((f32[128,1,640]{2,1,0:T(1,128)}), f32[128,1,640]{2,1,0:T(1,128)S(1)}, u32[]{:S(2)}, u32[]{:S(2)}) async-start(f32[128,1,640]{2,1,0:T(1,128)} %get-tuple-element.32), calls=%async_computation.1 | async-start | bytes 655360 | tf_op jit(solution)/shard_map/all_to_all | solution.py:495
  46.3 0.9 copy-start.2
  62.6 3.4 %collective-permute-start.2 = (bf16[128,1024]{1,0:T(8,128)(2,1)S(1)}, bf16[128,1024]{1,0:T(8,128)(2,1)S(1)}, u32[]{:S(2)}, u32[]{:S(2)}) collective-permute-start(bf16[128,1024]{1,0:T(8,128)(2,1)S(1)} %get-tuple-element.36.dfield_ref), channel_id=1, source_target_pairs={{0,1},{1,0},{2,3},{3,2},{4,5},{5,4},{6,7},{7,6},{8,9},{9,8},{10,11... | collective-permute-start | bytes 786440 | tf_op jit(solution)/shard_map/ppermute | solution.py:499
  62.6 3.3 %collective-permute-start.1 = (bf16[512,128]{1,0:T(8,128)(2,1)S(1)}, bf16[512,128]{1,0:T(8,128)(2,1)S(1)}, u32[]{:S(2)}, u32[]{:S(2)}) collective-permute-start(bf16[512,128]{1,0:T(8,128)(2,1)S(1)} %get-tuple-element.31), channel_id=1, source_target_pairs={{0,1},{1,0},{2,3},{3,2},{4,5},{5,4},{6,7},{7,6},{8,9},{9,8},{10,11... | collective-permute-start | bytes 393224 | tf_op jit(solution)/shard_map/ppermute | solution.py:497
  64.8 1.2 %collective-permute-start.3 = (f32[16,128]{1,0:T(8,128)S(1)}, f32[16,128]{1,0:T(8,128)S(1)}, u32[]{:S(2)}, u32[]{:S(2)}) collective-permute-start(f32[16,128]{1,0:T(8,128)S(1)} %get-tuple-element.39.note_ref), channel_id=1, source_target_pairs={{0,1},{1,0},{2,3},{3,2},{4,5},{5,4},{6,7},{7,6},{8,9},{9,8},{10,11... | collective-permute-start | bytes 24584 | tf_op jit(solution)/shard_map/ppermute | solution.py:501
  67.7 23.6 %all-to-all-start.2 = ((bf16[16,32,1152]{2,1,0:T(8,128)(2,1)}), bf16[16,32,1152]{2,1,0:T(8,128)(2,1)S(1)}, u32[]{:S(2)}, u32[]{:S(2)}) async-start(bf16[16,32,1152]{2,1,0:T(8,128)(2,1)} %pair_terms.1), calls=%async_computation.2 | async-start | bytes 2359296 | tf_op jit(solution)/shard_map/all_to_all | solution.py:488
  91.3 1.0 copy-start.3
  94.5 5.9 %collective-permute-start.4 = (bf16[32,1280]{1,0:T(8,128)(2,1)}, bf16[32,1280]{1,0:T(8,128)(2,1)S(1)}, u32[]{:S(2)}, u32[]{:S(2)}) collective-permute-start(bf16[32,1280]{1,0:T(8,128)(2,1)} %get-tuple-element.41), channel_id=1, source_target_pairs={{0,32},{32,64},{64,96},{96,0},{1,33},{33,65},{65,97},{97,1},{2,34}... | collective-permute-start | bytes 245768 | tf_op jit(solution)/shard_map/ppermute | solution.py:505
  95.4 6.2 %collective-permute-start.5 = (bf16[32,1280]{1,0:T(8,128)(2,1)}, bf16[32,1280]{1,0:T(8,128)(2,1)S(1)}, u32[]{:S(2)}, u32[]{:S(2)}) collective-permute-start(bf16[32,1280]{1,0:T(8,128)(2,1)} %get-tuple-element.42), channel_id=1, source_target_pairs={{0,64},{32,96},{64,0},{96,32},{1,65},{33,97},{65,1},{97,33},{2,66}... | collective-permute-start | bytes 245768 | tf_op jit(solution)/shard_map/ppermute | solution.py:505
  96.9 5.2 %collective-permute-start.6 = (bf16[32,1280]{1,0:T(8,128)(2,1)}, bf16[32,1280]{1,0:T(8,128)(2,1)S(1)}, u32[]{:S(2)}, u32[]{:S(2)}) collective-permute-start(bf16[32,1280]{1,0:T(8,128)(2,1)} %get-tuple-element.43), channel_id=1, source_target_pairs={{0,96},{32,0},{64,32},{96,64},{1,97},{33,1},{65,33},{97,65},{2,98}... | collective-permute-start | bytes 245768 | tf_op jit(solution)/shard_map/ppermute | solution.py:505
  100.4 1.7 %copy-start.4 = (bf16[32,1280]{1,0:T(8,128)(2,1)}, bf16[32,1280]{1,0:T(8,128)(2,1)S(1)}, u32[]{:S(2)}) copy-start(bf16[32,1280]{1,0:T(8,128)(2,1)S(1)} %collective-permute-done.4.m1) | copy-start | bytes 245764
  101.6 0.6 copy-start.5
  102.1 0.6 copy-start.6

commit v4 on v3

--- a/solution.py
+++ b/solution.py
@@ -32,11 +32,13 @@
     return lax.dot_general(a, b, dims, preferred_element_type=f32, precision=precision)
 
 
-def pack_kernel(scene_ref, points_ref, spacing_ref, target_ref, out_ref, slot_ref, count_ref, pay_ref, tint_ref):
+def pack_kernel(place_ref, scene_ref, points_ref, spacing_ref, target_ref, *rest):
+    outs, (slot_ref, count_ref, row_ref, pay_ref, tint_ref) = rest[:8], rest[8:]
     rays = points_ref.shape[0]
+    group, core = place_ref[0], place_ref[1]
     for d in range(count_ref.shape[0]):
         count_ref[d] = 0
-    out_ref[...] = jnp.zeros_like(out_ref)
+    row_ref[...] = jnp.zeros_like(row_ref)
     pay_ref[:, 0:192] = points_ref[...]
     pay_ref[:, 192:256] = spacing_ref[...]
     target = jnp.concatenate([target_ref[...], jnp.zeros((5, rays), f32)], axis=0).T
@@ -52,28 +54,75 @@
         rank = count_ref[scene]
         count_ref[scene] = rank + 1
         slot_ref[r] = scene * 2 + rank
-        out_ref[scene, :, pl.ds(pl.multiple_of(rank * 256, 256), 256)] = pay_ref[r : r + 1, :]
-        out_ref[scene, :, 512:640] += tint_ref[rank, r : r + 1, :]
-
-
-def pack(ray_scene, points, spacing, targets, slots):
+        turn = jnp.bitwise_and(lax.shift_right_logical(scene, 5) - group, 3)
+        side = jnp.bitwise_and(scene + core, 1)
+        row = (turn * 2 + side) * 16 + jnp.bitwise_and(lax.shift_right_logical(scene, 1), 15)
+        row_ref[row, :, pl.ds(pl.multiple_of(rank * 256, 256), 256)] = pay_ref[r : r + 1, :]
+        row_ref[row, :, 512:640] += tint_ref[rank, r : r + 1, :]
+    for n, out in enumerate(outs):
+        out[...] = row_ref[n * 16 : (n + 1) * 16]
+
+
+def pack(place, ray_scene, points, spacing, targets, slots):
     rays = points.shape[0]
+    smem = pl.BlockSpec(memory_space=pltpu.SMEM)
+    vmem = pl.BlockSpec(memory_space=pltpu.VMEM)
     return pl.pallas_call(
         pack_kernel,
         out_shape=(
-            jax.ShapeDtypeStruct((slots, 1, 640), f32),
+            *(jax.ShapeDtypeStruct((slots // 8, 1, 640), f32),) * 8,
             jax.ShapeDtypeStruct((rays,), jnp.int32),
         ),
-        in_specs=[pl.BlockSpec(memory_space=pltpu.SMEM)] + [pl.BlockSpec(memory_space=pltpu.VMEM)] * 3,
-        out_specs=(pl.BlockSpec(memory_space=pltpu.VMEM), pl.BlockSpec(memory_space=pltpu.SMEM)),
+        in_specs=[smem, smem] + [vmem] * 3,
+        out_specs=(*(vmem,) * 8, smem),
         scratch_shapes=[
             pltpu.SMEM((slots,), jnp.int32),
+            pltpu.VMEM((slots, 1, 640), f32),
             pltpu.VMEM((rays, 256), f32),
             pltpu.VMEM((2, rays, 128), f32),
         ],
         cost_estimate=pl.CostEstimate(flops=200000, bytes_accessed=1000000, transcendentals=0),
         name="pack",
-    )(ray_scene, points, spacing, targets)
+    )(place, ray_scene, points, spacing, targets)
+
+
+def stack_kernel(place_ref, *rest):
+    parts, out_ref = rest[:8], rest[8]
+    group, core = place_ref[0], place_ref[1]
+    for n, part in enumerate(parts):
+        source = jnp.bitwise_and(group - n // 2, 3) * 2 + jnp.bitwise_and(core + n, 1)
+        for i in range(16):
+            out_ref[i, source] = part[i]
+
+
+def stack(place, parts):
+    vmem = pl.BlockSpec(memory_space=pltpu.VMEM)
+    return pl.pallas_call(
+        stack_kernel,
+        out_shape=jax.ShapeDtypeStruct((16, 8, 1, 640), f32),
+        in_specs=[pl.BlockSpec(memory_space=pltpu.SMEM)] + [vmem] * 8,
+        out_specs=vmem,
+        cost_estimate=pl.CostEstimate(flops=100_000, bytes_accessed=800_000, transcendentals=0),
+        name="stack",
+    )(place, *parts)
+
+
+def copies_kernel(rows_ref, out_ref):
+    rows = rows_ref[...]
+    for i in range(out_ref.shape[0]):
+        out_ref[i] = rows
+
+
+def copies(rows, count):
+    vmem = pl.BlockSpec(memory_space=pltpu.VMEM)
+    return pl.pallas_call(
+        copies_kernel,
+        out_shape=jax.ShapeDtypeStruct((count, *rows.shape), rows.dtype),
+        in_specs=[vmem],
+        out_specs=vmem,
+        cost_estimate=pl.CostEstimate(flops=0, bytes_accessed=1_000_000, transcendentals=0),
+        name="copies",
+    )(rows)
 
 
 def field_kernel(
@@ -358,7 +407,7 @@
     terms = (dot(keep_ref[...], dfield_ref[...]) + dot(other_ref[...], dother_ref[...])).astype(bf16)
     for i in range(16):
         out_ref[i, :, 0:1024] = terms[i * 32 : (i + 1) * 32, :]
-        rows = [turned_ref[pl.ds(2 * i + c, 4, stride=32), :] for c in range(2)]
+        rows = [turned_ref[pl.ds(8 * i + c, 4, stride=2), :] for c in range(2)]
         tint = two_terms(jnp.where(first, *rows))
         out_ref[i, :, 1024:1152] = jnp.concatenate(
             [*tint, *gain, jnp.zeros((8, 128), f32)], axis=0
@@ -487,12 +536,18 @@
     def among_same_core(x):
         return lax.all_to_all(x, "shard", split_axis=0, concat_axis=0, tiled=True, axis_index_groups=same_core)
 
-    own_rows = among_same_core(jnp.broadcast_to(head_weight[None], (shards // 2, *head_weight.shape)))
+    place = jnp.concatenate([group, core])
+    *parts, slot = pack(place, ray_scene, sample_points, sample_spacing, ray_targets, slots)
+    own_rows = among_same_core(copies(head_weight, shards // 2))
     own_rows = own_rows.reshape(512, 1024)
-    sent, slot = pack(ray_scene, sample_points, sample_spacing, ray_targets, slots)
-    sent, own_rows = lax.optimization_barrier((sent, own_rows))
+    for n in range(1, 8):
+        moves = [
+            (z * shards + i, (z + n // 2) % groups * shards + (i ^ (n % 2))) for z in range(groups) for i in range(shards)
+        ]
+        parts[n] = lax.ppermute(parts[n], both, moves)
+    sent, own_rows = lax.optimization_barrier((stack(place, parts), own_rows))
     other_rows = lax.ppermute(own_rows, "shard", across)
-    recv = lax.all_to_all(sent, both, split_axis=0, concat_axis=0, tiled=True).reshape(slots, 640)
+    recv = among_same_core(sent).reshape(slots, 640)
     weight, w0t, w1, w1t, keep, send = make_field(core, latents, own_rows, other_rows, gain_line)
     x_other = lax.ppermute(send, "shard", across)
     colors, d_field = render(recv, w0t, w1, w1t, color_head)

time: 105 us -> 101 us (0.962)
  waiting for transfers between devices: 51.7 us -> 8.62 us
  blocking collectives: 0 us -> 39 us
  Pallas kernels: 26 us -> 28.7 us
  local copies, waits for them, and re-layouts: 3.69 us -> 1.27 us
    all_to_all x0 -> x2, blocking collectives: none -> 39 us  [among_same_core(): lax.all_to_all(x, 'shard', split_axis=0, concat_axis=0, tiled=True, axis_...]
    all_to_all x2 -> x1, waiting for transfers between devices: 35.3 us -> 0.01 us  [among_same_core(): lax.all_to_all(x, 'shard', split_axis=0, concat_axis=0, tiled=True, axis_...]
    all_to_all x1 -> x0, waiting for transfers between devices: 11.4 us -> none  [body(): lax.all_to_all(sent, both, split_axis=0, concat_axis=0, tiled=True)]
    ppermute x0 -> x7, starting transfers between devices: none -> 9.25 us  [body(): parts[n] = lax.ppermute(parts[n], both, moves)]
    all_to_all x1 -> x0, starting transfers between devices: 7.41 us -> none  [body(): lax.all_to_all(sent, both, split_axis=0, concat_axis=0, tiled=True)]
    all_to_all x2 -> x1, starting transfers between devices: 10.8 us -> 7.12 us  [among_same_core(): lax.all_to_all(x, 'shard', split_axis=0, concat_axis=0, tiled=True, axis_...]
    pallas_call x1 -> x3, Pallas kernels: 2.25 us -> 5.95 us  [the longest x1 2.33 us: pack(): pl.pallas_call(pack_kernel, out_shape=(*(jax.ShapeDtypeStruct((slots // 8...]
    ppermute x0 -> x7, waiting for transfers between devices: none -> 3.2 us  [body(): parts[n] = lax.ppermute(parts[n], both, moves)]
  transfers between devices with their start and end apart: 10 -> 15, of which waited for: 7 -> 8; matrix products, arithmetic and copies ran while one was open for 0% -> 1% of each run, Pallas kernels for 4% -> 6%
where the time goes in v4:
time: 101 us
  blocking collectives  39 us (39%)
  Pallas kernels  28.7 us (28%)
  starting transfers between devices  22 us (22%)
  waiting for transfers between devices  8.62 us (9%)
  local copies, waits for them, and re-layouts  1.27 us (1%)
    all_to_all x2, blocking collectives, among_same_core(): lax.all_to_all(x, 'shard', split_axis=0, concat_axis=0, tiled=True, axis_...  39 us
    pallas_call x1, Pallas kernels, render(): pl.pallas_call(render_kernel, out_shape=(jax.ShapeDtypeStruct((8, slots),...  15.3 us
    ppermute x7, starting transfers between devices, body(): parts[n] = lax.ppermute(parts[n], both, moves)  9.25 us
    all_to_all x1, starting transfers between devices, among_same_core(): lax.all_to_all(x, 'shard', split_axis=0, concat_axis=0, tiled=True, axis_...  7.12 us
    ppermute x3, starting transfers between devices, body(): lax.ppermute(planes[k], 'grp', [(i, (i + k) % groups) for i in range(grou...  4.56 us
    ppermute x3, waiting for transfers between devices, body(): lax.ppermute(planes[k], 'grp', [(i, (i + k) % groups) for i in range(grou...  4.33 us
    ppermute x7, waiting for transfers between devices, body(): parts[n] = lax.ppermute(parts[n], both, moves)  3.2 us
    pallas_call x1, Pallas kernels, pack(): pl.pallas_call(pack_kernel, out_shape=(*(jax.ShapeDtypeStruct((slots // 8...  2.33 us
  transfers between devices with their start and end apart: 15, of which 8 were waited for; matrix products, arithmetic and copies ran while one was open for 1% of the time, Pallas kernels for 6%

profile of v4, /device:TPU:0, one launch (start us, length us, event | category | flops | bytes accessed | tf_op | source)
XLA Modules:
  0.0 100.9 jit_solution(690240204437024127)
XLA Ops:
  0.6 1.9 %copies.1 = bf16[16,32,1024]{2,1,0:T(8,128)(2,1)} custom-call(bf16[32,1024]{1,0:T(8,128)(2,1)} %rows_ref.1), custom_call_target="tpu_custom_call" | custom-call | bytes 1000000 | tf_op jit(solution)/shard_map/copies/pallas_call | solution.py:118
  2.6 7.1 %all-to-all-start = ((bf16[16,32,1024]{2,1,0:T(8,128)(2,1)}), bf16[16,32,1024]{2,1,0:T(8,128)(2,1)S(1)}, u32[]{:S(2)}, u32[]{:S(2)}) async-start(bf16[16,32,1024]{2,1,0:T(8,128)(2,1)} %copies.1), calls=%async_computation | async-start | bytes 2097152 | tf_op jit(solution)/shard_map/all_to_all | solution.py:537
  10.3 2.3 %pack.1 = (f32[16,1,640]{2,1,0:T(1,128)}, f32[16,1,640]{2,1,0:T(1,128)}, f32[16,1,640]{2,1,0:T(1,128)}, f32[16,1,640]{2,1,0:T(1,128)}, f32[16,1,640]{2,1,0:T(1,1...) custom-call(s32[2]{0:T(128)} %pad_add_fusion.place_ref, s32[64]{0:T(128)} %scene_ref.1, ...), custom_call_target="tpu_custom_call" | custom-call | flops 200000 | bytes 1000000 | tf_op jit(solution)/shard_map/pack/pallas_call | solution.py:70
  12.7 2.0 %collective-permute-start.1 = (f32[16,1,640]{2,1,0:T(1,128)}, f32[16,1,640]{2,1,0:T(1,128)S(1)}, u32[]{:S(2)}, u32[]{:S(2)}) collective-permute-start(f32[16,1,640]{2,1,0:T(1,128)} %get-tuple-element.37), channel_id=1, source_target_pairs={{0,32},{1,33},{2,34},{3,35},{4,36},{5,37},{6,38},{7,39},{8,40},{9,... | collective-permute-start | bytes 122888 | tf_op jit(solution)/shard_map/ppermute | solution.py:547
  14.7 1.7 %collective-permute-start.2 = (f32[16,1,640]{2,1,0:T(1,128)}, f32[16,1,640]{2,1,0:T(1,128)S(1)}, u32[]{:S(2)}, u32[]{:S(2)}) collective-permute-start(f32[16,1,640]{2,1,0:T(1,128)} %get-tuple-element.38), channel_id=1, source_target_pairs={{0,33},{1,32},{2,35},{3,34},{4,37},{5,36},{6,39},{7,38},{8,41},{9,... | collective-permute-start | bytes 122888 | tf_op jit(solution)/shard_map/ppermute | solution.py:547
  16.4 2.0 %collective-permute-start.3 = (f32[16,1,640]{2,1,0:T(1,128)}, f32[16,1,640]{2,1,0:T(1,128)S(1)}, u32[]{:S(2)}, u32[]{:S(2)}) collective-permute-start(f32[16,1,640]{2,1,0:T(1,128)} %get-tuple-element.39), channel_id=1, source_target_pairs={{0,64},{1,65},{2,66},{3,67},{4,68},{5,69},{6,70},{7,71},{8,72},{9,... | collective-permute-start | bytes 122888 | tf_op jit(solution)/shard_map/ppermute | solution.py:547
  18.4 1.2 %collective-permute-start.4 = (f32[16,1,640]{2,1,0:T(1,128)}, f32[16,1,640]{2,1,0:T(1,128)S(1)}, u32[]{:S(2)}, u32[]{:S(2)}) collective-permute-start(f32[16,1,640]{2,1,0:T(1,128)} %get-tuple-element.40), channel_id=1, source_target_pairs={{0,65},{1,64},{2,67},{3,66},{4,69},{5,68},{6,71},{7,70},{8,73},{9,... | collective-permute-start | bytes 122888 | tf_op jit(solution)/shard_map/ppermute | solution.py:547
  19.6 1.3 %collective-permute-start.5 = (f32[16,1,640]{2,1,0:T(1,128)}, f32[16,1,640]{2,1,0:T(1,128)S(1)}, u32[]{:S(2)}, u32[]{:S(2)}) collective-permute-start(f32[16,1,640]{2,1,0:T(1,128)} %get-tuple-element.41), channel_id=1, source_target_pairs={{0,96},{1,97},{2,98},{3,99},{4,100},{5,101},{6,102},{7,103},{8,104... | collective-permute-start | bytes 122888 | tf_op jit(solution)/shard_map/ppermute | solution.py:547
  20.9 1.0 collective-permute-start.6
  22.2 1.7 %collective-permute-done.4.rest_5_ = f32[16,1,640]{2,1,0:T(1,128)S(1)} collective-permute-done((f32[16,1,640]{2,1,0:T(1,128)}, f32[16,1,640]{2,1,0:T(1,128)S(1)}, u32[]{:S(2)}, u32[]{:S(2)}) %collective-permute-start.4) | collective-permute-done | bytes 40992 | tf_op jit(solution)/shard_map/ppermute | solution.py:547
  25.7 1.7 %stack.1 = f32[16,8,1,640]{3,2,1,0:T(1,128)} custom-call(s32[2]{0:T(128)} %pad_add_fusion.place_ref, f32[16,1,640]{2,1,0:T(1,128)} %get-tuple-element.35.rest_0_, f32[16,1,640]{2,1,0:T(1,128)} %copy-done.6, f32[16,1,640]{2,1,0:T(1,128)} %copy-done.7, f32[16,1,640]{2,1,0:T(1,128)} %copy-done.8, f32[16,1,640]{2,1,0:T(1,128)} %copy-done.9, ...), custom_call_target="tpu_custom_call" | custom-call | flops 100000 | bytes 800000 | tf_op jit(solution)/shard_map/stack/pallas_call | solution.py:100
  27.8 16.7 %all_to_all.15 = f32[16,8,1,640]{3,2,1,0:T(1,128)S(1)} all-to-all(f32[16,8,1,640]{3,2,1,0:T(1,128)} %stack.1), channel_id=1, replica_groups={{0,2,4,6,8,10,12,14,16,18,20,22,24,26,28,30},{1,3,5,7,9,11,13,15,17,19,..., dimensions={0} | all-to-all | bytes 655360 | tf_op jit(solution)/shard_map/all_to_all | solution.py:537
  44.6 0.9 field.1
  45.5 15.3 %render.1 = (f32[8,128]{1,0:T(8,128)S(1)}, bf16[128,1024]{1,0:T(8,128)(2,1)S(1)}) custom-call(f32[128,640]{1,0:T(8,128)S(1)} %bitcast.11, bf16[256,128]{1,0:T(8,128)(2,1)S(1)} %get-tuple-element.47.w0t_ref, bf16[256,256]{1,0:T(8,128)(2,1)S(1)} %get-tuple-element.48.w1_ref, bf16[256,256]{1,0:T(8,128)(2,1)S(1)} %get-tuple-element.49.w1t_ref, ...), custom_call_target="tpu_custom_call" | custom-call | flops 12000000000 | bytes 2000000 | tf_op jit(solution)/shard_map/render/pallas_call | solution.py:336
  61.4 1.7 %latent_gradient.1 = (bf16[128,1024]{1,0:T(8,128)(2,1)}, f32[16,128]{1,0:T(8,128)S(1)}) custom-call(bf16[128,1024]{1,0:T(8,128)(2,1)S(1)} %copy-done, bf16[1024,1024]{1,0:T(8,128)(2,1)S(1)} %get-tuple-element.51.weight_ref, f32[1,1024]{1,0:T(1,128)S(1)} %bitcast.13, bf16[128,1024]{1,0:T(8,128)(2,1)S(1)} %get-tuple-element.50.dfield_ref, ...), custom_call_target="tpu_custom_call" | custom-call | flops 300000000 | bytes 3000000 | tf_op jit(solution)/shard_map/latent_gradient/pallas_call | solution.py:377
  63.2 1.1 %collective-permute-done.10.nother_ref = f32[16,128]{1,0:T(8,128)S(1)} collective-permute-done((f32[16,128]{1,0:T(8,128)S(1)}, f32[16,128]{1,0:T(8,128)S(1)}, u32[]{:S(2)}, u32[]{:S(2)}) %collective-permute-start.10) | collective-permute-done | bytes 8224 | tf_op jit(solution)/shard_map/ppermute | solution.py:556
  65.0 22.3 %all_to_all.16.terms_ref = bf16[16,32,1152]{2,1,0:T(8,128)(2,1)} all-to-all(bf16[16,32,1152]{2,1,0:T(8,128)(2,1)S(1)} %pair_terms.1), channel_id=1, replica_groups={{0,2,4,6,8,10,12,14,16,18,20,22,24,26,28,30},{1,3,5,7,9,11,13,15,17,19,..., dimensions={0} | all-to-all | bytes 2359296 | tf_op jit(solution)/shard_map/all_to_all | solution.py:537
  87.3 2.2 %plane_sum.1 = (bf16[32,1280]{1,0:T(8,128)(2,1)}, bf16[32,1280]{1,0:T(8,128)(2,1)}, bf16[32,1280]{1,0:T(8,128)(2,1)}, bf16[32,1280]{1,0:T(8,128)(2,1)}) custom-call(s32[1]{0:T(128)} %bitcast.group_ref, bf16[16,32,1152]{2,1,0:T(8,128)(2,1)} %all_to_all.16.terms_ref), custom_call_target="tpu_custom_call" | custom-call | flops 1000000 | bytes 1500000 | tf_op jit(solution)/shard_map/plane_sum/pallas_call | solution.py:454
  89.4 1.1 %collective-permute-start.11 = (bf16[32,1280]{1,0:T(8,128)(2,1)}, bf16[32,1280]{1,0:T(8,128)(2,1)S(1)}, u32[]{:S(2)}, u32[]{:S(2)}) collective-permute-start(bf16[32,1280]{1,0:T(8,128)(2,1)} %get-tuple-element.55), channel_id=1, source_target_pairs={{0,32},{32,64},{64,96},{96,0},{1,33},{33,65},{65,97},{97,1},{2,34}... | collective-permute-start | bytes 245768 | tf_op jit(solution)/shard_map/ppermute | solution.py:560
  90.5 3.1 %collective-permute-start.12 = (bf16[32,1280]{1,0:T(8,128)(2,1)}, bf16[32,1280]{1,0:T(8,128)(2,1)S(1)}, u32[]{:S(2)}, u32[]{:S(2)}) collective-permute-start(bf16[32,1280]{1,0:T(8,128)(2,1)} %get-tuple-element.56), channel_id=1, source_target_pairs={{0,64},{32,96},{64,0},{96,32},{1,65},{33,97},{65,1},{97,33},{2,66}... | collective-permute-start | bytes 245768 | tf_op jit(solution)/shard_map/ppermute | solution.py:560
  94.0 1.9 %collective-permute-done.11.m1 = bf16[32,1280]{1,0:T(8,128)(2,1)S(1)} collective-permute-done((bf16[32,1280]{1,0:T(8,128)(2,1)}, bf16[32,1280]{1,0:T(8,128)(2,1)S(1)}, u32[]{:S(2)}, u32[]{:S(2)}) %collective-permute-start.11) | collective-permute-done | bytes 81952 | tf_op jit(solution)/shard_map/ppermute | solution.py:560
  95.9 1.3 %collective-permute-done.12.m2 = bf16[32,1280]{1,0:T(8,128)(2,1)S(1)} collective-permute-done((bf16[32,1280]{1,0:T(8,128)(2,1)}, bf16[32,1280]{1,0:T(8,128)(2,1)S(1)}, u32[]{:S(2)}, u32[]{:S(2)}) %collective-permute-start.12) | collective-permute-done | bytes 81952 | tf_op jit(solution)/shard_map/ppermute | solution.py:560
  97.2 1.1 %collective-permute-done.13.m3 = bf16[32,1280]{1,0:T(8,128)(2,1)S(1)} collective-permute-done((bf16[32,1280]{1,0:T(8,128)(2,1)}, bf16[32,1280]{1,0:T(8,128)(2,1)S(1)}, u32[]{:S(2)}, u32[]{:S(2)}) %collective-permute-start.13) | collective-permute-done | bytes 81952 | tf_op jit(solution)/shard_map/ppermute | solution.py:560
  99.0 2.0 %finish.1 = (f32[3,64]{1,0:T(4,128)}, f32[1,1]{1,0:T(1,128)}, f32[32,1024]{1,0:T(8,128)}, f32[8,128]{1,0:T(8,128)}) custom-call(s32[1]{0:T(128)} %bitcast.group_ref, s32[64]{0:T(128)} %get-tuple-element.34.slot_ref, bf16[32,1280]{1,0:T(8,128)(2,1)} %get-tuple-element.54.m0, bf16[32,1280]{1,0:T(8,128)(2,1)} %copy-done.3, bf16[32,1280]{1,0:T(8,128)(2,1)} %copy-done.4, ...), custom_call_target="tpu_custom_call" | custom-call | flops 300000 | bytes 500000 | tf_op jit(solution)/shard_map/finish/pallas_call | solution.py:501
  (45 shorter events, 5.4 us)
Async XLA Ops:
  2.6 24.9 %all-to-all-start = ((bf16[16,32,1024]{2,1,0:T(8,128)(2,1)}), bf16[16,32,1024]{2,1,0:T(8,128)(2,1)S(1)}, u32[]{:S(2)}, u32[]{:S(2)}) async-start(bf16[16,32,1024]{2,1,0:T(8,128)(2,1)} %copies.1), calls=%async_computation | async-start | bytes 2097152 | tf_op jit(solution)/shard_map/all_to_all | solution.py:537
  9.7 34.8 %copy-start = (bf16[128,1024]{1,0:T(8,128)(2,1)S(1)}, bf16[128,1024]{1,0:T(8,128)(2,1)}, u32[]{:S(2)}) copy-start(bf16[128,1024]{1,0:T(8,128)(2,1)} %latent_ref.3) | copy-start | bytes 786436
  9.7 34.8 %copy-start.1 = (f32[1024]{0:T(1024)S(1)}, f32[1024]{0:T(1024)}, u32[]{:S(2)}) copy-start(f32[1024]{0:T(1024)} %param.10) | copy-start | bytes 12292
  12.6 7.0 %collective-permute-start = (f32[16,1,640]{2,1,0:T(1,128)}, f32[16,1,640]{2,1,0:T(1,128)S(1)}, u32[]{:S(2)}, u32[]{:S(2)}) collective-permute-start(f32[16,1,640]{2,1,0:T(1,128)} %get-tuple-element.36), channel_id=1, source_target_pairs={{0,1},{1,0},{2,3},{3,2},{4,5},{5,4},{6,7},{7,6},{8,9},{9,8},{10,11... | collective-permute-start | bytes 122888 | tf_op jit(solution)/shard_map/ppermute | solution.py:547
  12.7 8.2 %collective-permute-start.1 = (f32[16,1,640]{2,1,0:T(1,128)}, f32[16,1,640]{2,1,0:T(1,128)S(1)}, u32[]{:S(2)}, u32[]{:S(2)}) collective-permute-start(f32[16,1,640]{2,1,0:T(1,128)} %get-tuple-element.37), channel_id=1, source_target_pairs={{0,32},{1,33},{2,34},{3,35},{4,36},{5,37},{6,38},{7,39},{8,40},{9,... | collective-permute-start | bytes 122888 | tf_op jit(solution)/shard_map/ppermute | solution.py:547
  14.7 7.2 %collective-permute-start.2 = (f32[16,1,640]{2,1,0:T(1,128)}, f32[16,1,640]{2,1,0:T(1,128)S(1)}, u32[]{:S(2)}, u32[]{:S(2)}) collective-permute-start(f32[16,1,640]{2,1,0:T(1,128)} %get-tuple-element.38), channel_id=1, source_target_pairs={{0,33},{1,32},{2,35},{3,34},{4,37},{5,36},{6,39},{7,38},{8,41},{9,... | collective-permute-start | bytes 122888 | tf_op jit(solution)/shard_map/ppermute | solution.py:547
  16.4 5.8 %collective-permute-start.3 = (f32[16,1,640]{2,1,0:T(1,128)}, f32[16,1,640]{2,1,0:T(1,128)S(1)}, u32[]{:S(2)}, u32[]{:S(2)}) collective-permute-start(f32[16,1,640]{2,1,0:T(1,128)} %get-tuple-element.39), channel_id=1, source_target_pairs={{0,64},{1,65},{2,66},{3,67},{4,68},{5,69},{6,70},{7,71},{8,72},{9,... | collective-permute-start | bytes 122888 | tf_op jit(solution)/shard_map/ppermute | solution.py:547
  18.4 5.5 %collective-permute-start.4 = (f32[16,1,640]{2,1,0:T(1,128)}, f32[16,1,640]{2,1,0:T(1,128)S(1)}, u32[]{:S(2)}, u32[]{:S(2)}) collective-permute-start(f32[16,1,640]{2,1,0:T(1,128)} %get-tuple-element.40), channel_id=1, source_target_pairs={{0,65},{1,64},{2,67},{3,66},{4,69},{5,68},{6,71},{7,70},{8,73},{9,... | collective-permute-start | bytes 122888 | tf_op jit(solution)/shard_map/ppermute | solution.py:547
  19.6 5.5 %copy-start.6 = (f32[16,1,640]{2,1,0:T(1,128)}, f32[16,1,640]{2,1,0:T(1,128)S(1)}, u32[]{:S(2)}) copy-start(f32[16,1,640]{2,1,0:T(1,128)S(1)} %collective-permute-done.rest_1_) | copy-start | bytes 122884
  19.6 5.1 %collective-permute-start.5 = (f32[16,1,640]{2,1,0:T(1,128)}, f32[16,1,640]{2,1,0:T(1,128)S(1)}, u32[]{:S(2)}, u32[]{:S(2)}) collective-permute-start(f32[16,1,640]{2,1,0:T(1,128)} %get-tuple-element.41), channel_id=1, source_target_pairs={{0,96},{1,97},{2,98},{3,99},{4,100},{5,101},{6,102},{7,103},{8,104... | collective-permute-start | bytes 122888 | tf_op jit(solution)/shard_map/ppermute | solution.py:547
  20.9 4.2 %copy-start.7 = (f32[16,1,640]{2,1,0:T(1,128)}, f32[16,1,640]{2,1,0:T(1,128)S(1)}, u32[]{:S(2)}) copy-start(f32[16,1,640]{2,1,0:T(1,128)S(1)} %collective-permute-done.1.rest_2_) | copy-start | bytes 122884
  20.9 4.2 %collective-permute-start.6 = (f32[16,1,640]{2,1,0:T(1,128)}, f32[16,1,640]{2,1,0:T(1,128)S(1)}, u32[]{:S(2)}, u32[]{:S(2)}) collective-permute-start(f32[16,1,640]{2,1,0:T(1,128)} %get-tuple-element.42), channel_id=1, source_target_pairs={{0,97},{1,96},{2,99},{3,98},{4,101},{5,100},{6,103},{7,102},{8,105... | collective-permute-start | bytes 122888 | tf_op jit(solution)/shard_map/ppermute | solution.py:547
  21.9 3.2 %copy-start.8 = (f32[16,1,640]{2,1,0:T(1,128)}, f32[16,1,640]{2,1,0:T(1,128)S(1)}, u32[]{:S(2)}) copy-start(f32[16,1,640]{2,1,0:T(1,128)S(1)} %collective-permute-done.2.rest_3_) | copy-start | bytes 122884
  22.2 3.0 %copy-start.9 = (f32[16,1,640]{2,1,0:T(1,128)}, f32[16,1,640]{2,1,0:T(1,128)S(1)}, u32[]{:S(2)}) copy-start(f32[16,1,640]{2,1,0:T(1,128)S(1)} %collective-permute-done.3.rest_4_) | copy-start | bytes 122884
  23.9 1.2 %copy-start.10 = (f32[16,1,640]{2,1,0:T(1,128)}, f32[16,1,640]{2,1,0:T(1,128)S(1)}, u32[]{:S(2)}) copy-start(f32[16,1,640]{2,1,0:T(1,128)S(1)} %collective-permute-done.4.rest_5_) | copy-start | bytes 122884
  27.4 17.1 %collective-permute-start.7 = (bf16[512,1024]{1,0:T(8,128)(2,1)S(1)}, bf16[512,1024]{1,0:T(8,128)(2,1)S(1)}, u32[]{:S(2)}, u32[]{:S(2)}) collective-permute-start(bf16[512,1024]{1,0:T(8,128)(2,1)S(1)} %bitcast.9), channel_id=1, source_target_pairs={{0,1},{1,0},{2,3},{3,2},{4,5},{5,4},{6,7},{7,6},{8,9},{9,8},{10,11... | collective-permute-start | bytes 3145736 | tf_op jit(solution)/shard_map/ppermute | solution.py:549
  60.8 3.4 %collective-permute-start.9 = (bf16[128,1024]{1,0:T(8,128)(2,1)S(1)}, bf16[128,1024]{1,0:T(8,128)(2,1)S(1)}, u32[]{:S(2)}, u32[]{:S(2)}) collective-permute-start(bf16[128,1024]{1,0:T(8,128)(2,1)S(1)} %get-tuple-element.50.dfield_ref), channel_id=1, source_target_pairs={{0,1},{1,0},{2,3},{3,2},{4,5},{5,4},{6,7},{7,6},{8,9},{9,8},{10,11... | collective-permute-start | bytes 786440 | tf_op jit(solution)/shard_map/ppermute | solution.py:554
  60.9 3.3 %collective-permute-start.8 = (bf16[512,128]{1,0:T(8,128)(2,1)S(1)}, bf16[512,128]{1,0:T(8,128)(2,1)S(1)}, u32[]{:S(2)}, u32[]{:S(2)}) collective-permute-start(bf16[512,128]{1,0:T(8,128)(2,1)S(1)} %get-tuple-element.45), channel_id=1, source_target_pairs={{0,1},{1,0},{2,3},{3,2},{4,5},{5,4},{6,7},{7,6},{8,9},{9,8},{10,11... | collective-permute-start | bytes 393224 | tf_op jit(solution)/shard_map/ppermute | solution.py:552
  63.1 1.2 %collective-permute-start.10 = (f32[16,128]{1,0:T(8,128)S(1)}, f32[16,128]{1,0:T(8,128)S(1)}, u32[]{:S(2)}, u32[]{:S(2)}) collective-permute-start(f32[16,128]{1,0:T(8,128)S(1)} %get-tuple-element.53.note_ref), channel_id=1, source_target_pairs={{0,1},{1,0},{2,3},{3,2},{4,5},{5,4},{6,7},{7,6},{8,9},{9,8},{10,11... | collective-permute-start | bytes 24584 | tf_op jit(solution)/shard_map/ppermute | solution.py:556
  89.4 6.5 %collective-permute-start.11 = (bf16[32,1280]{1,0:T(8,128)(2,1)}, bf16[32,1280]{1,0:T(8,128)(2,1)S(1)}, u32[]{:S(2)}, u32[]{:S(2)}) collective-permute-start(bf16[32,1280]{1,0:T(8,128)(2,1)} %get-tuple-element.55), channel_id=1, source_target_pairs={{0,32},{32,64},{64,96},{96,0},{1,33},{33,65},{65,97},{97,1},{2,34}... | collective-permute-start | bytes 245768 | tf_op jit(solution)/shard_map/ppermute | solution.py:560
  90.5 6.6 %collective-permute-start.12 = (bf16[32,1280]{1,0:T(8,128)(2,1)}, bf16[32,1280]{1,0:T(8,128)(2,1)S(1)}, u32[]{:S(2)}, u32[]{:S(2)}) collective-permute-start(bf16[32,1280]{1,0:T(8,128)(2,1)} %get-tuple-element.56), channel_id=1, source_target_pairs={{0,64},{32,96},{64,0},{96,32},{1,65},{33,97},{65,1},{97,33},{2,66}... | collective-permute-start | bytes 245768 | tf_op jit(solution)/shard_map/ppermute | solution.py:560
  93.7 4.7 %collective-permute-start.13 = (bf16[32,1280]{1,0:T(8,128)(2,1)}, bf16[32,1280]{1,0:T(8,128)(2,1)S(1)}, u32[]{:S(2)}, u32[]{:S(2)}) collective-permute-start(bf16[32,1280]{1,0:T(8,128)(2,1)} %get-tuple-element.57), channel_id=1, source_target_pairs={{0,96},{32,0},{64,32},{96,64},{1,97},{33,1},{65,33},{97,65},{2,98}... | collective-permute-start | bytes 245768 | tf_op jit(solution)/shard_map/ppermute | solution.py:560
  95.9 2.4 %copy-start.3 = (bf16[32,1280]{1,0:T(8,128)(2,1)}, bf16[32,1280]{1,0:T(8,128)(2,1)S(1)}, u32[]{:S(2)}) copy-start(bf16[32,1280]{1,0:T(8,128)(2,1)S(1)} %collective-permute-done.11.m1) | copy-start | bytes 245764
  97.2 1.2 %copy-start.4 = (bf16[32,1280]{1,0:T(8,128)(2,1)}, bf16[32,1280]{1,0:T(8,128)(2,1)S(1)}, u32[]{:S(2)}) copy-start(bf16[32,1280]{1,0:T(8,128)(2,1)S(1)} %collective-permute-done.12.m2) | copy-start | bytes 245764
  (4 other events, 2.8 us)

commit v5 on v4

--- a/solution.py
+++ b/solution.py
@@ -81,6 +81,7 @@
             pltpu.VMEM((rays, 256), f32),
             pltpu.VMEM((2, rays, 128), f32),
         ],
+        compiler_params=pltpu.CompilerParams(vmem_limit_bytes=4 * 1024 * 1024),
         cost_estimate=pl.CostEstimate(flops=200000, bytes_accessed=1000000, transcendentals=0),
         name="pack",
     )(place, ray_scene, points, spacing, targets)
@@ -102,6 +103,7 @@
         out_shape=jax.ShapeDtypeStruct((16, 8, 1, 640), f32),
         in_specs=[pl.BlockSpec(memory_space=pltpu.SMEM)] + [vmem] * 8,
         out_specs=vmem,
+        compiler_params=pltpu.CompilerParams(vmem_limit_bytes=4 * 1024 * 1024),
         cost_estimate=pl.CostEstimate(flops=100_000, bytes_accessed=800_000, transcendentals=0),
         name="stack",
     )(place, *parts)
@@ -120,6 +122,7 @@
         out_shape=jax.ShapeDtypeStruct((count, *rows.shape), rows.dtype),
         in_specs=[vmem],
         out_specs=vmem,
+        compiler_params=pltpu.CompilerParams(vmem_limit_bytes=4 * 1024 * 1024),
         cost_estimate=pl.CostEstimate(flops=0, bytes_accessed=1_000_000, transcendentals=0),
         name="copies",
     )(rows)
@@ -457,6 +460,7 @@
         in_specs=[pl.BlockSpec(memory_space=pltpu.SMEM), vmem],
         out_specs=(vmem,) * 4,
         scratch_shapes=[pltpu.VMEM((4, 16, 128), f32)],
+        compiler_params=pltpu.CompilerParams(vmem_limit_bytes=8 * 1024 * 1024),
         cost_estimate=pl.CostEstimate(flops=1_000_000, bytes_accessed=1_500_000, transcendentals=0),
         name="plane_sum",
     )(group, terms)
@@ -509,6 +513,7 @@
         in_specs=[smem, smem] + [vmem] * 4,
         out_specs=(vmem,) * 4,
         scratch_shapes=[pltpu.VMEM((64, 1, 128), f32), pltpu.VMEM((rays, 128), f32)],
+        compiler_params=pltpu.CompilerParams(vmem_limit_bytes=4 * 1024 * 1024),
         cost_estimate=pl.CostEstimate(flops=300_000, bytes_accessed=500_000, transcendentals=0),
         name="finish",
     )(group, slot, *planes)

time: 101 us -> 95.1 us (0.942)
  Pallas kernels: 28.7 us -> 23.9 us
  blocking collectives: 39 us -> 36.4 us
  waiting for transfers between devices: 8.62 us -> 10.3 us
    all_to_all x1, waiting for transfers between devices: 0.01 us -> 2.74 us  [among_same_core(): lax.all_to_all(x, 'shard', split_axis=0, concat_axis=0, tiled=True, axis_...]
    all_to_all x2, blocking collectives: 39 us -> 36.4 us  [among_same_core(): lax.all_to_all(x, 'shard', split_axis=0, concat_axis=0, tiled=True, axis_...]
    pallas_call x1, Pallas kernels: 2.16 us -> 0.2 us  [plane_sum(): pl.pallas_call(plane_kernel, out_shape=(jax.ShapeDtypeStruct((32, 1280),...]
    pallas_call x1, Pallas kernels: 1.69 us -> 0.59 us  [stack(): pl.pallas_call(stack_kernel, out_shape=jax.ShapeDtypeStruct((16, 8, 1, 64...]
  transfers between devices with their start and end apart: 15 -> 15, of which waited for: 8 -> 8; matrix products, arithmetic and copies ran while one was open for 1% -> 0% of each run, Pallas kernels for 6% -> 4%
where the time goes in v5:
time: 95.1 us; the launch traced here: 94.8 us
  blocking collectives  36.4 us (38%)
  Pallas kernels  23.9 us (25%)
  starting transfers between devices  22.5 us (24%)
  waiting for transfers between devices  10.3 us (11%)
    all_to_all x2, blocking collectives, among_same_core(): lax.all_to_all(x, 'shard', split_axis=0, concat_axis=0, tiled=True, axis_...  36.4 us
    pallas_call x1, Pallas kernels, render(): pl.pallas_call(render_kernel, out_shape=(jax.ShapeDtypeStruct((8, slots),...  15.3 us
    ppermute x7, starting transfers between devices, body(): parts[n] = lax.ppermute(parts[n], both, moves)  9.25 us
    all_to_all x1, starting transfers between devices, among_same_core(): lax.all_to_all(x, 'shard', split_axis=0, concat_axis=0, tiled=True, axis_...  7.26 us
    ppermute x3, starting transfers between devices, body(): lax.ppermute(planes[k], 'grp', [(i, (i + k) % groups) for i in range(grou...  5.28 us
    ppermute x3, waiting for transfers between devices, body(): lax.ppermute(planes[k], 'grp', [(i, (i + k) % groups) for i in range(grou...  3.48 us
    ppermute x7, waiting for transfers between devices, body(): parts[n] = lax.ppermute(parts[n], both, moves)  2.99 us
    all_to_all x1, waiting for transfers between devices, among_same_core(): lax.all_to_all(x, 'shard', split_axis=0, concat_axis=0, tiled=True, axis_...  2.74 us
  transfers between devices with their start and end apart: 15, of which 8 were waited for; matrix products, arithmetic and copies ran while one was open for 0% of the time, Pallas kernels for 4%

profile of v5, /device:TPU:0, one launch (start us, length us, event | category | flops | bytes accessed | tf_op | source)
XLA Modules:
  0.0 94.8 jit_solution(4725769848623143755)
XLA Ops:
  1.5 1.1 %copies.1 = bf16[16,32,1024]{2,1,0:T(8,128)(2,1)} custom-call(bf16[32,1024]{1,0:T(8,128)(2,1)S(1)} %copy-done.1), custom_call_target="tpu_custom_call" | custom-call | bytes 1000000 | tf_op jit(solution)/shard_map/copies/pallas_call | solution.py:120
  2.6 7.3 %all-to-all-start = ((bf16[16,32,1024]{2,1,0:T(8,128)(2,1)}), bf16[16,32,1024]{2,1,0:T(8,128)(2,1)S(1)}, u32[]{:S(2)}, u32[]{:S(2)}) async-start(bf16[16,32,1024]{2,1,0:T(8,128)(2,1)} %copies.1), calls=%async_computation | async-start | bytes 2097152 | tf_op jit(solution)/shard_map/all_to_all | solution.py:542
  10.0 2.0 %pack.1 = (f32[16,1,640]{2,1,0:T(1,128)S(1)}, f32[16,1,640]{2,1,0:T(1,128)S(1)}, f32[16,1,640]{2,1,0:T(1,128)S(1)}, f32[16,1,640]{2,1,0:T(1,128)S(1)}, f32[16,1,...) custom-call(s32[2]{0:T(128)S(1)} %pad_add_fusion.place_ref, ...), custom_call_target="tpu_custom_call" | custom-call | flops 200000 | bytes 1000000 | tf_op jit(solution)/shard_map/pack/pallas_call | solution.py:70
  12.0 2.0 %collective-permute-start.1 = (f32[16,1,640]{2,1,0:T(1,128)S(1)}, f32[16,1,640]{2,1,0:T(1,128)S(1)}, u32[]{:S(2)}, u32[]{:S(2)}) collective-permute-start(f32[16,1,640]{2,1,0:T(1,128)S(1)} %get-tuple-element.37), channel_id=1, source_target_pairs={{0,32},{1,33},{2,34},{3,35},{4,36},{5,37},{6,38},{7,39},{8,40},{9,... | collective-permute-start | bytes 122888 | tf_op jit(solution)/shard_map/ppermute | solution.py:552
  14.0 1.7 %collective-permute-start.2 = (f32[16,1,640]{2,1,0:T(1,128)S(1)}, f32[16,1,640]{2,1,0:T(1,128)S(1)}, u32[]{:S(2)}, u32[]{:S(2)}) collective-permute-start(f32[16,1,640]{2,1,0:T(1,128)S(1)} %get-tuple-element.38), channel_id=1, source_target_pairs={{0,33},{1,32},{2,35},{3,34},{4,37},{5,36},{6,39},{7,38},{8,41},{9,... | collective-permute-start | bytes 122888 | tf_op jit(solution)/shard_map/ppermute | solution.py:552
  15.7 2.0 %collective-permute-start.3 = (f32[16,1,640]{2,1,0:T(1,128)S(1)}, f32[16,1,640]{2,1,0:T(1,128)S(1)}, u32[]{:S(2)}, u32[]{:S(2)}) collective-permute-start(f32[16,1,640]{2,1,0:T(1,128)S(1)} %get-tuple-element.39), channel_id=1, source_target_pairs={{0,64},{1,65},{2,66},{3,67},{4,68},{5,69},{6,70},{7,71},{8,72},{9,... | collective-permute-start | bytes 122888 | tf_op jit(solution)/shard_map/ppermute | solution.py:552
  17.7 1.2 %collective-permute-start.4 = (f32[16,1,640]{2,1,0:T(1,128)S(1)}, f32[16,1,640]{2,1,0:T(1,128)S(1)}, u32[]{:S(2)}, u32[]{:S(2)}) collective-permute-start(f32[16,1,640]{2,1,0:T(1,128)S(1)} %get-tuple-element.40), channel_id=1, source_target_pairs={{0,65},{1,64},{2,67},{3,66},{4,69},{5,68},{6,71},{7,70},{8,73},{9,... | collective-permute-start | bytes 122888 | tf_op jit(solution)/shard_map/ppermute | solution.py:552
  18.9 1.3 %collective-permute-start.5 = (f32[16,1,640]{2,1,0:T(1,128)S(1)}, f32[16,1,640]{2,1,0:T(1,128)S(1)}, u32[]{:S(2)}, u32[]{:S(2)}) collective-permute-start(f32[16,1,640]{2,1,0:T(1,128)S(1)} %get-tuple-element.41), channel_id=1, source_target_pairs={{0,96},{1,97},{2,98},{3,99},{4,100},{5,101},{6,102},{7,103},{8,104... | collective-permute-start | bytes 122888 | tf_op jit(solution)/shard_map/ppermute | solution.py:552
  20.2 1.0 %collective-permute-start.6 = (f32[16,1,640]{2,1,0:T(1,128)S(1)}, f32[16,1,640]{2,1,0:T(1,128)S(1)}, u32[]{:S(2)}, u32[]{:S(2)}) collective-permute-start(f32[16,1,640]{2,1,0:T(1,128)S(1)} %get-tuple-element.42), channel_id=1, source_target_pairs={{0,97},{1,96},{2,99},{3,98},{4,101},{5,100},{6,103},{7,102},{8,105... | collective-permute-start | bytes 122888 | tf_op jit(solution)/shard_map/ppermute | solution.py:552
  21.2 1.7 %collective-permute-done.4.rest_5_ = f32[16,1,640]{2,1,0:T(1,128)S(1)} collective-permute-done((f32[16,1,640]{2,1,0:T(1,128)S(1)}, f32[16,1,640]{2,1,0:T(1,128)S(1)}, u32[]{:S(2)}, u32[]{:S(2)}) %collective-permute-start.4) | collective-permute-done | bytes 40992 | tf_op jit(solution)/shard_map/ppermute | solution.py:552
  24.8 2.7 %all-to-all-done = bf16[16,32,1024]{2,1,0:T(8,128)(2,1)S(1)} async-done(((bf16[16,32,1024]{2,1,0:T(8,128)(2,1)}), bf16[16,32,1024]{2,1,0:T(8,128)(2,1)S(1)}, u32[]{:S(2)}, u32[]{:S(2)}) %all-to-all-start) | async-done | bytes 1048608 | tf_op jit(solution)/shard_map/all_to_all | solution.py:542
  27.5 14.2 %all_to_all.15 = f32[16,8,1,640]{3,2,1,0:T(1,128)S(1)} all-to-all(f32[16,8,1,640]{3,2,1,0:T(1,128)S(1)} %stack.1), channel_id=1, replica_groups={{0,2,4,6,8,10,12,14,16,18,20,22,24,26,28,30},{1,3,5,7,9,11,13,15,17,19,..., dimensions={0} | all-to-all | bytes 655360 | tf_op jit(solution)/shard_map/all_to_all | solution.py:542
  41.8 0.9 field.1
  42.7 15.3 %render.1 = (f32[8,128]{1,0:T(8,128)S(1)}, bf16[128,1024]{1,0:T(8,128)(2,1)S(1)}) custom-call(f32[128,640]{1,0:T(8,128)S(1)} %bitcast.11, bf16[256,128]{1,0:T(8,128)(2,1)S(1)} %get-tuple-element.47.w0t_ref, bf16[256,256]{1,0:T(8,128)(2,1)S(1)} %get-tuple-element.48.w1_ref, bf16[256,256]{1,0:T(8,128)(2,1)S(1)} %get-tuple-element.49.w1t_ref, ...), custom_call_target="tpu_custom_call" | custom-call | flops 12000000000 | bytes 2000000 | tf_op jit(solution)/shard_map/render/pallas_call | solution.py:339
  58.6 1.7 %latent_gradient.1 = (bf16[128,1024]{1,0:T(8,128)(2,1)}, f32[16,128]{1,0:T(8,128)S(1)}) custom-call(bf16[128,1024]{1,0:T(8,128)(2,1)S(1)} %copy-done, bf16[1024,1024]{1,0:T(8,128)(2,1)S(1)} %get-tuple-element.51.weight_ref, f32[1,1024]{1,0:T(1,128)S(1)} %bitcast.13, bf16[128,1024]{1,0:T(8,128)(2,1)S(1)} %get-tuple-element.50.dfield_ref, ...), custom_call_target="tpu_custom_call" | custom-call | flops 300000000 | bytes 3000000 | tf_op jit(solution)/shard_map/latent_gradient/pallas_call | solution.py:380
  60.3 1.1 %collective-permute-done.10.nother_ref = f32[16,128]{1,0:T(8,128)S(1)} collective-permute-done((f32[16,128]{1,0:T(8,128)S(1)}, f32[16,128]{1,0:T(8,128)S(1)}, u32[]{:S(2)}, u32[]{:S(2)}) %collective-permute-start.10) | collective-permute-done | bytes 8224 | tf_op jit(solution)/shard_map/ppermute | solution.py:561
  62.1 22.2 %all_to_all.16.terms_ref = bf16[16,32,1152]{2,1,0:T(8,128)(2,1)S(1)} all-to-all(bf16[16,32,1152]{2,1,0:T(8,128)(2,1)S(1)} %pair_terms.1), channel_id=1, replica_groups={{0,2,4,6,8,10,12,14,16,18,20,22,24,26,28,30},{1,3,5,7,9,11,13,15,17,19,..., dimensions={0} | all-to-all | bytes 2359296 | tf_op jit(solution)/shard_map/all_to_all | solution.py:542
  84.5 1.2 %collective-permute-start.11 = (bf16[32,1280]{1,0:T(8,128)(2,1)S(1)}, bf16[32,1280]{1,0:T(8,128)(2,1)S(1)}, u32[]{:S(2)}, u32[]{:S(2)}) collective-permute-start(bf16[32,1280]{1,0:T(8,128)(2,1)S(1)} %get-tuple-element.55), channel_id=1, source_target_pairs={{0,32},{32,64},{64,96},{96,0},{1,33},{33,65},{65,97},{97,1},{2,34}... | collective-permute-start | bytes 245768 | tf_op jit(solution)/shard_map/ppermute | solution.py:565
  85.7 3.1 %collective-permute-start.12 = (bf16[32,1280]{1,0:T(8,128)(2,1)S(1)}, bf16[32,1280]{1,0:T(8,128)(2,1)S(1)}, u32[]{:S(2)}, u32[]{:S(2)}) collective-permute-start(bf16[32,1280]{1,0:T(8,128)(2,1)S(1)} %get-tuple-element.56), channel_id=1, source_target_pairs={{0,64},{32,96},{64,0},{96,32},{1,65},{33,97},{65,1},{97,33},{2,66}... | collective-permute-start | bytes 245768 | tf_op jit(solution)/shard_map/ppermute | solution.py:565
  88.8 1.0 %collective-permute-start.13 = (bf16[32,1280]{1,0:T(8,128)(2,1)S(1)}, bf16[32,1280]{1,0:T(8,128)(2,1)S(1)}, u32[]{:S(2)}, u32[]{:S(2)}) collective-permute-start(bf16[32,1280]{1,0:T(8,128)(2,1)S(1)} %get-tuple-element.57), channel_id=1, source_target_pairs={{0,96},{32,0},{64,32},{96,64},{1,97},{33,1},{65,33},{97,65},{2,98}... | collective-permute-start | bytes 245768 | tf_op jit(solution)/shard_map/ppermute | solution.py:565
  89.8 1.1 %collective-permute-done.11.m1 = bf16[32,1280]{1,0:T(8,128)(2,1)S(1)} collective-permute-done((bf16[32,1280]{1,0:T(8,128)(2,1)S(1)}, bf16[32,1280]{1,0:T(8,128)(2,1)S(1)}, u32[]{:S(2)}, u32[]{:S(2)}) %collective-permute-start.11) | collective-permute-done | bytes 81952 | tf_op jit(solution)/shard_map/ppermute | solution.py:565
  90.8 1.3 %collective-permute-done.12.m2 = bf16[32,1280]{1,0:T(8,128)(2,1)S(1)} collective-permute-done((bf16[32,1280]{1,0:T(8,128)(2,1)S(1)}, bf16[32,1280]{1,0:T(8,128)(2,1)S(1)}, u32[]{:S(2)}, u32[]{:S(2)}) %collective-permute-start.12) | collective-permute-done | bytes 81952 | tf_op jit(solution)/shard_map/ppermute | solution.py:565
  92.1 1.1 %collective-permute-done.13.m3 = bf16[32,1280]{1,0:T(8,128)(2,1)S(1)} collective-permute-done((bf16[32,1280]{1,0:T(8,128)(2,1)S(1)}, bf16[32,1280]{1,0:T(8,128)(2,1)S(1)}, u32[]{:S(2)}, u32[]{:S(2)}) %collective-permute-start.13) | collective-permute-done | bytes 81952 | tf_op jit(solution)/shard_map/ppermute | solution.py:565
  93.3 1.5 %finish.1 = (f32[3,64]{1,0:T(4,128)}, f32[1,1]{1,0:T(1,128)}, f32[32,1024]{1,0:T(8,128)}, f32[8,128]{1,0:T(8,128)}) custom-call(s32[1]{0:T(128)} %bitcast.group_ref, s32[64]{0:T(128)S(1)} %get-tuple-element.34.slot_ref, bf16[32,1280]{1,0:T(8,128)(2,1)S(1)} %get-tuple-element.54.m0, bf16[32,1280]{1,0:T(8,128)(2,1)S(1)} %collective-permute-done.11.m1, ...), custom_call_target="tpu_custom_call" | custom-call | flops 300000 | bytes 500000 | tf_op jit(solution)/shard_map/finish/pallas_call | solution.py:505
  (35 shorter events, 4.5 us)
Async XLA Ops:
  0.6 0.8 copy-start.1
  2.6 7.4 %copy-start.2 = (f32[64,192]{1,0:T(8,128)S(1)}, f32[64,192]{1,0:T(8,128)}, u32[]{:S(2)}) copy-start(f32[64,192]{1,0:T(8,128)} %points_ref.1) | copy-start | bytes 147460
  2.6 7.4 %copy-start.3 = (f32[64,64]{1,0:T(8,128)S(1)}, f32[64,64]{1,0:T(8,128)}, u32[]{:S(2)}) copy-start(f32[64,64]{1,0:T(8,128)} %spacing_ref.1) | copy-start | bytes 49156
  2.6 7.4 %copy-start.5 = (f32[3,64]{1,0:T(4,128)S(1)}, f32[3,64]{1,0:T(4,128)}, u32[]{:S(2)}) copy-start(f32[3,64]{1,0:T(4,128)} %target_ref.1) | copy-start | bytes 2308
  2.6 7.4 %copy-start.6 = (s32[64]{0:T(128)S(1)}, s32[64]{0:T(128)}, u32[]{:S(2)}) copy-start(s32[64]{0:T(128)} %scene_ref.1) | copy-start | bytes 772
  2.6 25.0 %all-to-all-start = ((bf16[16,32,1024]{2,1,0:T(8,128)(2,1)}), bf16[16,32,1024]{2,1,0:T(8,128)(2,1)S(1)}, u32[]{:S(2)}, u32[]{:S(2)}) async-start(bf16[16,32,1024]{2,1,0:T(8,128)(2,1)} %copies.1), calls=%async_computation | async-start | bytes 2097152 | tf_op jit(solution)/shard_map/all_to_all | solution.py:542
  9.8 31.9 %copy-start = (bf16[128,1024]{1,0:T(8,128)(2,1)S(1)}, bf16[128,1024]{1,0:T(8,128)(2,1)}, u32[]{:S(2)}) copy-start(bf16[128,1024]{1,0:T(8,128)(2,1)} %latent_ref.3) | copy-start | bytes 786436
  9.9 31.9 %copy-start.4 = (f32[1024]{0:T(1024)S(1)}, f32[1024]{0:T(1024)}, u32[]{:S(2)}) copy-start(f32[1024]{0:T(1024)} %param.10) | copy-start | bytes 12292
  11.9 7.0 %collective-permute-start = (f32[16,1,640]{2,1,0:T(1,128)S(1)}, f32[16,1,640]{2,1,0:T(1,128)S(1)}, u32[]{:S(2)}, u32[]{:S(2)}) collective-permute-start(f32[16,1,640]{2,1,0:T(1,128)S(1)} %get-tuple-element.36), channel_id=1, source_target_pairs={{0,1},{1,0},{2,3},{3,2},{4,5},{5,4},{6,7},{7,6},{8,9},{9,8},{10,11... | collective-permute-start | bytes 122888 | tf_op jit(solution)/shard_map/ppermute | solution.py:552
  12.0 8.2 %collective-permute-start.1 = (f32[16,1,640]{2,1,0:T(1,128)S(1)}, f32[16,1,640]{2,1,0:T(1,128)S(1)}, u32[]{:S(2)}, u32[]{:S(2)}) collective-permute-start(f32[16,1,640]{2,1,0:T(1,128)S(1)} %get-tuple-element.37), channel_id=1, source_target_pairs={{0,32},{1,33},{2,34},{3,35},{4,36},{5,37},{6,38},{7,39},{8,40},{9,... | collective-permute-start | bytes 122888 | tf_op jit(solution)/shard_map/ppermute | solution.py:552
  14.0 7.2 %collective-permute-start.2 = (f32[16,1,640]{2,1,0:T(1,128)S(1)}, f32[16,1,640]{2,1,0:T(1,128)S(1)}, u32[]{:S(2)}, u32[]{:S(2)}) collective-permute-start(f32[16,1,640]{2,1,0:T(1,128)S(1)} %get-tuple-element.38), channel_id=1, source_target_pairs={{0,33},{1,32},{2,35},{3,34},{4,37},{5,36},{6,39},{7,38},{8,41},{9,... | collective-permute-start | bytes 122888 | tf_op jit(solution)/shard_map/ppermute | solution.py:552
  15.7 5.5 %collective-permute-start.3 = (f32[16,1,640]{2,1,0:T(1,128)S(1)}, f32[16,1,640]{2,1,0:T(1,128)S(1)}, u32[]{:S(2)}, u32[]{:S(2)}) collective-permute-start(f32[16,1,640]{2,1,0:T(1,128)S(1)} %get-tuple-element.39), channel_id=1, source_target_pairs={{0,64},{1,65},{2,66},{3,67},{4,68},{5,69},{6,70},{7,71},{8,72},{9,... | collective-permute-start | bytes 122888 | tf_op jit(solution)/shard_map/ppermute | solution.py:552
  17.7 5.3 %collective-permute-start.4 = (f32[16,1,640]{2,1,0:T(1,128)S(1)}, f32[16,1,640]{2,1,0:T(1,128)S(1)}, u32[]{:S(2)}, u32[]{:S(2)}) collective-permute-start(f32[16,1,640]{2,1,0:T(1,128)S(1)} %get-tuple-element.40), channel_id=1, source_target_pairs={{0,65},{1,64},{2,67},{3,66},{4,69},{5,68},{6,71},{7,70},{8,73},{9,... | collective-permute-start | bytes 122888 | tf_op jit(solution)/shard_map/ppermute | solution.py:552
  18.9 4.9 %collective-permute-start.5 = (f32[16,1,640]{2,1,0:T(1,128)S(1)}, f32[16,1,640]{2,1,0:T(1,128)S(1)}, u32[]{:S(2)}, u32[]{:S(2)}) collective-permute-start(f32[16,1,640]{2,1,0:T(1,128)S(1)} %get-tuple-element.41), channel_id=1, source_target_pairs={{0,96},{1,97},{2,98},{3,99},{4,100},{5,101},{6,102},{7,103},{8,104... | collective-permute-start | bytes 122888 | tf_op jit(solution)/shard_map/ppermute | solution.py:552
  20.2 4.0 %collective-permute-start.6 = (f32[16,1,640]{2,1,0:T(1,128)S(1)}, f32[16,1,640]{2,1,0:T(1,128)S(1)}, u32[]{:S(2)}, u32[]{:S(2)}) collective-permute-start(f32[16,1,640]{2,1,0:T(1,128)S(1)} %get-tuple-element.42), channel_id=1, source_target_pairs={{0,97},{1,96},{2,99},{3,98},{4,101},{5,100},{6,103},{7,102},{8,105... | collective-permute-start | bytes 122888 | tf_op jit(solution)/shard_map/ppermute | solution.py:552
  27.5 14.2 %collective-permute-start.7 = (bf16[512,1024]{1,0:T(8,128)(2,1)S(1)}, bf16[512,1024]{1,0:T(8,128)(2,1)S(1)}, u32[]{:S(2)}, u32[]{:S(2)}) collective-permute-start(bf16[512,1024]{1,0:T(8,128)(2,1)S(1)} %bitcast.9), channel_id=1, source_target_pairs={{0,1},{1,0},{2,3},{3,2},{4,5},{5,4},{6,7},{7,6},{8,9},{9,8},{10,11... | collective-permute-start | bytes 3145736 | tf_op jit(solution)/shard_map/ppermute | solution.py:554
  41.8 0.9 copy-start.7
  58.0 3.4 %collective-permute-start.9 = (bf16[128,1024]{1,0:T(8,128)(2,1)S(1)}, bf16[128,1024]{1,0:T(8,128)(2,1)S(1)}, u32[]{:S(2)}, u32[]{:S(2)}) collective-permute-start(bf16[128,1024]{1,0:T(8,128)(2,1)S(1)} %get-tuple-element.50.dfield_ref), channel_id=1, source_target_pairs={{0,1},{1,0},{2,3},{3,2},{4,5},{5,4},{6,7},{7,6},{8,9},{9,8},{10,11... | collective-permute-start | bytes 786440 | tf_op jit(solution)/shard_map/ppermute | solution.py:559
  58.1 3.3 %collective-permute-start.8 = (bf16[512,128]{1,0:T(8,128)(2,1)S(1)}, bf16[512,128]{1,0:T(8,128)(2,1)S(1)}, u32[]{:S(2)}, u32[]{:S(2)}) collective-permute-start(bf16[512,128]{1,0:T(8,128)(2,1)S(1)} %get-tuple-element.45), channel_id=1, source_target_pairs={{0,1},{1,0},{2,3},{3,2},{4,5},{5,4},{6,7},{7,6},{8,9},{9,8},{10,11... | collective-permute-start | bytes 393224 | tf_op jit(solution)/shard_map/ppermute | solution.py:557
  60.2 1.2 %collective-permute-start.10 = (f32[16,128]{1,0:T(8,128)S(1)}, f32[16,128]{1,0:T(8,128)S(1)}, u32[]{:S(2)}, u32[]{:S(2)}) collective-permute-start(f32[16,128]{1,0:T(8,128)S(1)} %get-tuple-element.53.note_ref), channel_id=1, source_target_pairs={{0,1},{1,0},{2,3},{3,2},{4,5},{5,4},{6,7},{7,6},{8,9},{9,8},{10,11... | collective-permute-start | bytes 24584 | tf_op jit(solution)/shard_map/ppermute | solution.py:561
  84.5 6.3 %collective-permute-start.11 = (bf16[32,1280]{1,0:T(8,128)(2,1)S(1)}, bf16[32,1280]{1,0:T(8,128)(2,1)S(1)}, u32[]{:S(2)}, u32[]{:S(2)}) collective-permute-start(bf16[32,1280]{1,0:T(8,128)(2,1)S(1)} %get-tuple-element.55), channel_id=1, source_target_pairs={{0,32},{32,64},{64,96},{96,0},{1,33},{33,65},{65,97},{97,1},{2,34}... | collective-permute-start | bytes 245768 | tf_op jit(solution)/shard_map/ppermute | solution.py:565
  85.7 6.4 %collective-permute-start.12 = (bf16[32,1280]{1,0:T(8,128)(2,1)S(1)}, bf16[32,1280]{1,0:T(8,128)(2,1)S(1)}, u32[]{:S(2)}, u32[]{:S(2)}) collective-permute-start(bf16[32,1280]{1,0:T(8,128)(2,1)S(1)} %get-tuple-element.56), channel_id=1, source_target_pairs={{0,64},{32,96},{64,0},{96,32},{1,65},{33,97},{65,1},{97,33},{2,66}... | collective-permute-start | bytes 245768 | tf_op jit(solution)/shard_map/ppermute | solution.py:565
  88.8 4.4 %collective-permute-start.13 = (bf16[32,1280]{1,0:T(8,128)(2,1)S(1)}, bf16[32,1280]{1,0:T(8,128)(2,1)S(1)}, u32[]{:S(2)}, u32[]{:S(2)}) collective-permute-start(bf16[32,1280]{1,0:T(8,128)(2,1)S(1)} %get-tuple-element.57), channel_id=1, source_target_pairs={{0,96},{32,0},{64,32},{96,64},{1,97},{33,1},{65,33},{97,65},{2,98}... | collective-permute-start | bytes 245768 | tf_op jit(solution)/shard_map/ppermute | solution.py:565

commit v6 on v5

--- a/solution.py
+++ b/solution.py
@@ -140,6 +140,8 @@
     w1t_ref,
     keep_ref,
     send_ref,
+    hat_ref,
+    inv_ref,
     rows_ref,
     turned_ref,
 ):
@@ -150,6 +152,8 @@
             weight_ref[pl.ds(pl.multiple_of(i * 64 + part * 32, 32), 32), :] = ref[i * 32 : (i + 1) * 32, :]
     latent = latent_ref[...].astype(f32)
     inv_rms = lax.rsqrt(jnp.mean(latent * latent, axis=1, keepdims=True) + norm_eps)
+    hat_ref[...] = latent * inv_rms
+    inv_ref[...] = jnp.broadcast_to(inv_rms, inv_ref.shape)
     normed = latent * inv_rms * gain_ref[...]
     field = dot(normed.astype(bf16), weight_ref[...]).astype(bf16)
     stacked = jnp.concatenate([field[0:64, q * 256 : (q + 1) * 256] for q in range(4)], axis=0)
@@ -175,9 +179,13 @@
     shapes = ((1024, 1024), (256, 128), (256, 256), (256, 256), (512, 128), (512, 128))
     return pl.pallas_call(
         field_kernel,
-        out_shape=tuple(jax.ShapeDtypeStruct(shape, bf16) for shape in shapes),
+        out_shape=(
+            *(jax.ShapeDtypeStruct(shape, bf16) for shape in shapes),
+            jax.ShapeDtypeStruct((128, 1024), f32),
+            jax.ShapeDtypeStruct((128, 128), f32),
+        ),
         in_specs=[pl.BlockSpec(memory_space=pltpu.SMEM)] + [vmem] * 4,
-        out_specs=(vmem,) * 6,
+        out_specs=(vmem,) * 8,
         scratch_shapes=[pltpu.VMEM((2, 256, 128), f32), pltpu.VMEM((1024, 128), bf16)],
         compiler_params=pltpu.CompilerParams(vmem_limit_bytes=24 * 1024 * 1024),
         cost_estimate=pl.CostEstimate(flops=400_000_000, bytes_accessed=5_000_000, transcendentals=0),
@@ -361,10 +369,9 @@
     )(recv, w0t, w1, w1t, head)
 
 
-def latent_kernel(latent_ref, weight_ref, gain_ref, dfield_ref, color_ref, out_ref, note_ref):
-    latent = latent_ref[...].astype(f32)
-    inv_rms = lax.rsqrt(jnp.mean(latent * latent, axis=1, keepdims=True) + norm_eps)
-    x_hat = latent * inv_rms
+def latent_kernel(hat_ref, inv_ref, weight_ref, gain_ref, dfield_ref, color_ref, out_ref, note_ref):
+    x_hat = hat_ref[...]
+    inv_rms = inv_ref[:, 0:1]
     d_norm = dot(dfield_ref[...], weight_ref[...], (((1,), (1,)), ((), ())))
     term = d_norm * x_hat
     gain = jnp.sum(term, axis=0, keepdims=True)
@@ -375,20 +382,20 @@
         note_ref[8 + i : 9 + i, :] = gain[:, i * 128 : (i + 1) * 128]
 
 
-def latent_gradient(latents, weight, gain, d_field, colors):
+def latent_gradient(x_hat, inv_rms, weight, gain, d_field, colors):
     vmem = pl.BlockSpec(memory_space=pltpu.VMEM)
     return pl.pallas_call(
         latent_kernel,
         out_shape=(
-            jax.ShapeDtypeStruct(latents.shape, bf16),
+            jax.ShapeDtypeStruct(x_hat.shape, bf16),
             jax.ShapeDtypeStruct((16, 128), f32),
         ),
-        in_specs=[vmem] * 5,
+        in_specs=[vmem] * 6,
         out_specs=(vmem,) * 2,
         compiler_params=pltpu.CompilerParams(vmem_limit_bytes=24 * 1024 * 1024),
         cost_estimate=pl.CostEstimate(flops=300_000_000, bytes_accessed=3_000_000, transcendentals=0),
         name="latent_gradient",
-    )(latents, weight, gain, d_field, colors)
+    )(x_hat, inv_rms, weight, gain, d_field, colors)
 
 
 def two_terms(value):
@@ -407,7 +414,9 @@
     )
     turned_ref[...] = colors.T
     gain = two_terms(mine[8:16, :] + mate[8:16, :])
-    terms = (dot(keep_ref[...], dfield_ref[...]) + dot(other_ref[...], dother_ref[...])).astype(bf16)
+    x_both = jnp.concatenate([keep_ref[...], other_ref[...]], axis=1)
+    d_both = jnp.concatenate([dfield_ref[...], dother_ref[...]], axis=0)
+    terms = dot(x_both, d_both).astype(bf16)
     for i in range(16):
         out_ref[i, :, 0:1024] = terms[i * 32 : (i + 1) * 32, :]
         rows = [turned_ref[pl.ds(8 * i + c, 4, stride=2), :] for c in range(2)]
@@ -553,11 +562,11 @@
     sent, own_rows = lax.optimization_barrier((stack(place, parts), own_rows))
     other_rows = lax.ppermute(own_rows, "shard", across)
     recv = among_same_core(sent).reshape(slots, 640)
-    weight, w0t, w1, w1t, keep, send = make_field(core, latents, own_rows, other_rows, gain_line)
+    weight, w0t, w1, w1t, keep, send, x_hat, inv_rms = make_field(core, latents, own_rows, other_rows, gain_line)
     x_other = lax.ppermute(send, "shard", across)
     colors, d_field = render(recv, w0t, w1, w1t, color_head)
     d_other = lax.ppermute(d_field, "shard", across)
-    latent_grad, note = latent_gradient(latents, weight, gain_line, d_field, colors)
+    latent_grad, note = latent_gradient(x_hat, inv_rms, weight, gain_line, d_field, colors)
     note_other = lax.ppermute(note, "shard", across)
     paired = pair_terms(core, keep, x_other, d_field, d_other, note, note_other)
     planes = plane_sum(group, among_same_core(paired))

time: 95.1 us -> 94.9 us (level)
  no operation moved by 1% of the time
where the time goes in v6:
time: 94.9 us; the launch traced here: 94.5 us
  blocking collectives  36.4 us (38%)
  Pallas kernels  23.6 us (25%)
  starting transfers between devices  22.5 us (24%)
  waiting for transfers between devices  10.3 us (11%)
    all_to_all x2, blocking collectives, among_same_core(): lax.all_to_all(x, 'shard', split_axis=0, concat_axis=0, tiled=True, axis_...  36.4 us
    pallas_call x1, Pallas kernels, render(): pl.pallas_call(render_kernel, out_shape=(jax.ShapeDtypeStruct((8, slots),...  15.3 us
    ppermute x7, starting transfers between devices, body(): parts[n] = lax.ppermute(parts[n], both, moves)  9.25 us
    all_to_all x1, starting transfers between devices, among_same_core(): lax.all_to_all(x, 'shard', split_axis=0, concat_axis=0, tiled=True, axis_...  7.26 us
    ppermute x3, starting transfers between devices, body(): lax.ppermute(planes[k], 'grp', [(i, (i + k) % groups) for i in range(grou...  5.28 us
    ppermute x3, waiting for transfers between devices, body(): lax.ppermute(planes[k], 'grp', [(i, (i + k) % groups) for i in range(grou...  3.48 us
    ppermute x7, waiting for transfers between devices, body(): parts[n] = lax.ppermute(parts[n], both, moves)  2.99 us
    all_to_all x1, waiting for transfers between devices, among_same_core(): lax.all_to_all(x, 'shard', split_axis=0, concat_axis=0, tiled=True, axis_...  2.74 us
  transfers between devices with their start and end apart: 15, of which 8 were waited for; matrix products, arithmetic and copies ran while one was open for 0% of the time, Pallas kernels for 4%

profile of v6, /device:TPU:0, one launch (start us, length us, event | category | flops | bytes accessed | tf_op | source)
XLA Modules:
  0.0 94.5 jit_solution(8510213464617027768)
XLA Ops:
  1.5 1.1 %copies.1 = bf16[16,32,1024]{2,1,0:T(8,128)(2,1)} custom-call(bf16[32,1024]{1,0:T(8,128)(2,1)S(1)} %copy-done.1), custom_call_target="tpu_custom_call" | custom-call | bytes 1000000 | tf_op jit(solution)/shard_map/copies/pallas_call | solution.py:120
  2.6 7.3 %all-to-all-start = ((bf16[16,32,1024]{2,1,0:T(8,128)(2,1)}), bf16[16,32,1024]{2,1,0:T(8,128)(2,1)S(1)}, u32[]{:S(2)}, u32[]{:S(2)}) async-start(bf16[16,32,1024]{2,1,0:T(8,128)(2,1)} %copies.1), calls=%async_computation | async-start | bytes 2097152 | tf_op jit(solution)/shard_map/all_to_all | solution.py:551
  10.0 2.0 %pack.1 = (f32[16,1,640]{2,1,0:T(1,128)S(1)}, f32[16,1,640]{2,1,0:T(1,128)S(1)}, f32[16,1,640]{2,1,0:T(1,128)S(1)}, f32[16,1,640]{2,1,0:T(1,128)S(1)}, f32[16,1,...) custom-call(s32[2]{0:T(128)S(1)} %pad_add_fusion.place_ref, ...), custom_call_target="tpu_custom_call" | custom-call | flops 200000 | bytes 1000000 | tf_op jit(solution)/shard_map/pack/pallas_call | solution.py:70
  12.0 2.0 %collective-permute-start.1 = (f32[16,1,640]{2,1,0:T(1,128)S(1)}, f32[16,1,640]{2,1,0:T(1,128)S(1)}, u32[]{:S(2)}, u32[]{:S(2)}) collective-permute-start(f32[16,1,640]{2,1,0:T(1,128)S(1)} %get-tuple-element.39), channel_id=1, source_target_pairs={{0,32},{1,33},{2,34},{3,35},{4,36},{5,37},{6,38},{7,39},{8,40},{9,... | collective-permute-start | bytes 122888 | tf_op jit(solution)/shard_map/ppermute | solution.py:561
  14.0 1.7 %collective-permute-start.2 = (f32[16,1,640]{2,1,0:T(1,128)S(1)}, f32[16,1,640]{2,1,0:T(1,128)S(1)}, u32[]{:S(2)}, u32[]{:S(2)}) collective-permute-start(f32[16,1,640]{2,1,0:T(1,128)S(1)} %get-tuple-element.40), channel_id=1, source_target_pairs={{0,33},{1,32},{2,35},{3,34},{4,37},{5,36},{6,39},{7,38},{8,41},{9,... | collective-permute-start | bytes 122888 | tf_op jit(solution)/shard_map/ppermute | solution.py:561
  15.7 2.0 %collective-permute-start.3 = (f32[16,1,640]{2,1,0:T(1,128)S(1)}, f32[16,1,640]{2,1,0:T(1,128)S(1)}, u32[]{:S(2)}, u32[]{:S(2)}) collective-permute-start(f32[16,1,640]{2,1,0:T(1,128)S(1)} %get-tuple-element.41), channel_id=1, source_target_pairs={{0,64},{1,65},{2,66},{3,67},{4,68},{5,69},{6,70},{7,71},{8,72},{9,... | collective-permute-start | bytes 122888 | tf_op jit(solution)/shard_map/ppermute | solution.py:561
  17.7 1.2 %collective-permute-start.4 = (f32[16,1,640]{2,1,0:T(1,128)S(1)}, f32[16,1,640]{2,1,0:T(1,128)S(1)}, u32[]{:S(2)}, u32[]{:S(2)}) collective-permute-start(f32[16,1,640]{2,1,0:T(1,128)S(1)} %get-tuple-element.42), channel_id=1, source_target_pairs={{0,65},{1,64},{2,67},{3,66},{4,69},{5,68},{6,71},{7,70},{8,73},{9,... | collective-permute-start | bytes 122888 | tf_op jit(solution)/shard_map/ppermute | solution.py:561
  18.9 1.3 %collective-permute-start.5 = (f32[16,1,640]{2,1,0:T(1,128)S(1)}, f32[16,1,640]{2,1,0:T(1,128)S(1)}, u32[]{:S(2)}, u32[]{:S(2)}) collective-permute-start(f32[16,1,640]{2,1,0:T(1,128)S(1)} %get-tuple-element.43), channel_id=1, source_target_pairs={{0,96},{1,97},{2,98},{3,99},{4,100},{5,101},{6,102},{7,103},{8,104... | collective-permute-start | bytes 122888 | tf_op jit(solution)/shard_map/ppermute | solution.py:561
  20.2 1.0 %collective-permute-start.6 = (f32[16,1,640]{2,1,0:T(1,128)S(1)}, f32[16,1,640]{2,1,0:T(1,128)S(1)}, u32[]{:S(2)}, u32[]{:S(2)}) collective-permute-start(f32[16,1,640]{2,1,0:T(1,128)S(1)} %get-tuple-element.44), channel_id=1, source_target_pairs={{0,97},{1,96},{2,99},{3,98},{4,101},{5,100},{6,103},{7,102},{8,105... | collective-permute-start | bytes 122888 | tf_op jit(solution)/shard_map/ppermute | solution.py:561
  21.2 1.7 %collective-permute-done.4.rest_5_ = f32[16,1,640]{2,1,0:T(1,128)S(1)} collective-permute-done((f32[16,1,640]{2,1,0:T(1,128)S(1)}, f32[16,1,640]{2,1,0:T(1,128)S(1)}, u32[]{:S(2)}, u32[]{:S(2)}) %collective-permute-start.4) | collective-permute-done | bytes 40992 | tf_op jit(solution)/shard_map/ppermute | solution.py:561
  24.8 2.7 %all-to-all-done = bf16[16,32,1024]{2,1,0:T(8,128)(2,1)S(1)} async-done(((bf16[16,32,1024]{2,1,0:T(8,128)(2,1)}), bf16[16,32,1024]{2,1,0:T(8,128)(2,1)S(1)}, u32[]{:S(2)}, u32[]{:S(2)}) %all-to-all-start) | async-done | bytes 1048608 | tf_op jit(solution)/shard_map/all_to_all | solution.py:551
  27.5 14.2 %all_to_all.15 = f32[16,8,1,640]{3,2,1,0:T(1,128)S(1)} all-to-all(f32[16,8,1,640]{3,2,1,0:T(1,128)S(1)} %stack.1), channel_id=1, replica_groups={{0,2,4,6,8,10,12,14,16,18,20,22,24,26,28,30},{1,3,5,7,9,11,13,15,17,19,..., dimensions={0} | all-to-all | bytes 655360 | tf_op jit(solution)/shard_map/all_to_all | solution.py:551
  41.8 0.9 field.1
  42.7 15.3 %render.1 = (f32[8,128]{1,0:T(8,128)S(1)}, bf16[128,1024]{1,0:T(8,128)(2,1)S(1)}) custom-call(f32[128,640]{1,0:T(8,128)S(1)} %bitcast.11, bf16[256,128]{1,0:T(8,128)(2,1)S(1)} %get-tuple-element.49.w0t_ref, bf16[256,256]{1,0:T(8,128)(2,1)S(1)} %get-tuple-element.50.w1_ref, bf16[256,256]{1,0:T(8,128)(2,1)S(1)} %get-tuple-element.51.w1t_ref, ...), custom_call_target="tpu_custom_call" | custom-call | flops 12000000000 | bytes 2000000 | tf_op jit(solution)/shard_map/render/pallas_call | solution.py:347
  58.6 1.6 %latent_gradient.1 = (bf16[128,1024]{1,0:T(8,128)(2,1)}, f32[16,128]{1,0:T(8,128)S(1)}) custom-call(f32[128,1024]{1,0:T(8,128)S(1)} %get-tuple-element.53.hat_ref, f32[128,128]{1,0:T(8,128)S(1)} %get-tuple-element.54.inv_ref, bf16[1024,1024]{1,0:T(8,128)(2,1)S(1)} %get-tuple-element.55.weight_ref, f32[1,1024]{1,0:T(1,128)S(1)} %bitcast.13, ...), custom_call_target="tpu_custom_call" | custom-call | flops 300000000 | bytes 3000000 | tf_op jit(solution)/shard_map/latent_gradient/pallas_call | solution.py:387
  60.3 1.1 %collective-permute-done.10.nother_ref = f32[16,128]{1,0:T(8,128)S(1)} collective-permute-done((f32[16,128]{1,0:T(8,128)S(1)}, f32[16,128]{1,0:T(8,128)S(1)}, u32[]{:S(2)}, u32[]{:S(2)}) %collective-permute-start.10) | collective-permute-done | bytes 8224 | tf_op jit(solution)/shard_map/ppermute | solution.py:570
  61.9 22.2 %all_to_all.16.terms_ref = bf16[16,32,1152]{2,1,0:T(8,128)(2,1)S(1)} all-to-all(bf16[16,32,1152]{2,1,0:T(8,128)(2,1)S(1)} %pair_terms.1), channel_id=1, replica_groups={{0,2,4,6,8,10,12,14,16,18,20,22,24,26,28,30},{1,3,5,7,9,11,13,15,17,19,..., dimensions={0} | all-to-all | bytes 2359296 | tf_op jit(solution)/shard_map/all_to_all | solution.py:551
  84.2 1.2 %collective-permute-start.11 = (bf16[32,1280]{1,0:T(8,128)(2,1)S(1)}, bf16[32,1280]{1,0:T(8,128)(2,1)S(1)}, u32[]{:S(2)}, u32[]{:S(2)}) collective-permute-start(bf16[32,1280]{1,0:T(8,128)(2,1)S(1)} %get-tuple-element.59), channel_id=1, source_target_pairs={{0,32},{32,64},{64,96},{96,0},{1,33},{33,65},{65,97},{97,1},{2,34}... | collective-permute-start | bytes 245768 | tf_op jit(solution)/shard_map/ppermute | solution.py:574
  85.4 3.1 %collective-permute-start.12 = (bf16[32,1280]{1,0:T(8,128)(2,1)S(1)}, bf16[32,1280]{1,0:T(8,128)(2,1)S(1)}, u32[]{:S(2)}, u32[]{:S(2)}) collective-permute-start(bf16[32,1280]{1,0:T(8,128)(2,1)S(1)} %get-tuple-element.60), channel_id=1, source_target_pairs={{0,64},{32,96},{64,0},{96,32},{1,65},{33,97},{65,1},{97,33},{2,66}... | collective-permute-start | bytes 245768 | tf_op jit(solution)/shard_map/ppermute | solution.py:574
  88.6 1.0 %collective-permute-start.13 = (bf16[32,1280]{1,0:T(8,128)(2,1)S(1)}, bf16[32,1280]{1,0:T(8,128)(2,1)S(1)}, u32[]{:S(2)}, u32[]{:S(2)}) collective-permute-start(bf16[32,1280]{1,0:T(8,128)(2,1)S(1)} %get-tuple-element.61), channel_id=1, source_target_pairs={{0,96},{32,0},{64,32},{96,64},{1,97},{33,1},{65,33},{97,65},{2,98}... | collective-permute-start | bytes 245768 | tf_op jit(solution)/shard_map/ppermute | solution.py:574
  89.5 1.1 %collective-permute-done.11.m1 = bf16[32,1280]{1,0:T(8,128)(2,1)S(1)} collective-permute-done((bf16[32,1280]{1,0:T(8,128)(2,1)S(1)}, bf16[32,1280]{1,0:T(8,128)(2,1)S(1)}, u32[]{:S(2)}, u32[]{:S(2)}) %collective-permute-start.11) | collective-permute-done | bytes 81952 | tf_op jit(solution)/shard_map/ppermute | solution.py:574
  90.6 1.3 %collective-permute-done.12.m2 = bf16[32,1280]{1,0:T(8,128)(2,1)S(1)} collective-permute-done((bf16[32,1280]{1,0:T(8,128)(2,1)S(1)}, bf16[32,1280]{1,0:T(8,128)(2,1)S(1)}, u32[]{:S(2)}, u32[]{:S(2)}) %collective-permute-start.12) | collective-permute-done | bytes 81952 | tf_op jit(solution)/shard_map/ppermute | solution.py:574
  91.9 1.1 %collective-permute-done.13.m3 = bf16[32,1280]{1,0:T(8,128)(2,1)S(1)} collective-permute-done((bf16[32,1280]{1,0:T(8,128)(2,1)S(1)}, bf16[32,1280]{1,0:T(8,128)(2,1)S(1)}, u32[]{:S(2)}, u32[]{:S(2)}) %collective-permute-start.13) | collective-permute-done | bytes 81952 | tf_op jit(solution)/shard_map/ppermute | solution.py:574
  93.0 1.5 %finish.1 = (f32[3,64]{1,0:T(4,128)}, f32[1,1]{1,0:T(1,128)}, f32[32,1024]{1,0:T(8,128)}, f32[8,128]{1,0:T(8,128)}) custom-call(s32[1]{0:T(128)} %bitcast.group_ref, s32[64]{0:T(128)S(1)} %get-tuple-element.36.slot_ref, bf16[32,1280]{1,0:T(8,128)(2,1)S(1)} %get-tuple-element.58.m0, bf16[32,1280]{1,0:T(8,128)(2,1)S(1)} %collective-permute-done.11.m1, ...), custom_call_target="tpu_custom_call" | custom-call | flops 300000 | bytes 500000 | tf_op jit(solution)/shard_map/finish/pallas_call | solution.py:514
  (35 shorter events, 4.2 us)
Async XLA Ops:
  0.6 0.8 copy-start.1
  2.6 7.4 %copy-start.2 = (f32[64,192]{1,0:T(8,128)S(1)}, f32[64,192]{1,0:T(8,128)}, u32[]{:S(2)}) copy-start(f32[64,192]{1,0:T(8,128)} %points_ref.1) | copy-start | bytes 147460
  2.6 7.4 %copy-start.3 = (f32[64,64]{1,0:T(8,128)S(1)}, f32[64,64]{1,0:T(8,128)}, u32[]{:S(2)}) copy-start(f32[64,64]{1,0:T(8,128)} %spacing_ref.1) | copy-start | bytes 49156
  2.6 7.4 %copy-start.5 = (f32[3,64]{1,0:T(4,128)S(1)}, f32[3,64]{1,0:T(4,128)}, u32[]{:S(2)}) copy-start(f32[3,64]{1,0:T(4,128)} %target_ref.1) | copy-start | bytes 2308
  2.6 7.4 %copy-start.6 = (s32[64]{0:T(128)S(1)}, s32[64]{0:T(128)}, u32[]{:S(2)}) copy-start(s32[64]{0:T(128)} %scene_ref.1) | copy-start | bytes 772
  2.6 25.0 %all-to-all-start = ((bf16[16,32,1024]{2,1,0:T(8,128)(2,1)}), bf16[16,32,1024]{2,1,0:T(8,128)(2,1)S(1)}, u32[]{:S(2)}, u32[]{:S(2)}) async-start(bf16[16,32,1024]{2,1,0:T(8,128)(2,1)} %copies.1), calls=%async_computation | async-start | bytes 2097152 | tf_op jit(solution)/shard_map/all_to_all | solution.py:551
  9.8 31.9 %copy-start = (bf16[128,1024]{1,0:T(8,128)(2,1)S(1)}, bf16[128,1024]{1,0:T(8,128)(2,1)}, u32[]{:S(2)}) copy-start(bf16[128,1024]{1,0:T(8,128)(2,1)} %latent_ref.1) | copy-start | bytes 786436
  9.9 31.9 %copy-start.4 = (f32[1024]{0:T(1024)S(1)}, f32[1024]{0:T(1024)}, u32[]{:S(2)}) copy-start(f32[1024]{0:T(1024)} %param.10) | copy-start | bytes 12292
  11.9 7.0 %collective-permute-start = (f32[16,1,640]{2,1,0:T(1,128)S(1)}, f32[16,1,640]{2,1,0:T(1,128)S(1)}, u32[]{:S(2)}, u32[]{:S(2)}) collective-permute-start(f32[16,1,640]{2,1,0:T(1,128)S(1)} %get-tuple-element.38), channel_id=1, source_target_pairs={{0,1},{1,0},{2,3},{3,2},{4,5},{5,4},{6,7},{7,6},{8,9},{9,8},{10,11... | collective-permute-start | bytes 122888 | tf_op jit(solution)/shard_map/ppermute | solution.py:561
  12.0 8.2 %collective-permute-start.1 = (f32[16,1,640]{2,1,0:T(1,128)S(1)}, f32[16,1,640]{2,1,0:T(1,128)S(1)}, u32[]{:S(2)}, u32[]{:S(2)}) collective-permute-start(f32[16,1,640]{2,1,0:T(1,128)S(1)} %get-tuple-element.39), channel_id=1, source_target_pairs={{0,32},{1,33},{2,34},{3,35},{4,36},{5,37},{6,38},{7,39},{8,40},{9,... | collective-permute-start | bytes 122888 | tf_op jit(solution)/shard_map/ppermute | solution.py:561
  14.0 7.2 %collective-permute-start.2 = (f32[16,1,640]{2,1,0:T(1,128)S(1)}, f32[16,1,640]{2,1,0:T(1,128)S(1)}, u32[]{:S(2)}, u32[]{:S(2)}) collective-permute-start(f32[16,1,640]{2,1,0:T(1,128)S(1)} %get-tuple-element.40), channel_id=1, source_target_pairs={{0,33},{1,32},{2,35},{3,34},{4,37},{5,36},{6,39},{7,38},{8,41},{9,... | collective-permute-start | bytes 122888 | tf_op jit(solution)/shard_map/ppermute | solution.py:561
  15.7 5.5 %collective-permute-start.3 = (f32[16,1,640]{2,1,0:T(1,128)S(1)}, f32[16,1,640]{2,1,0:T(1,128)S(1)}, u32[]{:S(2)}, u32[]{:S(2)}) collective-permute-start(f32[16,1,640]{2,1,0:T(1,128)S(1)} %get-tuple-element.41), channel_id=1, source_target_pairs={{0,64},{1,65},{2,66},{3,67},{4,68},{5,69},{6,70},{7,71},{8,72},{9,... | collective-permute-start | bytes 122888 | tf_op jit(solution)/shard_map/ppermute | solution.py:561
  17.7 5.3 %collective-permute-start.4 = (f32[16,1,640]{2,1,0:T(1,128)S(1)}, f32[16,1,640]{2,1,0:T(1,128)S(1)}, u32[]{:S(2)}, u32[]{:S(2)}) collective-permute-start(f32[16,1,640]{2,1,0:T(1,128)S(1)} %get-tuple-element.42), channel_id=1, source_target_pairs={{0,65},{1,64},{2,67},{3,66},{4,69},{5,68},{6,71},{7,70},{8,73},{9,... | collective-permute-start | bytes 122888 | tf_op jit(solution)/shard_map/ppermute | solution.py:561
  18.9 4.9 %collective-permute-start.5 = (f32[16,1,640]{2,1,0:T(1,128)S(1)}, f32[16,1,640]{2,1,0:T(1,128)S(1)}, u32[]{:S(2)}, u32[]{:S(2)}) collective-permute-start(f32[16,1,640]{2,1,0:T(1,128)S(1)} %get-tuple-element.43), channel_id=1, source_target_pairs={{0,96},{1,97},{2,98},{3,99},{4,100},{5,101},{6,102},{7,103},{8,104... | collective-permute-start | bytes 122888 | tf_op jit(solution)/shard_map/ppermute | solution.py:561
  20.2 4.0 %collective-permute-start.6 = (f32[16,1,640]{2,1,0:T(1,128)S(1)}, f32[16,1,640]{2,1,0:T(1,128)S(1)}, u32[]{:S(2)}, u32[]{:S(2)}) collective-permute-start(f32[16,1,640]{2,1,0:T(1,128)S(1)} %get-tuple-element.44), channel_id=1, source_target_pairs={{0,97},{1,96},{2,99},{3,98},{4,101},{5,100},{6,103},{7,102},{8,105... | collective-permute-start | bytes 122888 | tf_op jit(solution)/shard_map/ppermute | solution.py:561
  27.5 14.2 %collective-permute-start.7 = (bf16[512,1024]{1,0:T(8,128)(2,1)S(1)}, bf16[512,1024]{1,0:T(8,128)(2,1)S(1)}, u32[]{:S(2)}, u32[]{:S(2)}) collective-permute-start(bf16[512,1024]{1,0:T(8,128)(2,1)S(1)} %bitcast.9), channel_id=1, source_target_pairs={{0,1},{1,0},{2,3},{3,2},{4,5},{5,4},{6,7},{7,6},{8,9},{9,8},{10,11... | collective-permute-start | bytes 3145736 | tf_op jit(solution)/shard_map/ppermute | solution.py:563
  41.8 0.9 copy-start.7
  58.0 3.4 %collective-permute-start.9 = (bf16[128,1024]{1,0:T(8,128)(2,1)S(1)}, bf16[128,1024]{1,0:T(8,128)(2,1)S(1)}, u32[]{:S(2)}, u32[]{:S(2)}) collective-permute-start(bf16[128,1024]{1,0:T(8,128)(2,1)S(1)} %get-tuple-element.52.dfield_ref), channel_id=1, source_target_pairs={{0,1},{1,0},{2,3},{3,2},{4,5},{5,4},{6,7},{7,6},{8,9},{9,8},{10,11... | collective-permute-start | bytes 786440 | tf_op jit(solution)/shard_map/ppermute | solution.py:568
  58.1 3.3 %collective-permute-start.8 = (bf16[512,128]{1,0:T(8,128)(2,1)S(1)}, bf16[512,128]{1,0:T(8,128)(2,1)S(1)}, u32[]{:S(2)}, u32[]{:S(2)}) collective-permute-start(bf16[512,128]{1,0:T(8,128)(2,1)S(1)} %get-tuple-element.47), channel_id=1, source_target_pairs={{0,1},{1,0},{2,3},{3,2},{4,5},{5,4},{6,7},{7,6},{8,9},{9,8},{10,11... | collective-permute-start | bytes 393224 | tf_op jit(solution)/shard_map/ppermute | solution.py:566
  60.2 1.2 %collective-permute-start.10 = (f32[16,128]{1,0:T(8,128)S(1)}, f32[16,128]{1,0:T(8,128)S(1)}, u32[]{:S(2)}, u32[]{:S(2)}) collective-permute-start(f32[16,128]{1,0:T(8,128)S(1)} %get-tuple-element.57.note_ref), channel_id=1, source_target_pairs={{0,1},{1,0},{2,3},{3,2},{4,5},{5,4},{6,7},{7,6},{8,9},{9,8},{10,11... | collective-permute-start | bytes 24584 | tf_op jit(solution)/shard_map/ppermute | solution.py:570
  84.2 6.3 %collective-permute-start.11 = (bf16[32,1280]{1,0:T(8,128)(2,1)S(1)}, bf16[32,1280]{1,0:T(8,128)(2,1)S(1)}, u32[]{:S(2)}, u32[]{:S(2)}) collective-permute-start(bf16[32,1280]{1,0:T(8,128)(2,1)S(1)} %get-tuple-element.59), channel_id=1, source_target_pairs={{0,32},{32,64},{64,96},{96,0},{1,33},{33,65},{65,97},{97,1},{2,34}... | collective-permute-start | bytes 245768 | tf_op jit(solution)/shard_map/ppermute | solution.py:574
  85.4 6.4 %collective-permute-start.12 = (bf16[32,1280]{1,0:T(8,128)(2,1)S(1)}, bf16[32,1280]{1,0:T(8,128)(2,1)S(1)}, u32[]{:S(2)}, u32[]{:S(2)}) collective-permute-start(bf16[32,1280]{1,0:T(8,128)(2,1)S(1)} %get-tuple-element.60), channel_id=1, source_target_pairs={{0,64},{32,96},{64,0},{96,32},{1,65},{33,97},{65,1},{97,33},{2,66}... | collective-permute-start | bytes 245768 | tf_op jit(solution)/shard_map/ppermute | solution.py:574
  88.6 4.4 %collective-permute-start.13 = (bf16[32,1280]{1,0:T(8,128)(2,1)S(1)}, bf16[32,1280]{1,0:T(8,128)(2,1)S(1)}, u32[]{:S(2)}, u32[]{:S(2)}) collective-permute-start(bf16[32,1280]{1,0:T(8,128)(2,1)S(1)} %get-tuple-element.61), channel_id=1, source_target_pairs={{0,96},{32,0},{64,32},{96,64},{1,97},{33,1},{65,33},{97,65},{2,98}... | collective-permute-start | bytes 245768 | tf_op jit(solution)/shard_map/ppermute | solution.py:574
